TPU v7x, 32 devices: a whole 2x2x4 slice. The times are simulated.
32 devices in a mesh: wide: 8 (over y, x, core), narrow: 4 (over z).
Axes of the slice: x: 2, y: 2, z: 4, core: 2. Of those that a mesh axis runs over, the one named last changes fastest.
Arguments:
- tokens: bfloat16 [8192, 768], P(('wide', 'narrow')), may hold values from -6 to 6
- lengths: int32 [32], P(('wide', 'narrow')), may hold values from 1 to 256, 4096 in all
- cotangent: bfloat16 [8192, 768], P(('wide', 'narrow')), may hold values from -6 to 6
- w_query: bfloat16 [768, 768], P(('wide', 'narrow')), may hold values from -0.21875 to 0.21875
- w_key: bfloat16 [768, 768], P(('wide', 'narrow')), may hold values from -0.21875 to 0.21875
- w_value: bfloat16 [768, 768], P(('wide', 'narrow')), may hold values from -0.21875 to 0.21875
- w_out: bfloat16 [768, 768], P(('wide', 'narrow')), may hold values from -0.875 to 0.875
- w_fc1: bfloat16 [768, 3072], P(None, ('wide', 'narrow')), may hold values from -0.21875 to 0.21875
- w_fc2: bfloat16 [3072, 768], P(('wide', 'narrow')), may hold values from -0.109375 to 0.109375
- fc1_bias: bfloat16 [3072], P(('wide', 'narrow')), may hold values from -3 to 3
- vectors: bfloat16 [15, 768], P(None, ('wide', 'narrow')), may hold values from -4 to 4
Outputs:
- output: bfloat16 [8192, 768], P(('wide', 'narrow'))
- input_grad: bfloat16 [8192, 768], P(('wide', 'narrow'))
- grad_query: float32 [768, 768], P(('wide', 'narrow'))
- grad_key: float32 [768, 768], P(('wide', 'narrow'))
- grad_value: float32 [768, 768], P(('wide', 'narrow'))
- grad_out: float32 [768, 768], P(('wide', 'narrow'))
- grad_fc1: float32 [768, 3072], P(None, ('wide', 'narrow'))
- grad_fc2: float32 [3072, 768], P(('wide', 'narrow'))
- grad_fc1_bias: float32 [3072], P(('wide', 'narrow'))
- grad_vectors: float32 [15, 768], P(None, ('wide', 'narrow'))
Inputs may be any that keep to these rules, and one draw needn't show every extreme that they name: `lengths`: one slot has exactly 256 used rows in every draw.
All inputs are finite; a program needn't handle non-finite values. No bound on the sum of `lengths` on one device may be relied on, other than what follows from the above.
Results may differ from a plain program's by a relative error of at most 0.019.
Values may be sent and summed in bfloat16 or wider, within the bound.
A program may use at most 192 MiB of HBM per device.

v0:
```python
from functools import partial

import jax
import jax.numpy as jnp
from jax import lax
from jax.sharding import PartitionSpec as P

HEAD_SIZE = 64
STATE = 64


EPSILON = 1e-05


def normalize(values):
    average = jnp.mean(values, axis=-1, keepdims=True)
    centred = values - average
    variance = jnp.mean(centred * centred, axis=-1, keepdims=True)
    inverse = lax.rsqrt(variance + EPSILON)
    return (centred * inverse, inverse)


def norm_back(grad_in, scaled, inverse):
    first = jnp.mean(grad_in, axis=-1, keepdims=True)
    second = jnp.mean(grad_in * scaled, axis=-1, keepdims=True)
    return inverse * (grad_in - first - scaled * second)


def shift_mix(key_raw, shift_taps):
    summed = key_raw * shift_taps[0]
    for offset in range(1, 4):
        delayed = jnp.concatenate(
            [jnp.zeros((offset, key_raw.shape[1]), key_raw.dtype), key_raw[:-offset]], axis=0
        )
        summed = summed + delayed * shift_taps[offset]
    return summed


def kernel_rows(coefficient, decay_rate, length_all):
    distance = jnp.arange(length_all).astype(jnp.float32)
    decays = jnp.exp(-decay_rate[:, :, None] * distance[None, None, :])
    return jnp.sum(coefficient[:, :, None] * decays, axis=1) / STATE


def toeplitz(kernel_row):
    length_all = kernel_row.shape[0]
    wrapped = jnp.concatenate(
        [kernel_row[:1], jnp.zeros((length_all,), kernel_row.dtype), kernel_row[:0:-1]]
    )
    tiled_row = jnp.tile(wrapped, length_all)[: length_all * (2 * length_all - 1)]
    return tiled_row.reshape(length_all, 2 * length_all - 1)[:, :length_all]


def split_heads(values, row_count):
    return values.reshape(row_count, -1, HEAD_SIZE).transpose(1, 0, 2)


def merge_heads(per_head):
    head_count = per_head.shape[0]
    row_count = per_head.shape[1]
    merged = per_head.transpose(1, 0, 2).reshape(row_count, head_count * HEAD_SIZE)
    return merged


def pack_rows(matrices, shard_count):
    return jnp.concatenate(
        [matrix.reshape(shard_count, -1) for matrix in matrices], axis=1
    ).reshape(-1)


def unpack_rows(flat, matrices, shard_count):
    pieces = []
    offset = 0
    for matrix in matrices:
        rows_own = matrix.shape[0] // shard_count
        extent = matrix.size // shard_count
        pieces.append(flat[offset : offset + extent].reshape((rows_own,) + matrix.shape[1:]))
        offset = offset + extent
    return pieces


def mixer_forward(queries, keys, values, kernel, row_count):

    def head_forward(parts):
        query_head, key_head, value_head, kernel_row = parts
        scores = jnp.dot(query_head, key_head.T, preferred_element_type=jnp.float32) / HEAD_SIZE
        weights_mix = (scores * toeplitz(kernel_row)).astype(jnp.bfloat16)
        return jnp.dot(weights_mix, value_head, preferred_element_type=jnp.float32)

    per_head = lax.map(
        head_forward,
        (
            split_heads(queries, row_count),
            split_heads(keys, row_count),
            split_heads(values, row_count),
            kernel,
        ),
    )
    return merge_heads(per_head)


def mixer_backward(queries, keys, values, grad_mixed, kernel, row_count):

    def head_backward(parts):
        query_head, key_head, value_head, grad_head, kernel_row = parts
        scores = jnp.dot(query_head, key_head.T, preferred_element_type=jnp.float32) / HEAD_SIZE
        toeplitz_mat, pullback = jax.vjp(toeplitz, kernel_row)
        weights_mix = (scores * toeplitz_mat).astype(jnp.bfloat16)
        grad_weights = jnp.dot(grad_head, value_head.T, preferred_element_type=jnp.float32)
        grad_values = jnp.dot(weights_mix.T, grad_head, preferred_element_type=jnp.float32)
        grad_scores = (grad_weights * toeplitz_mat).astype(jnp.bfloat16)
        grad_queries = (
            jnp.dot(grad_scores, key_head, preferred_element_type=jnp.float32) / HEAD_SIZE
        )
        grad_keys = (
            jnp.dot(grad_scores.T, query_head, preferred_element_type=jnp.float32) / HEAD_SIZE
        )
        grad_kernel = pullback(grad_weights * scores)[0]
        return (grad_queries, grad_keys, grad_values, grad_kernel)

    head_grads = lax.map(
        head_backward,
        (
            split_heads(queries, row_count),
            split_heads(keys, row_count),
            split_heads(values, row_count),
            split_heads(grad_mixed, row_count),
            kernel,
        ),
    )
    grad_kernel = head_grads[3]
    return (
        merge_heads(head_grads[0]),
        merge_heads(head_grads[1]),
        merge_heads(head_grads[2]),
        grad_kernel,
    )


def on_device(
    tokens, lengths, cotangent, w_query, w_key, w_value, w_out, w_fc1, w_fc2, fc1_bias, vectors
):
    shard_count = lax.axis_size(("wide", "narrow"))
    gathered = (
        lax.all_gather(w_query, ("wide", "narrow"), axis=0, tiled=True),
        lax.all_gather(w_key, ("wide", "narrow"), axis=0, tiled=True),
        lax.all_gather(w_value, ("wide", "narrow"), axis=0, tiled=True),
        lax.all_gather(w_out, ("wide", "narrow"), axis=0, tiled=True),
        lax.all_gather(w_fc1, ("wide", "narrow"), axis=1, tiled=True),
        lax.all_gather(w_fc2, ("wide", "narrow"), axis=0, tiled=True),
        lax.all_gather(fc1_bias, ("wide", "narrow"), axis=0, tiled=True),
        lax.all_gather(vectors, ("wide", "narrow"), axis=1, tiled=True),
    )
    query_full, key_full, value_full, out_full, fc1_full, fc2_full, bias_full, vector_full = (
        gathered
    )
    params = vector_full.astype(jnp.float32)
    fc1_shift = bias_full.astype(jnp.float32)
    seq_len = tokens.shape[0]
    head_count = params.shape[1] // HEAD_SIZE
    seq_length = lengths[0]
    valid_mask = (jnp.arange(seq_len) < seq_length).astype(jnp.float32)[:, None]
    residual = tokens.astype(jnp.float32)
    scaled1, inverse1 = normalize(residual)
    normed = (scaled1 * params[0] + params[1]).astype(jnp.bfloat16)
    queries = (jnp.dot(normed, query_full, preferred_element_type=jnp.float32) + params[2]).astype(
        jnp.bfloat16
    )
    key_raw = jnp.dot(normed, key_full, preferred_element_type=jnp.float32) + params[3]
    keys = (shift_mix(key_raw, params[5:9]) * valid_mask).astype(jnp.bfloat16)
    values = (
        (jnp.dot(normed, value_full, preferred_element_type=jnp.float32) + params[4]) * valid_mask
    ).astype(jnp.bfloat16)
    coefficient = params[9].reshape(head_count, STATE)
    decay_rate = params[10].reshape(head_count, STATE)
    kernel_fn = partial(kernel_rows, length_all=seq_len)
    kernel, kernel_pull = jax.vjp(kernel_fn, coefficient, decay_rate)
    mixed = mixer_forward(queries, keys, values, kernel, seq_len)
    mixed_out = (mixed * valid_mask).astype(jnp.bfloat16)
    hidden = (
        residual + jnp.dot(mixed_out, out_full, preferred_element_type=jnp.float32) + params[11]
    )
    scaled2, inverse2 = normalize(hidden)
    normed2 = (scaled2 * params[12] + params[13]).astype(jnp.bfloat16)
    pre_act = jnp.dot(normed2, fc1_full, preferred_element_type=jnp.float32) + fc1_shift
    activated = jax.nn.gelu(pre_act).astype(jnp.bfloat16)
    output = (
        hidden + jnp.dot(activated, fc2_full, preferred_element_type=jnp.float32) + params[14]
    ).astype(jnp.bfloat16)
    again = (
        lax.all_gather(w_query, ("wide", "narrow"), axis=0, tiled=True),
        lax.all_gather(w_key, ("wide", "narrow"), axis=0, tiled=True),
        lax.all_gather(w_value, ("wide", "narrow"), axis=0, tiled=True),
        lax.all_gather(w_out, ("wide", "narrow"), axis=0, tiled=True),
        lax.all_gather(w_fc1, ("wide", "narrow"), axis=1, tiled=True),
        lax.all_gather(w_fc2, ("wide", "narrow"), axis=0, tiled=True),
        lax.all_gather(fc1_bias, ("wide", "narrow"), axis=0, tiled=True),
        lax.all_gather(vectors, ("wide", "narrow"), axis=1, tiled=True),
    )
    query_back, key_back, value_back, out_back, fc1_back, fc2_back = (
        again[0],
        again[1],
        again[2],
        again[3],
        again[4],
        again[5],
    )
    grad_top = cotangent.astype(jnp.float32)
    grad_fc2 = jnp.dot(activated.T, cotangent, preferred_element_type=jnp.float32)
    grad_activated = jnp.dot(cotangent, fc2_back.T, preferred_element_type=jnp.float32)
    gelu_value, gelu_pull = jax.vjp(jax.nn.gelu, pre_act)
    grad_pre = gelu_pull(grad_activated)[0].astype(jnp.bfloat16)
    grad_fc1_turned = jnp.dot(grad_pre.T, normed2, preferred_element_type=jnp.float32)
    grad_fc1_bias = jnp.sum(grad_pre.astype(jnp.float32), axis=0)[:, None]
    mlp_terms = [grad_fc1_turned, grad_fc2, grad_fc1_bias]
    mlp_flat = lax.psum_scatter(
        pack_rows(mlp_terms, shard_count), ("wide", "narrow"), scatter_dimension=0, tiled=True
    )
    mlp_sums = unpack_rows(mlp_flat, mlp_terms, shard_count)
    grad_normed2 = jnp.dot(grad_pre, fc1_back.T, preferred_element_type=jnp.float32)
    grad_hidden = grad_top + norm_back(grad_normed2 * params[12], scaled2, inverse2)
    grad_attn = grad_hidden.astype(jnp.bfloat16)
    grad_out = jnp.dot(mixed_out.T, grad_attn, preferred_element_type=jnp.float32)
    grad_mixed = (
        jnp.dot(grad_attn, out_back.T, preferred_element_type=jnp.float32) * valid_mask
    ).astype(jnp.bfloat16)
    grad_q, grad_k, grad_v, grad_kernel = mixer_backward(
        queries, keys, values, grad_mixed, kernel, seq_len
    )
    grad_queries = grad_q.astype(jnp.bfloat16)
    grad_values = (grad_v * valid_mask).astype(jnp.bfloat16)
    shift_value, shift_pull = jax.vjp(shift_mix, key_raw, params[5:9])
    grad_key_full, grad_taps = shift_pull(grad_k * valid_mask)
    grad_key_raw = grad_key_full.astype(jnp.bfloat16)
    grad_query = jnp.dot(normed.T, grad_queries, preferred_element_type=jnp.float32)
    grad_key = jnp.dot(normed.T, grad_key_raw, preferred_element_type=jnp.float32)
    grad_value = jnp.dot(normed.T, grad_values, preferred_element_type=jnp.float32)
    grad_normed = jnp.dot(grad_queries, query_back.T, preferred_element_type=jnp.float32)
    grad_normed = grad_normed + jnp.dot(
        grad_key_raw, key_back.T, preferred_element_type=jnp.float32
    )
    grad_normed = grad_normed + jnp.dot(
        grad_values, value_back.T, preferred_element_type=jnp.float32
    )
    input_grad = (grad_hidden + norm_back(grad_normed * params[0], scaled1, inverse1)).astype(
        jnp.bfloat16
    )
    grad_coef, grad_rate = kernel_pull(grad_kernel)
    grad_vectors = jnp.concatenate(
        [
            jnp.sum(grad_normed * scaled1, axis=0)[None],
            jnp.sum(grad_normed, axis=0)[None],
            jnp.sum(grad_queries.astype(jnp.float32), axis=0)[None],
            jnp.sum(grad_key_raw.astype(jnp.float32), axis=0)[None],
            jnp.sum(grad_values.astype(jnp.float32), axis=0)[None],
            grad_taps,
            grad_coef.reshape(1, -1),
            grad_rate.reshape(1, -1),
            jnp.sum(grad_attn.astype(jnp.float32), axis=0)[None],
            jnp.sum(grad_normed2 * scaled2, axis=0)[None],
            jnp.sum(grad_normed2, axis=0)[None],
            jnp.sum(grad_top, axis=0)[None],
        ],
        axis=0,
    )
    mixer_terms = [grad_query, grad_key, grad_value, grad_out, grad_vectors.T]
    mixer_flat = lax.psum_scatter(
        pack_rows(mixer_terms, shard_count), ("wide", "narrow"), scatter_dimension=0, tiled=True
    )
    mixer_sums = unpack_rows(mixer_flat, mixer_terms, shard_count)
    return (
        output,
        input_grad,
        mixer_sums[0],
        mixer_sums[1],
        mixer_sums[2],
        mixer_sums[3],
        mlp_sums[0].T,
        mlp_sums[1],
        mlp_sums[2].reshape(-1),
        mixer_sums[4].T,
    )


def solution(mesh):
    placed = (
        P(("wide", "narrow"), None),
        P(("wide", "narrow")),
        P(("wide", "narrow"), None),
        P(("wide", "narrow"), None),
        P(("wide", "narrow"), None),
        P(("wide", "narrow"), None),
        P(("wide", "narrow"), None),
        P(None, ("wide", "narrow")),
        P(("wide", "narrow"), None),
        P(("wide", "narrow")),
        P(None, ("wide", "narrow")),
    )
    return jax.shard_map(
        on_device,
        mesh=mesh,
        in_specs=placed,
        out_specs=(
            P(("wide", "narrow"), None),
            P(("wide", "narrow"), None),
            P(("wide", "narrow"), None),
            P(("wide", "narrow"), None),
            P(("wide", "narrow"), None),
            P(("wide", "narrow"), None),
            P(None, ("wide", "narrow")),
            P(("wide", "narrow"), None),
            P(("wide", "narrow")),
            P(None, ("wide", "narrow")),
        ),
        check_vma=False,
    )
```

profile of v0, /device:TPU:0, one launch (start us, length us, event | category | flops | bytes accessed | tf_op | source)
XLA Modules:
  0.0 1127.0 jit_solution(4267035099200901943)
XLA Ops:
  12.0 71.0 %all-gather = bf16[32,24,15]{1,2,0:T(8,128)(2,1)S(1)} all-gather(bf16[1,24,15]{1,2,0:T(8,128)(2,1)} %bitcast.217), channel_id=1, replica_groups=mesh['wide'=8,'narrow'=4] {'wide','narrow'}, dimensions={0}, use_global_device_ids=true | all-gather | bytes 23760 | tf_op jit(solution)/shard_map/all_gather | solution.py:152
  88.5 37.1 %all-reduce.13 = bf16[3072]{0:T(1024)(128)(2,1)S(1)} all-reduce(bf16[3072]{0:T(1024)(128)(2,1)S(1)} %dynamic-update-slice), channel_id=1, replica_groups=mesh['wide'=8,'narrow'=4] {'wide','narrow'}, use_global_device_ids=true, to_apply=%add.13 | all-reduce | flops 3072 | bytes 12288
  125.6 1.8 fusion.56
  128.8 1.8 convolution_add_fusion.5
  132.5 46.9 %all-gather.12.cloned.1.call-done = bf16[768,768]{1,0:T(8,128)(2,1)} async-done(((bf16[24,768]{1,0:T(8,128)(2,1)}), bf16[768,768]{1,0:T(8,128)(2,1)}) %all-gather.12.cloned.1.call-update) | async-done | bytes 1179664 | tf_op jit(solution)/shard_map/all_gather | solution.py:147
  179.5 1.8 fusion.57
  182.7 57.0 %while.26 = (s32[]{:T(128)}, f32[12,256,64]{1,2,0:T(8,128)S(1)}, bf16[12,256,64]{2,1,0:T(8,128)(2,1)}, bf16[12,256,64]{2,1,0:T(8,128)(2,1)}, f32[12,256]{1,0:T(8...) while((s32[]{:T(128)}, f32[12,256,64]{1,2,0:T(8,128)S(1)}, ...), condition=%wide.region_4.5_spmd, body=%wide.region_3.4_spmd.sunk | while | flops 16974852 | bytes 3159165 | solution.py:90
  240.0 2.1 fusion.94
  242.4 58.0 %all-gather.18.cloned.1.call-done = bf16[3072,768]{1,0:T(8,128)(2,1)} async-done(((bf16[96,768]{1,0:T(8,128)(2,1)}), bf16[3072,768]{1,0:T(8,128)(2,1)}) %all-gather.18.cloned.1.call-update) | async-done | bytes 4718608 | tf_op jit(solution)/shard_map/all_gather | solution.py:150
  300.4 5.5 fusion.95
  305.9 59.5 %all-gather.16.cloned.1.call-done = bf16[768,3072]{0,1:T(8,128)(2,1)} async-done(((bf16[768,96]{0,1:T(8,128)(2,1)}), bf16[768,3072]{0,1:T(8,128)(2,1)}) %all-gather.16.cloned.1.call-update) | async-done | bytes 4718608 | tf_op jit(solution)/shard_map/all_gather | solution.py:149
  365.5 9.4 convert_reduce_fusion
  374.8 2.1 multiply_reduce_fusion
  381.6 162.5 %while.27 = (s32[]{:T(128)}, bf16[12,256,64]{1,2,0:T(8,128)(2,1)}, f32[12,256,64]{1,2,0:T(8,128)}, f32[12,256,64]{1,2,0:T(8,128)}, f32[12,256]{1,0:T(8,128)}, /*...) while((s32[]{:T(128)}, bf16[12,256,64]{1,2,0:T(8,128)(2,1)}, ...), condition=%wide.region_11.12_spmd, body=%wide.region_9.11_spmd.sunk | while | flops 42501120 | bytes 9659809 | solution.py:121
  387.5 1.7 fusion.146
  401.0 1.7 fusion.146
  414.6 1.7 fusion.146
  428.1 1.7 fusion.146
  441.6 1.7 fusion.146
  455.1 1.7 fusion.146
  468.6 1.7 fusion.146
  482.2 1.7 fusion.146
  495.7 1.7 fusion.146
  509.2 1.7 fusion.146
  522.8 1.7 fusion.146
  536.3 1.7 fusion.146
  549.7 2.0 fusion.76
  551.7 5.2 fusion.80
  559.1 1.8 convert_reduce_fusion.6
  560.9 3.1 fusion.85
  564.0 2.9 reshape.231
  566.9 3.3 constant_dynamic-update-slice_fusion.4
  571.8 2.1 fusion.83
  574.0 2.9 reshape.232
  576.9 2.2 fusion.79
  579.0 2.9 reshape.233
  581.9 3.0 reshape.234
  584.9 1.9 fusion.96
  587.6 2.1 fusion.72
  591.8 3.4 constant_dynamic-update-slice_fusion.3
  599.9 13.5 %reshape.241 = f32[2370816]{0:T(1024)} reshape(f32[32,74088]{1,0:T(8,128)} %constant_dynamic-update-slice_fusion) | data formatting | bytes 18966528 | tf_op jit(solution)/shard_map/reshape | solution.py:68
  613.5 7.7 fusion.81
  621.3 8.2 reshape.247
  629.5 8.1 reshape.246
  637.5 16.8 %pad_maximum_fusion.2 = f32[32,147552]{1,0:T(8,128)} fusion(f32[32,96]{1,0:T(8,128)S(1)} %reshape_broadcast_in_dim.3, f32[32,73728]{1,0:T(8,128)} %reshape.247, f32[32,73728]{1,0:T(8,128)} %reshape.246), kind=kLoop, calls=%fused_computation.54 | loop fusion | flops 9443328 | bytes 37773312 | tf_op jit(solution)/shard_map/concatenate | solution.py:66
  654.3 22.8 %reshape.248 = f32[4721664]{0:T(1024)} reshape(f32[32,147552]{1,0:T(8,128)} %pad_maximum_fusion.2) | data formatting | bytes 37773312 | tf_op jit(solution)/shard_map/reshape | solution.py:68
  679.3 7.0 fusion.55
  686.3 424.2 %all-reduce.19.cloned.1.call-done = (f32[2370816]{0:T(1024)}, f32[4721664]{0:T(1024)}) async-done(((f32[2370816]{0:T(1024)}, f32[4721664]{0:T(1024)}), (f32[2370816]{0:T(1024)}, f32[4721664]{0:T(1024)})) %all-reduce.19.cloned.1.call-update) | async-done | bytes 28369936
  (632 shorter events, 245.2 us)
Async XLA Ops:
  7.2 118.4 %copy-start = (bf16[256,768]{1,0:T(8,128)(2,1)S(1)}, bf16[256,768]{1,0:T(8,128)(2,1)}, u32[]{:S(2)}) copy-start(bf16[256,768]{1,0:T(8,128)(2,1)} %param.15) | copy-start | bytes 1179652
  7.2 81.1 %copy-start.63 = (bf16[96]{0:T(256)(128)(2,1)S(1)}, bf16[96]{0:T(256)(128)(2,1)}, u32[]{:S(2)}) copy-start(bf16[96]{0:T(256)(128)(2,1)} %param.24) | copy-start | bytes 580
  7.2 118.4 %all-gather.8.cloned.1.call-start = ((), (), s32[]{:S(2)}) async-start(), calls=%async_computation | async-start | bytes 1216512 | tf_op jit(solution)/shard_map/all_gather | solution.py:145
  7.9 120.9 %all-gather.10.cloned.1.call-start = ((), (), s32[]{:S(2)}) async-start(), calls=%async_computation.1 | async-start | bytes 1216512 | tf_op jit(solution)/shard_map/all_gather | solution.py:146
  8.7 170.8 %all-gather.12.cloned.1.call-start = ((), (), s32[]{:S(2)}) async-start(), calls=%async_computation.2 | async-start | bytes 1216512 | tf_op jit(solution)/shard_map/all_gather | solution.py:147
  9.4 230.6 %all-gather.14.cloned.1.call-start = ((), (), s32[]{:S(2)}) async-start(), calls=%async_computation.3 | async-start | bytes 1216512 | tf_op jit(solution)/shard_map/all_gather | solution.py:148
  10.0 290.4 %all-gather.18.cloned.1.call-start = ((), (), s32[]{:S(2)}) async-start(), calls=%async_computation.5 | async-start | bytes 4866048 | tf_op jit(solution)/shard_map/all_gather | solution.py:150
  10.6 354.9 %all-gather.16.cloned.1.call-start = ((), (), s32[]{:S(2)}) async-start(), calls=%async_computation.4 | async-start | bytes 4866048 | tf_op jit(solution)/shard_map/all_gather | solution.py:149
  11.2 1099.4 %all-reduce.19.cloned.1.call-start = ((), (), s32[]{:S(2)}) async-start(), calls=%async_computation.6 | async-start | bytes 56745984
  11.2 116.4 %copy-start.64 = (f32[256]{0:T(256)}, f32[256]{0:T(256)S(1)}, u32[]{:S(2)}) copy-start(f32[256]{0:T(256)S(1)} %iota_convert_fusion) | copy-start | bytes 3076
  84.1 46.6 %copy-start.28 = (f32[768]{0:T(1024)}, f32[768]{0:T(1024)S(1)}, u32[]{:S(2)}) copy-start(f32[768]{0:T(1024)S(1)} %get-tuple-element.228) | copy-start | bytes 9220
  84.1 46.6 %copy-start.30 = (f32[768]{0:T(1024)}, f32[768]{0:T(1024)S(1)}, u32[]{:S(2)}) copy-start(f32[768]{0:T(1024)S(1)} %get-tuple-element.225) | copy-start | bytes 9220
  84.1 46.6 %copy-start.32 = (f32[768]{0:T(1024)}, f32[768]{0:T(1024)S(1)}, u32[]{:S(2)}) copy-start(f32[768]{0:T(1024)S(1)} %get-tuple-element.226) | copy-start | bytes 9220
  84.1 46.6 %copy-start.34 = (f32[768]{0:T(1024)}, f32[768]{0:T(1024)S(1)}, u32[]{:S(2)}) copy-start(f32[768]{0:T(1024)S(1)} %get-tuple-element.227) | copy-start | bytes 9220
  84.1 281.3 %copy-start.43 = (f32[768]{0:T(1024)}, f32[768]{0:T(1024)S(1)}, u32[]{:S(2)}) copy-start(f32[768]{0:T(1024)S(1)} %get-tuple-element.220) | copy-start | bytes 9220
  84.1 292.8 %copy-start.26 = (f32[768]{0:T(1024)}, f32[768]{0:T(1024)S(1)}, u32[]{:S(2)}) copy-start(f32[768]{0:T(1024)S(1)} %get-tuple-element.218) | copy-start | bytes 9220
  86.6 92.9 %copy-start.22 = (f32[256]{0:T(256)}, f32[256]{0:T(256)S(1)}, u32[]{:S(2)}) copy-start(f32[256]{0:T(256)S(1)} %add_rsqrt_fusion.1) | copy-start | bytes 3076
  87.3 43.4 %copy-start.53 = (f32[12,64]{1,0:T(8,128)}, f32[12,64]{1,0:T(8,128)S(1)}, u32[]{:S(2)}) copy-start(f32[12,64]{1,0:T(8,128)S(1)} %neg.27) | copy-start | bytes 9220
  87.4 43.3 %copy-start.55 = (f32[12,64]{1,0:T(8,128)}, f32[12,64]{1,0:T(8,128)S(1)}, u32[]{:S(2)}) copy-start(f32[12,64]{1,0:T(8,128)S(1)} %mul.335) | copy-start | bytes 9220
  239.7 60.7 %copy-start.10 = (bf16[256,768]{1,0:T(8,128)(2,1)S(1)}, bf16[256,768]{1,0:T(8,128)(2,1)}, u32[]{:S(2)}) copy-start(bf16[256,768]{1,0:T(8,128)(2,1)} %param.17) | copy-start | bytes 1179652
  240.0 65.9 %copy-start.6 = (f32[256,768]{1,0:T(8,128)}, f32[256,768]{1,0:T(8,128)S(1)}, u32[]{:S(2)}) copy-start(f32[256,768]{1,0:T(8,128)S(1)} %copy.87) | copy-start | bytes 2359300
  242.2 134.8 %copy-start.38 = (f32[256]{0:T(256)}, f32[256]{0:T(256)S(1)}, u32[]{:S(2)}) copy-start(f32[256]{0:T(256)S(1)} %broadcast_multiply_fusion.7) | copy-start | bytes 3076
  242.4 134.6 %copy-start.51 = (f32[256]{0:T(256)}, f32[256]{0:T(256)S(1)}, u32[]{:S(2)}) copy-start(f32[256]{0:T(256)S(1)} %add_rsqrt_fusion) | copy-start | bytes 3076
  365.5 9.4 copy-start.62
  378.0 3.6 copy-start.1
  548.6 3.1 copy-start.19
  548.6 3.1 copy-start.27
  548.6 3.1 copy-start.39
  548.6 3.1 copy-start.44
  548.7 3.0 copy-start.52
  551.7 5.2 copy-start.5
  566.9 3.4 copy-start.14
  566.9 3.4 copy-start.15
  566.9 3.4 copy-start.16
  566.9 3.4 copy-start.29
  566.9 4.9 copy-start.23
  581.9 5.0 copy-start.13
  586.9 3.0 copy-start.45
  587.0 3.0 copy-start.54
  587.0 3.0 copy-start.56
  587.0 3.0 copy-start.65
  587.0 3.7 copy-start.41
  587.0 3.7 copy-start.60
  587.0 3.7 copy-start.59
  587.0 3.7 copy-start.40
  591.8 3.4 copy-start.4
  599.9 13.5 %copy-start.50 = (f32[3072]{0:T(1024)S(1)}, f32[3072]{0:T(1024)}, u32[]{:S(2)}) copy-start(f32[3072]{0:T(1024)} %get-tuple-element.269) | copy-start | bytes 36868
  599.9 13.6 %copy-start.11 = (bf16[256,768]{1,0:T(8,128)(2,1)S(1)}, bf16[256,768]{1,0:T(8,128)(2,1)}, u32[]{:S(2)}) copy-start(bf16[256,768]{1,0:T(8,128)(2,1)} %param.17) | copy-start | bytes 1179652
  (25 other events, 57.5 us)
Sparse Core Ops, SparseCore 0:
  10.8 56.8 all-gather.7
  70.5 53.0 all-gather.9
  126.4 52.9 all-gather.11
  182.1 53.0 all-gather.13
  237.9 62.5 all-gather.17
  303.1 62.3 all-gather.15
  677.2 433.2 all-reduce.18
where the time goes:
time: 1140 us; the launch traced here: 1130 us
  waiting for transfers between devices  592 us (52%)
  local copies, waits for them, and re-layouts  192 us (17%)
  matrix products  158 us (14%)
  blocking collectives  108 us (9%)
  other arithmetic  58.8 us (5%)
  between operations  15.8 us (1%)
    unnamed x8, waiting for transfers between devices  428 us
    all_gather x1, blocking collectives, on_device(): lax.all_gather(vectors, ('wide', 'narrow'), axis=1, tiled=True)  71 us
    all_gather x1, waiting for transfers between devices, on_device(): lax.all_gather(w_fc1, ('wide', 'narrow'), axis=1, tiled=True)  59.5 us
    all_gather x1, waiting for transfers between devices, on_device(): lax.all_gather(w_fc2, ('wide', 'narrow'), axis=0, tiled=True)  58 us
    all_gather x1, waiting for transfers between devices, on_device(): lax.all_gather(w_value, ('wide', 'narrow'), axis=0, tiled=True)  46.9 us
    unnamed x1, blocking collectives  37.1 us
    reshape x2, local copies, waits for them, and re-layouts, pack_rows(): return jnp.concatenate([matrix.reshape(shard_count, -1) for matrix in mat...  36.3 us
    slice x24, local copies, waits for them, and re-layouts, toeplitz(): kernel_row[:1]  28.9 us
  transfers between devices with their start and end apart: 7, of which 4 were waited for; matrix products, arithmetic and copies ran while one was open for 8% of the time, Pallas kernels for 0%

commit v1 on v0

--- a/solution.py
+++ b/solution.py
@@ -1,8 +1,12 @@
+import math
 from functools import partial
+from types import SimpleNamespace
 
 import jax
 import jax.numpy as jnp
 from jax import lax
+from jax.experimental import pallas as pl
+from jax.experimental.pallas import tpu as pltpu
 from jax.sharding import PartitionSpec as P
 
 HEAD_SIZE = 64
@@ -282,6 +286,884 @@
     )
 
 
+f32, bf16 = jnp.float32, jnp.bfloat16
+MESH = pl.DeviceIdType.MESH
+
+
+def dg(left, right, left_dim, right_dim):
+    return lax.dot_general(
+        left, right, (((left_dim,), (right_dim,)), ((), ())), preferred_element_type=f32
+    )
+
+
+def when(condition, body):
+    if condition is None:
+        body()
+    else:
+        pl.when(condition)(body)
+
+
+def both(first, second):
+    if first is None:
+        return second
+    if second is None:
+        return first
+    return jnp.logical_and(first, second)
+
+
+class Links:
+    def __init__(self, depth):
+        wide, z = lax.axis_index("wide"), lax.axis_index("narrow")
+        self.depth = depth
+        self.z, self.core = z, lax.rem(wide, 2)
+        self.x, self.y = lax.rem(lax.div(wide, 2), 2), lax.div(wide, 4)
+        self.me = self.y * 2 + self.x
+        self.xs = self.y * 2 + (1 - self.x)
+        self.ys = (1 - self.y) * 2 + self.x
+        self.ds = (1 - self.y) * 2 + (1 - self.x)
+        self.sib_dev = (self.me * 2 + (1 - self.core), z)
+        self.x_dev = (self.xs * 2 + self.core, z)
+        self.y_dev = (self.ys * 2 + self.core, z)
+        self.up_dev = (wide, z + 1)
+        self.down_dev = (wide, z - 1)
+        self.has_up = z < depth - 1
+        self.has_down = z > 0
+        self.pending = []
+
+    def barrier(self):
+        semaphore = pltpu.get_barrier_semaphore()
+
+        def greet(device):
+            pl.semaphore_signal(semaphore, inc=1, device_id=device, device_id_type=MESH)
+
+        for device in (self.sib_dev, self.x_dev, self.y_dev):
+            greet(device)
+        pl.when(self.has_up)(lambda: greet(self.up_dev))
+        pl.when(self.has_down)(lambda: greet(self.down_dev))
+        peers = 3 + self.has_up.astype(jnp.int32) + self.has_down.astype(jnp.int32)
+        pl.semaphore_wait(semaphore, peers)
+
+    def start(self, condition, source, target, send, receive, device):
+        def build():
+            return pltpu.make_async_remote_copy(
+                src_ref=source(),
+                dst_ref=target(),
+                send_sem=send(),
+                recv_sem=receive(),
+                device_id=device,
+                device_id_type=MESH,
+            )
+
+        when(condition, lambda: build().start())
+        self.pending.append((condition, build))
+
+    def arrive(self, target, receive):
+        pltpu.make_async_remote_copy(
+            src_ref=target,
+            dst_ref=target,
+            send_sem=receive,
+            recv_sem=receive,
+            device_id=self.sib_dev,
+            device_id_type=MESH,
+        ).wait_recv()
+
+    def drain(self):
+        for condition, build in self.pending:
+            when(condition, lambda build=build: build().wait_send())
+        self.pending = []
+
+
+def gather_z_first(k, buf, index, low, rows, half, ss, rs, sib_index=None):
+    depth = k.depth
+
+    def block(yx, zs, lo=0, n=rows):
+        return buf.at[index(yx, zs), pl.ds(low + lo, n)]
+
+    def send(condition, yx, zs, lo, n, device, s, r):
+        ref = lambda: block(yx, zs, lo, n)
+        k.start(condition, ref, ref, lambda: ss.at[s], lambda: rs.at[r], device)
+
+    def to_sib(condition, yx, zs):
+        if sib_index is not None:
+            send(condition, yx, zs, 0, rows, k.sib_dev, 6 * depth + yx * depth + zs, 5 * depth + yx * depth + zs)
+
+    def outward(condition, zs):
+        send(condition, k.me, zs, 0, rows, k.x_dev, 2 * depth + zs, depth + zs)
+        send(condition, k.me, zs, 0, rows, k.y_dev, 3 * depth + zs, 2 * depth + zs)
+        to_sib(condition, k.me, zs)
+
+    def along(condition, zs, up, down):
+        if up:
+            send(both(condition, k.has_up), k.me, zs, 0, rows, k.up_dev, zs, zs)
+        if down:
+            send(both(condition, k.has_down), k.me, zs, 0, rows, k.down_dev, depth + zs, zs)
+
+    def z_step(d):
+        for condition, zs, up in ((k.z >= d, k.z - d, True), (k.z + d < depth, k.z + d, False)):
+            pl.when(condition)(lambda zs=zs: k.arrive(block(k.me, zs), rs.at[zs]))
+            along(condition, zs, up, not up)
+            outward(condition, zs)
+
+    def places(d):
+        if d == 0:
+            return ((None, k.z),)
+        return ((k.z >= d, k.z - d), (k.z + d < depth, k.z + d))
+
+    def xy_step(d):
+        for condition, zs in places(d):
+            when(condition, lambda zs=zs: k.arrive(block(k.xs, zs), rs.at[depth + zs]))
+            send(condition, k.xs, zs, 0, half, k.y_dev, 5 * depth + zs, 4 * depth + zs)
+            to_sib(condition, k.xs, zs)
+            when(condition, lambda zs=zs: k.arrive(block(k.ys, zs), rs.at[2 * depth + zs]))
+            send(condition, k.ys, zs, half, rows - half, k.x_dev, 4 * depth + zs, 3 * depth + zs)
+            to_sib(condition, k.ys, zs)
+
+    def diagonal(d):
+        for condition, zs in places(d):
+            when(condition, lambda zs=zs: k.arrive(block(k.ds, zs, 0, half), rs.at[4 * depth + zs]))
+            when(condition, lambda zs=zs: k.arrive(block(k.ds, zs, half, rows - half), rs.at[3 * depth + zs]))
+            to_sib(condition, k.ds, zs)
+
+    along(None, k.z, True, True)
+    outward(None, k.z)
+    yield
+    for d in range(1, depth):
+        z_step(d)
+        yield
+        xy_step(d - 1)
+        yield
+    xy_step(depth - 1)
+    yield
+    for d in range(depth):
+        diagonal(d)
+    yield
+    if sib_index is not None:
+        for yx in range(4):
+            for zs in range(depth):
+                k.arrive(buf.at[sib_index(yx, zs), pl.ds(low, rows)], rs.at[5 * depth + yx * depth + zs])
+    yield
+
+
+def gather_z_last(k, buf, index, low, rows, half, ss, rs):
+    depth = k.depth
+    yx_of = (k.me, k.xs, k.ys, k.ds)
+
+    def block(yx, zs, lo=0, n=rows):
+        return buf.at[index(yx, zs), pl.ds(low + lo, n)]
+
+    def send(condition, yx, zs, lo, n, device, s, r):
+        ref = lambda: block(yx, zs, lo, n)
+        k.start(condition, ref, ref, lambda: ss.at[s], lambda: rs.at[r], device)
+
+    def along(condition, which, zs, up, down):
+        yx = yx_of[which]
+        place = which * depth + zs
+        if up:
+            send(both(condition, k.has_up), yx, zs, 0, rows, k.up_dev, 4 + place, 4 + place)
+        if down:
+            send(both(condition, k.has_down), yx, zs, 0, rows, k.down_dev, 4 + 4 * depth + place, 4 + place)
+
+    def z_step(which, d):
+        for condition, zs, up in ((k.z >= d, k.z - d, True), (k.z + d < depth, k.z + d, False)):
+            pl.when(condition)(
+                lambda zs=zs: k.arrive(block(yx_of[which], zs), rs.at[4 + which * depth + zs])
+            )
+            along(condition, which, zs, up, not up)
+
+    send(None, k.me, k.z, 0, rows, k.x_dev, 0, 0)
+    send(None, k.me, k.z, 0, rows, k.y_dev, 1, 1)
+    along(None, 0, k.z, True, True)
+    yield
+    k.arrive(block(k.xs, k.z), rs.at[0])
+    send(None, k.xs, k.z, 0, half, k.y_dev, 2, 2)
+    along(None, 1, k.z, True, True)
+    k.arrive(block(k.ys, k.z), rs.at[1])
+    send(None, k.ys, k.z, half, rows - half, k.x_dev, 3, 3)
+    along(None, 2, k.z, True, True)
+    yield
+    k.arrive(block(k.ds, k.z, 0, half), rs.at[2])
+    k.arrive(block(k.ds, k.z, half, rows - half), rs.at[3])
+    along(None, 3, k.z, True, True)
+    yield
+    for d in range(1, depth):
+        for which in range(4):
+            z_step(which, d)
+        yield
+
+
+def add_into(ref, *others):
+    total = ref[...].astype(f32)
+    for other in others:
+        total = total + other[...].astype(f32)
+    ref[...] = total.astype(ref.dtype)
+
+
+def scatter_z_last(k, buf, index, low, rows, half, slots, ss, rs, finish):
+    depth = k.depth
+    from_x_diag, from_y_diag, from_x, from_y, from_up, from_down = slots
+    order = ([0, depth - 1] + list(range(1, depth - 1)))[:depth]
+
+    def block(yx, zd, lo=0, n=rows):
+        return buf.at[index(yx, zd), pl.ds(low + lo, n)]
+
+    def send(condition, source, target, device, s, r):
+        k.start(condition, source, target, lambda: ss.at[s], lambda: rs.at[r], device)
+
+    rest = rows - half
+    for zd in order:
+        send(None, lambda zd=zd: block(k.ds, zd, 0, half), lambda zd=zd: from_y_diag.at[zd], k.y_dev, zd, zd)
+        send(None, lambda zd=zd: block(k.ds, zd, half, rest), lambda zd=zd: from_x_diag.at[zd], k.x_dev, depth + zd, depth + zd)
+    yield
+    for zd in order:
+        send(None, lambda zd=zd: block(k.xs, zd, half, rest), lambda zd=zd: from_x.at[zd, pl.ds(half, rest)], k.x_dev, 2 * depth + zd, 2 * depth + zd)
+        send(None, lambda zd=zd: block(k.ys, zd, 0, half), lambda zd=zd: from_y.at[zd, pl.ds(0, half)], k.y_dev, 3 * depth + zd, 3 * depth + zd)
+    yield
+    for zd in order:
+        k.arrive(from_y_diag.at[zd], rs.at[zd])
+        add_into(block(k.xs, zd, 0, half), from_y_diag.at[zd])
+        send(None, lambda zd=zd: block(k.xs, zd, 0, half), lambda zd=zd: from_x.at[zd, pl.ds(0, half)], k.x_dev, 4 * depth + zd, 4 * depth + zd)
+        k.arrive(from_x_diag.at[zd], rs.at[depth + zd])
+        add_into(block(k.ys, zd, half, rest), from_x_diag.at[zd])
+        send(None, lambda zd=zd: block(k.ys, zd, half, rest), lambda zd=zd: from_y.at[zd, pl.ds(half, rest)], k.y_dev, 5 * depth + zd, 5 * depth + zd)
+        yield
+
+    def collect(zd):
+        k.arrive(from_x.at[zd, pl.ds(half, rest)], rs.at[2 * depth + zd])
+        k.arrive(from_y.at[zd, pl.ds(0, half)], rs.at[3 * depth + zd])
+        k.arrive(from_x.at[zd, pl.ds(0, half)], rs.at[4 * depth + zd])
+        k.arrive(from_y.at[zd, pl.ds(half, rest)], rs.at[5 * depth + zd])
+        add_into(block(k.me, zd), from_x.at[zd], from_y.at[zd])
+
+    for zd in order:
+        collect(zd)
+
+        def down(zd=zd):
+            def take():
+                k.arrive(from_up.at[zd], rs.at[6 * depth + zd])
+                add_into(block(k.me, zd), from_up.at[zd])
+
+            pl.when(k.has_up)(take)
+
+        def up(zd=zd):
+            def take():
+                k.arrive(from_down.at[zd], rs.at[7 * depth + zd])
+                add_into(block(k.me, zd), from_down.at[zd])
+
+            pl.when(k.has_down)(take)
+
+        pl.when(k.z > zd)(down)
+        send(k.z > zd, lambda zd=zd: block(k.me, zd), lambda zd=zd: from_up.at[zd], k.down_dev, 6 * depth + zd, 6 * depth + zd)
+        pl.when(k.z < zd)(up)
+        send(k.z < zd, lambda zd=zd: block(k.me, zd), lambda zd=zd: from_down.at[zd], k.up_dev, 7 * depth + zd, 7 * depth + zd)
+        yield
+
+    finish(block(k.me, k.z), False)
+
+    def last_up():
+        k.arrive(from_up.at[k.z], rs.at[6 * depth + k.z])
+        finish(from_up.at[k.z], True)
+
+    def last_down():
+        k.arrive(from_down.at[k.z], rs.at[7 * depth + k.z])
+        finish(from_down.at[k.z], True)
+
+    pl.when(k.has_up)(last_up)
+    pl.when(k.has_down)(last_down)
+    yield
+
+
+def scatter_z_first(k, buf, index, low, rows, half, slots, ss, rs, finish):
+    depth = k.depth
+    from_x_diag, from_y_diag, from_x, from_y, from_up, from_down = slots
+    yx_of = (k.me, k.xs, k.ys, k.ds)
+    order = ([0, depth - 1] + list(range(1, depth - 1)))[:depth]
+    rest = rows - half
+
+    def block(yx, zd, lo=0, n=rows):
+        return buf.at[index(yx, zd), pl.ds(low + lo, n)]
+
+    def send(condition, source, target, device, s, r):
+        k.start(condition, source, target, lambda: ss.at[s], lambda: rs.at[r], device)
+
+    def z_step(zd, which):
+        yx = yx_of[which]
+        place = which * depth + zd
+
+        def down():
+            def take():
+                k.arrive(from_up.at[place], rs.at[place])
+                add_into(block(yx, zd), from_up.at[place])
+
+            pl.when(k.has_up)(take)
+
+        def up():
+            def take():
+                k.arrive(from_down.at[place], rs.at[4 * depth + place])
+                add_into(block(yx, zd), from_down.at[place])
+
+            pl.when(k.has_down)(take)
+
+        pl.when(k.z > zd)(down)
+        send(k.z > zd, lambda: block(yx, zd), lambda: from_up.at[place], k.down_dev, place, place)
+        pl.when(k.z < zd)(up)
+        send(k.z < zd, lambda: block(yx, zd), lambda: from_down.at[place], k.up_dev, 4 * depth + place, 4 * depth + place)
+
+    for zd in order:
+        for which in (3, 1, 2, 0):
+            z_step(zd, which)
+        yield
+
+    def own(which):
+        yx = yx_of[which]
+        place = which * depth + k.z
+
+        def take_up():
+            k.arrive(from_up.at[place], rs.at[place])
+            add_into(block(yx, k.z), from_up.at[place])
+
+        def take_down():
+            k.arrive(from_down.at[place], rs.at[4 * depth + place])
+            add_into(block(yx, k.z), from_down.at[place])
+
+        pl.when(k.has_up)(take_up)
+        pl.when(k.has_down)(take_down)
+
+    base = 8 * depth
+    own(3)
+    send(None, lambda: block(k.ds, k.z, 0, half), lambda: from_y_diag.at[0], k.y_dev, base, base)
+    send(None, lambda: block(k.ds, k.z, half, rest), lambda: from_x_diag.at[0], k.x_dev, base + 1, base + 1)
+    own(1)
+    send(None, lambda: block(k.xs, k.z, half, rest), lambda: from_x.at[0, pl.ds(half, rest)], k.x_dev, base + 2, base + 2)
+    own(2)
+    send(None, lambda: block(k.ys, k.z, 0, half), lambda: from_y.at[0, pl.ds(0, half)], k.y_dev, base + 3, base + 3)
+    own(0)
+    yield
+    k.arrive(from_y_diag.at[0], rs.at[base])
+    add_into(block(k.xs, k.z, 0, half), from_y_diag.at[0])
+    send(None, lambda: block(k.xs, k.z, 0, half), lambda: from_x.at[0, pl.ds(0, half)], k.x_dev, base + 4, base + 4)
+    k.arrive(from_x_diag.at[0], rs.at[base + 1])
+    add_into(block(k.ys, k.z, half, rest), from_x_diag.at[0])
+    send(None, lambda: block(k.ys, k.z, half, rest), lambda: from_y.at[0, pl.ds(half, rest)], k.y_dev, base + 5, base + 5)
+    yield
+    finish(block(k.me, k.z), False)
+    k.arrive(from_x.at[0, pl.ds(half, rest)], rs.at[base + 2])
+    k.arrive(from_x.at[0, pl.ds(0, half)], rs.at[base + 4])
+    finish(from_x.at[0], True)
+    k.arrive(from_y.at[0, pl.ds(0, half)], rs.at[base + 3])
+    k.arrive(from_y.at[0, pl.ds(half, rest)], rs.at[base + 5])
+    finish(from_y.at[0], True)
+    yield
+
+
+def advance(steps, count=None):
+    if count is None:
+        for _ in steps:
+            pass
+    else:
+        for _ in range(count):
+            next(steps, None)
+
+
+SEQ, WIDTH, UNITS = 256, 768, 96
+HEADS = WIDTH // HEAD_SIZE
+
+
+def row_loop(total, step, body):
+    def once(i, carry):
+        body(pl.multiple_of(i * step, step), step)
+        return carry
+
+    lax.fori_loop(0, total // step, once, 0)
+
+
+def lane_shift(values, offset, left):
+    extent = values.shape[1]
+    lane = lax.broadcasted_iota(jnp.int32, values.shape, 1)
+    if left:
+        return jnp.where(lane < extent - offset, pltpu.roll(values, extent - offset, 1), 0.0)
+    return jnp.where(lane >= offset, pltpu.roll(values, offset, 1), 0.0)
+
+
+def head_rows(h):
+    return pl.ds(pl.multiple_of(h * HEAD_SIZE, HEAD_SIZE), HEAD_SIZE)
+
+
+def scratch_of(depth):
+    devices, blocks = 8 * depth, 4 * depth
+    table = {
+        "qk": ((devices, UNITS, WIDTH), bf16),
+        "ff": ((blocks, 2 * UNITS, WIDTH), bf16),
+        "sm": ((devices, 16, 128), f32),
+        "gff": ((blocks, 2 * UNITS, WIDTH), bf16),
+        "gs": ((devices, 16, 128), f32),
+        "sr": ((blocks, UNITS, WIDTH), bf16),
+        "srs": ((blocks, 16, 128), f32),
+        "wq": ((WIDTH, WIDTH), bf16),
+        "wk": ((WIDTH, WIDTH), bf16),
+        "wv": ((WIDTH, WIDTH), bf16),
+        "wo": ((WIDTH, WIDTH), bf16),
+        "s1": ((SEQ, WIDTH), f32),
+        "i1": ((SEQ, 128), f32),
+        "nm": ((SEQ, WIDTH), bf16),
+        "hid": ((SEQ, WIDTH), f32),
+        "s2": ((SEQ, WIDTH), f32),
+        "i2": ((SEQ, 128), f32),
+        "n2": ((2 * SEQ, WIDTH), bf16),
+        "ct": ((2 * SEQ, WIDTH), bf16),
+        "outp": ((2 * SEQ, WIDTH), f32),
+        "dn2": ((2 * SEQ, WIDTH), f32),
+        "outr": ((SEQ, WIDTH), f32),
+        "dn2r": ((SEQ, WIDTH), f32),
+        "act": ((2 * SEQ, UNITS * depth), bf16),
+        "dp": ((2 * SEQ, UNITS * depth), bf16),
+        "da": ((SEQ, WIDTH), bf16),
+        "dn": ((SEQ, WIDTH), f32),
+        "nmt": ((WIDTH, SEQ), bf16),
+        "qt": ((WIDTH, SEQ), bf16),
+        "kt": ((WIDTH, SEQ), bf16),
+        "vt": ((WIDTH, SEQ), bf16),
+        "krt": ((WIDTH, SEQ), f32),
+        "mt": ((WIDTH, SEQ), bf16),
+        "dmt": ((WIDTH, SEQ), bf16),
+        "dqt": ((WIDTH, SEQ), bf16),
+        "dkt": ((WIDTH, SEQ), bf16),
+        "dvt": ((WIDTH, SEQ), bf16),
+        "kft": ((WIDTH, SEQ), bf16),
+        "vft": ((WIDTH, SEQ), bf16),
+        "ex": ((WIDTH, SEQ), f32),
+        "tt": ((HEADS, SEQ, SEQ), f32),
+        "vec": ((16, WIDTH), f32),
+        "vecc": ((WIDTH, 128), f32),
+        "colsum": ((WIDTH, 128), f32),
+        "gvec": ((16, WIDTH), f32),
+        "bias": ((4, 8, UNITS * depth), f32),
+        "gbias": ((blocks, 8, 128), f32),
+    }
+    for name, rows, half, lanes, kind in (
+        ("q", UNITS, UNITS // 2, WIDTH, bf16),
+        ("b", 128, 64, WIDTH, bf16),
+        ("t", 16, 8, 128, f32),
+    ):
+        table["r" + name + "dx"] = ((depth, rows - half, lanes), kind)
+        table["r" + name + "dy"] = ((depth, half, lanes), kind)
+        for place in ("x", "y", "u", "d"):
+            table["r" + name + place] = ((depth, rows, lanes), kind)
+    table["rcdx"] = table["rcdy"] = ((1, 32, WIDTH), bf16)
+    table["rcx"] = table["rcy"] = ((1, 64, WIDTH), bf16)
+    table["rcu"] = table["rcd"] = ((blocks, 64, WIDTH), bf16)
+    for name, count in (
+        ("gq", 10 * depth), ("gb", 10 * depth), ("gt", 10 * depth), ("gc", 4 + 8 * depth),
+        ("sq", 8 * depth), ("sb", 8 * depth), ("st", 8 * depth), ("sc", 8 * depth + 6), ("e", 12),
+    ):
+        table[name + "_s"] = table[name + "_r"] = count
+    return table
+
+
+INPUTS = ("tok", "cot", "length", "mats", "feed", "small")
+OUTPUTS = ("out", "dinp", "gwq", "gwk", "gwv", "gwo", "gfc1", "gfc2", "gsmall")
+
+
+def layer_kernel(depth, *refs):
+    names = INPUTS + OUTPUTS + tuple(scratch_of(depth))
+    m = SimpleNamespace(**dict(zip(names, refs, strict=True)))
+    k = Links(depth)
+    core = k.core
+
+    def in_all(yx, zs):
+        return (yx * 2 + core) * depth + zs
+
+    def in_all_sib(yx, zs):
+        return (yx * 2 + (1 - core)) * depth + zs
+
+    def in_core(yx, zs):
+        return yx * depth + zs
+
+    def chip_rows(start, step):
+        return pl.ds(pl.multiple_of(core * SEQ + start, step), step)
+
+    core_rows = pl.ds(pl.multiple_of(core * SEQ, SEQ), SEQ)
+    sib_rows = pl.ds(pl.multiple_of((1 - core) * SEQ, SEQ), SEQ)
+
+    def swap(place, source, target):
+        k.start(None, lambda: source, lambda: target, lambda: m.e_s.at[place], lambda: m.e_r.at[place], k.sib_dev)
+
+    own_all, own_core = in_all(k.me, k.z), in_core(k.me, k.z)
+    m.qk[own_all] = m.mats[...]
+    m.sm[own_all] = m.small[...]
+    m.ff[own_core] = m.feed[...]
+    m.ct[core_rows] = m.cot[...]
+
+    k.barrier()
+    g_small = gather_z_first(k, m.sm, in_all, 0, 16, 8, m.gt_s, m.gt_r, in_all_sib)
+    g_mats = gather_z_first(k, m.qk, in_all, 0, UNITS, UNITS // 2, m.gq_s, m.gq_r, in_all_sib)
+    g_feed = gather_z_first(k, m.ff, in_core, 0, 128, 64, m.gb_s, m.gb_r)
+    g_last = gather_z_last(k, m.ff, in_core, 128, 64, 32, m.gc_s, m.gc_r)
+    advance(g_small, 1)
+    advance(g_mats, 1)
+    swap(0, m.ct.at[core_rows], m.ct.at[core_rows])
+
+    def norm1(start, step):
+        rows = pl.ds(start, step)
+        tokens = m.tok[rows].astype(f32)
+        centred = tokens - jnp.mean(tokens, axis=1, keepdims=True)
+        inverse = lax.rsqrt(jnp.mean(centred * centred, axis=1, keepdims=True) + EPSILON)
+        m.s1[rows] = centred * inverse
+        m.i1[rows] = jnp.broadcast_to(inverse, (step, 128))
+
+    row_loop(SEQ, 32, norm1)
+    advance(g_small)
+
+    total = jnp.zeros((16, WIDTH), f32)
+    for wide in range(8):
+        part = jnp.zeros((16, 128), f32)
+        for zs in range(depth):
+            tile = m.sm[wide * depth + zs]
+            part = part + (pltpu.roll(tile, 24 * zs, 1) if zs else tile)
+        padded = jnp.concatenate([part, jnp.zeros((16, WIDTH - 128), f32)], axis=1)
+        total = total + (pltpu.roll(padded, 96 * wide, 1) if wide else padded)
+    m.vec[...] = total
+    m.vecc[...] = jnp.transpose(jnp.concatenate([total, jnp.zeros((112, WIDTH), f32)], axis=0))
+    for yx in range(4):
+        line = jnp.zeros((16, UNITS * depth), f32)
+        for zs in range(depth):
+            tile = jnp.concatenate([m.sm[in_all(yx, zs)], jnp.zeros((16, UNITS * depth - 128), f32)], axis=1)
+            line = line + (pltpu.roll(tile, UNITS * zs, 1) if zs else tile)
+        m.bias[yx] = line[8:16]
+
+    day = lax.broadcasted_iota(jnp.int32, (1, SEQ), 1).astype(f32)
+    s_at = lax.broadcasted_iota(jnp.int32, (SEQ, SEQ), 0)
+    t_at = lax.broadcasted_iota(jnp.int32, (SEQ, SEQ), 1)
+    valid = (lax.broadcasted_iota(jnp.int32, (1, SEQ), 1) < m.length[0]).astype(f32)
+
+    def head_kernel(h, carry):
+        rows = head_rows(h)
+        decays = jnp.exp(-m.vecc[rows, 10:11] * day)
+        m.ex[rows] = decays
+        line = jnp.sum(m.vecc[rows, 9:10] * decays, axis=0, keepdims=True) * (1.0 / STATE)
+        matrix = pltpu.roll(jnp.broadcast_to(line, (SEQ, SEQ)), 0, 1, stride=1, stride_axis=0)
+        m.tt[h] = jnp.where(t_at >= s_at, matrix, 0.0)
+        return carry
+
+    lax.fori_loop(0, HEADS, head_kernel, 0)
+
+    def gain1(start, step):
+        rows = pl.ds(start, step)
+        m.nm[rows] = (m.s1[rows] * m.vec[0:1] + m.vec[1:2]).astype(bf16)
+
+    row_loop(SEQ, 32, gain1)
+    m.nmt[...] = jnp.transpose(m.nm[...])
+
+    advance(g_mats)
+    advance(g_feed, 1)
+    advance(g_last, 1)
+
+    def unpack(w, carry):
+        rows = pl.ds(pl.multiple_of(w * 96, 96), 96)
+        for place, (first, second) in enumerate(((m.wq, m.wk), (m.wv, m.wo))):
+            pair = m.qk[pl.ds(w * depth, depth), 48 * place : 48 * place + 48, :].astype(f32)
+            first[rows] = pair[:, :24].reshape(96, WIDTH).astype(bf16)
+            second[rows] = pair[:, 24:].reshape(96, WIDTH).astype(bf16)
+        return carry
+
+    lax.fori_loop(0, 8, unpack, 0)
+
+    m.qt[...] = jnp.transpose(dg(m.nm[...], m.wq[...], 1, 0) + m.vec[2:3]).astype(bf16)
+    m.krt[...] = jnp.transpose(dg(m.nm[...], m.wk[...], 1, 0) + m.vec[3:4])
+    m.vt[...] = (jnp.transpose(dg(m.nm[...], m.wv[...], 1, 0) + m.vec[4:5]) * valid).astype(bf16)
+
+    def mix_head(h, carry):
+        rows = head_rows(h)
+        raw = m.krt[rows]
+        summed = raw * m.vecc[rows, 5:6]
+        for j in range(1, 4):
+            summed = summed + lane_shift(raw, j, False) * m.vecc[rows, 5 + j : 6 + j]
+        keys = (summed * valid).astype(bf16)
+        m.kt[rows] = keys
+        scores = dg(keys, m.qt[rows], 0, 0) * (1.0 / HEAD_SIZE)
+        weights = (scores * m.tt[h]).astype(bf16)
+        m.mt[rows] = (dg(m.vt[rows], weights, 1, 0) * valid).astype(bf16)
+        return carry
+
+    lax.fori_loop(0, HEADS, mix_head, 0)
+    m.hid[...] = dg(m.mt[...], m.wo[...], 0, 0)
+
+    def norm2(start, step):
+        rows = pl.ds(start, step)
+        hidden = m.tok[rows].astype(f32) + m.hid[rows] + m.vec[11:12]
+        m.hid[rows] = hidden
+        centred = hidden - jnp.mean(hidden, axis=1, keepdims=True)
+        inverse = lax.rsqrt(jnp.mean(centred * centred, axis=1, keepdims=True) + EPSILON)
+        scaled = centred * inverse
+        m.s2[rows] = scaled
+        m.i2[rows] = jnp.broadcast_to(inverse, (step, 128))
+        m.n2[chip_rows(start, step)] = (scaled * m.vec[12:13] + m.vec[13:14]).astype(bf16)
+
+    row_loop(SEQ, 32, norm2)
+    swap(1, m.n2.at[core_rows], m.n2.at[core_rows])
+
+    advance(g_feed)
+    advance(g_last)
+    k.arrive(m.ct.at[sib_rows], m.e_r.at[0])
+    k.arrive(m.n2.at[sib_rows], m.e_r.at[1])
+
+    root = math.sqrt(2.0 / math.pi)
+    chunk = UNITS * depth
+    lane = lax.broadcasted_iota(jnp.int32, (1, 128), 1)
+    for which, yx in enumerate((k.me, k.xs, k.ys, k.ds)):
+        blocks = pl.ds(yx * depth, depth)
+        fc1 = m.ff[blocks, 0:UNITS, :].reshape(chunk, WIDTH)
+        fc2 = m.ff[blocks, UNITS : 2 * UNITS, :].reshape(chunk, WIDTH)
+        for r in range(2):
+            rows = pl.ds(r * SEQ, SEQ)
+            pre = dg(m.n2[rows], fc1, 1, 1) + m.bias[yx, 7:8]
+            square = pre * pre
+            tanh = jnp.tanh(root * pre * (1.0 + 0.044715 * square))
+            half = 0.5 * (1.0 + tanh)
+            slope = half + 0.5 * pre * (1.0 - tanh * tanh) * (root * (1.0 + 3 * 0.044715 * square))
+            activated = (pre * half).astype(bf16)
+            grad_pre = (dg(m.ct[rows], fc2, 1, 1) * slope).astype(bf16)
+            m.act[rows] = activated
+            m.dp[rows] = grad_pre
+            if which == 0:
+                m.outp[rows] = dg(activated, fc2, 1, 0)
+                m.dn2[rows] = dg(grad_pre, fc1, 1, 0)
+            else:
+                m.outp[rows] += dg(activated, fc2, 1, 0)
+                m.dn2[rows] += dg(grad_pre, fc1, 1, 0)
+        if which == 3:
+            k.drain()
+            swap(2, m.dn2.at[sib_rows], m.dn2r)
+            swap(3, m.outp.at[sib_rows], m.outr)
+        m.gff[blocks, 0:UNITS] = dg(m.dp[...], m.n2[...], 0, 0).astype(bf16).reshape(depth, UNITS, WIDTH)
+        m.gff[blocks, UNITS : 2 * UNITS] = (
+            dg(m.act[...], m.ct[...], 0, 0).astype(bf16).reshape(depth, UNITS, WIDTH)
+        )
+        sums = jnp.sum(m.dp[...].astype(f32), axis=0, keepdims=True)
+        for zs in range(depth):
+            line = (pltpu.roll(sums, chunk - UNITS * zs, 1) if zs else sums)[:, :128]
+            m.gbias[yx * depth + zs] = jnp.broadcast_to(jnp.where(lane < UNITS, line, 0.0), (8, 128))
+
+    def finish_feed(ref, more):
+        value = ref[...].astype(f32)
+        for target, low, high in ((m.gfc1, 0, UNITS), (m.gfc2.at[0:32], UNITS, 128)):
+            target[...] = target[...] + value[low:high] if more else value[low:high]
+
+    def finish_last(ref, more):
+        value = ref[...].astype(f32)
+        m.gfc2[32:96] = m.gfc2[32:96] + value if more else value
+
+    def finish_mats(ref, more):
+        value = ref[...].astype(f32)
+        for place, target in enumerate((m.gwq, m.gwk, m.gwv, m.gwo)):
+            part = value[24 * place : 24 * place + 24]
+            target[...] = target[...] + part if more else part
+
+    def finish_small(ref, more):
+        m.gsmall[...] = m.gsmall[...] + ref[...] if more else ref[...]
+
+    s_feed = scatter_z_last(
+        k, m.gff, in_core, 0, 128, 64, (m.rbdx, m.rbdy, m.rbx, m.rby, m.rbu, m.rbd), m.sb_s, m.sb_r, finish_feed
+    )
+    s_last = scatter_z_first(
+        k, m.gff, in_core, 128, 64, 32, (m.rcdx, m.rcdy, m.rcx, m.rcy, m.rcu, m.rcd), m.sc_s, m.sc_r, finish_last
+    )
+    s_mats = scatter_z_last(
+        k, m.qk, in_all, 0, UNITS, UNITS // 2, (m.rqdx, m.rqdy, m.rqx, m.rqy, m.rqu, m.rqd), m.sq_s, m.sq_r, finish_mats
+    )
+    s_small = scatter_z_last(
+        k, m.gs, in_all, 0, 16, 8, (m.rtdx, m.rtdy, m.rtx, m.rty, m.rtu, m.rtd), m.st_s, m.st_r, finish_small
+    )
+    advance(s_feed, 2)
+    advance(s_last, 1)
+
+    m.gvec[...] = jnp.zeros((16, WIDTH), f32)
+    k.arrive(m.dn2r, m.e_r.at[2])
+
+    def back2(start, step):
+        rows = pl.ds(start, step)
+        grad_normed = m.dn2[chip_rows(start, step)] + m.dn2r[rows]
+        scaled = m.s2[rows]
+        grad_in = grad_normed * m.vec[12:13]
+        first = jnp.mean(grad_in, axis=1, keepdims=True)
+        second = jnp.mean(grad_in * scaled, axis=1, keepdims=True)
+        top = m.cot[rows].astype(f32)
+        grad_hidden = top + m.i2[rows, 0:1] * (grad_in - first - scaled * second)
+        m.s2[rows] = grad_hidden
+        rounded = grad_hidden.astype(bf16)
+        m.da[rows] = rounded
+        m.gvec[11:12] += jnp.sum(rounded.astype(f32), axis=0, keepdims=True)
+        m.gvec[12:13] += jnp.sum(grad_normed * scaled, axis=0, keepdims=True)
+        m.gvec[13:14] += jnp.sum(grad_normed, axis=0, keepdims=True)
+        m.gvec[14:15] += jnp.sum(top, axis=0, keepdims=True)
+
+    row_loop(SEQ, 32, back2)
+    m.dmt[...] = (jnp.transpose(dg(m.da[...], m.wo[...], 1, 1)) * valid).astype(bf16)
+
+    def back_head(h, carry):
+        rows = head_rows(h)
+        queries, keys, grad_mixed, kernel = m.qt[rows], m.kt[rows], m.dmt[rows], m.tt[h]
+        scores = dg(keys, queries, 0, 0) * (1.0 / HEAD_SIZE)
+        weights = (scores * kernel).astype(bf16)
+        grad_weights = dg(m.vt[rows], grad_mixed, 0, 0)
+        grad_values = (dg(grad_mixed, weights, 1, 1) * valid).astype(bf16)
+        m.dvt[rows] = grad_values
+        grad_scores = (grad_weights * kernel).astype(bf16)
+        grad_queries = (dg(keys, grad_scores, 1, 0) * (1.0 / HEAD_SIZE)).astype(bf16)
+        m.dqt[rows] = grad_queries
+        grad_keys = dg(queries, grad_scores, 1, 1) * (1.0 / HEAD_SIZE) * valid
+        raw = m.krt[rows]
+        at = lax.broadcasted_iota(jnp.int32, (HEAD_SIZE, 128), 1)
+        grad_raw = grad_keys * m.vecc[rows, 5:6]
+        sums = jnp.where(at == 5, jnp.sum(grad_keys * raw, axis=1, keepdims=True), 0.0)
+        for j in range(1, 4):
+            grad_raw = grad_raw + lane_shift(grad_keys, j, True) * m.vecc[rows, 5 + j : 6 + j]
+            tap = jnp.sum(grad_keys * lane_shift(raw, j, False), axis=1, keepdims=True)
+            sums = jnp.where(at == 5 + j, tap, sums)
+        rounded = grad_raw.astype(bf16)
+        m.dkt[rows] = rounded
+        for place, value in ((2, grad_queries), (3, rounded), (4, grad_values)):
+            sums = jnp.where(at == place, jnp.sum(value.astype(f32), axis=1, keepdims=True), sums)
+        m.colsum[rows] = sums
+        return carry
+
+    lax.fori_loop(0, HEADS, back_head, 0)
+
+    def pack(w, carry):
+        rows = pl.ds(pl.multiple_of(w * 96, 96), 96)
+        normed = m.nmt[rows]
+        grads = (
+            dg(normed, m.dqt[...], 1, 1),
+            dg(normed, m.dkt[...], 1, 1),
+            dg(normed, m.dvt[...], 1, 1),
+            dg(m.mt[rows], m.da[...], 1, 0),
+        )
+        for place in range(2):
+            pair = [grad.reshape(depth, 24, WIDTH) for grad in grads[2 * place : 2 * place + 2]]
+            m.qk[pl.ds(w * depth, depth), 48 * place : 48 * place + 48, :] = jnp.concatenate(pair, axis=1).astype(bf16)
+        return carry
+
+    lax.fori_loop(0, 8, pack, 0)
+    for yx in range(4):
+        swap(4 + yx, m.qk.at[pl.ds(in_all_sib(yx, 0), depth)], m.sr.at[pl.ds(yx * depth, depth)])
+
+    advance(s_feed, 2)
+
+    m.dn[...] = jnp.transpose(
+        dg(m.wq[...], m.dqt[...], 1, 0) + dg(m.wk[...], m.dkt[...], 1, 0) + dg(m.wv[...], m.dvt[...], 1, 0)
+    )
+
+    def back1(start, step):
+        rows = pl.ds(start, step)
+        grad_normed, scaled = m.dn[rows], m.s1[rows]
+        grad_in = grad_normed * m.vec[0:1]
+        first = jnp.mean(grad_in, axis=1, keepdims=True)
+        second = jnp.mean(grad_in * scaled, axis=1, keepdims=True)
+        m.dinp[rows] = (m.s2[rows] + m.i1[rows, 0:1] * (grad_in - first - scaled * second)).astype(bf16)
+        m.gvec[0:1] += jnp.sum(grad_normed * scaled, axis=0, keepdims=True)
+        m.gvec[1:2] += jnp.sum(grad_normed, axis=0, keepdims=True)
+
+    row_loop(SEQ, 32, back1)
+
+    for yx in range(4):
+        k.arrive(m.sr.at[pl.ds(yx * depth, depth)], m.e_r.at[4 + yx])
+
+        def presum(zs, carry, yx=yx):
+            add_into(m.qk.at[in_all(yx, zs)], m.sr.at[yx * depth + zs])
+            return carry
+
+        lax.fori_loop(0, depth, presum, 0)
+    advance(s_mats, 2)
+
+    flip = (s_at + t_at == SEQ - 1).astype(bf16)
+    m.kft[...] = dg(m.kt[...], flip, 1, 0).astype(bf16)
+    m.vft[...] = dg(m.vt[...], flip, 1, 0).astype(bf16)
+
+    def kernel_head(h, carry):
+        rows = head_rows(h)
+        scores = dg(m.kft[rows], m.qt[rows], 0, 0) * (1.0 / HEAD_SIZE)
+        grad_weights = dg(m.vft[rows], m.dmt[rows], 0, 0)
+        product = jnp.where(s_at + t_at >= SEQ - 1, scores * grad_weights, 0.0)
+        lined = pltpu.roll(product, 1, 1, stride=1, stride_axis=0)
+        grad_kernel = jnp.sum(lined, axis=0, keepdims=True) * (1.0 / STATE)
+        part = m.ex[rows] * grad_kernel
+        at = lax.broadcasted_iota(jnp.int32, (HEAD_SIZE, 128), 1)
+        grad_rate = -m.vecc[rows, 9:10] * jnp.sum(part * day, axis=1, keepdims=True)
+        sums = jnp.where(at == 9, jnp.sum(part, axis=1, keepdims=True), m.colsum[rows])
+        m.colsum[rows] = jnp.where(at == 10, grad_rate, sums)
+        return carry
+
+    lax.fori_loop(0, HEADS, kernel_head, 0)
+    grads = m.gvec[...] + jnp.transpose(m.colsum[...])[0:16]
+    row_at = lax.broadcasted_iota(jnp.int32, (16, 128), 0)
+    lane_at = lax.broadcasted_iota(jnp.int32, (16, 128), 1)
+    for wide in range(8):
+        turned = (pltpu.roll(grads, WIDTH - 96 * wide, 1) if wide else grads)[:, :128]
+        for zs in range(depth):
+            tile = pltpu.roll(turned, 128 - 24 * zs, 1) if zs else turned
+            tile = jnp.where((lane_at < 24) & (row_at < 15), tile, 0.0)
+            own = jnp.concatenate([jnp.zeros((8, 128), f32), m.gbias[(wide // 2) * depth + zs]], axis=0)
+            mine = (row_at == 15) & (core == wide % 2)
+            m.gs[wide * depth + zs] = jnp.where(mine, own, tile)
+    for yx in range(4):
+        swap(8 + yx, m.gs.at[pl.ds(in_all_sib(yx, 0), depth)], m.srs.at[pl.ds(yx * depth, depth)])
+
+    def finish_out(start, step):
+        rows = pl.ds(start, step)
+        m.out[rows] = (m.hid[rows] + (m.outp[chip_rows(start, step)] + m.outr[rows]) + m.vec[14:15]).astype(bf16)
+
+    k.arrive(m.outr, m.e_r.at[3])
+    row_loop(SEQ, 32, finish_out)
+    for yx in range(4):
+        k.arrive(m.srs.at[pl.ds(yx * depth, depth)], m.e_r.at[8 + yx])
+        for zs in range(depth):
+            add_into(m.gs.at[in_all(yx, zs)], m.srs.at[yx * depth + zs])
+    advance(s_small, 2)
+    advance(s_feed)
+    advance(s_last)
+    advance(s_mats)
+    advance(s_small)
+    k.drain()
+
+
+def on_device_fast(
+    tokens, lengths, cotangent, w_query, w_key, w_value, w_out, w_fc1, w_fc2, fc1_bias, vectors
+):
+    depth = lax.axis_size("narrow")
+    mats = jnp.concatenate([w_query, w_key, w_value, w_out], axis=0)
+    feed = jnp.concatenate([w_fc1.T, w_fc2], axis=0)
+    small = jnp.concatenate(
+        [jnp.pad(vectors, ((0, 0), (0, 104))), jnp.pad(fc1_bias, (0, 32))[None]], axis=0
+    ).astype(f32)
+    scratch = []
+    for entry in scratch_of(depth).values():
+        scratch.append(pltpu.SemaphoreType.DMA((entry,)) if isinstance(entry, int) else pltpu.VMEM(*entry))
+    in_vmem = pl.BlockSpec(memory_space=pltpu.VMEM)
+    in_smem = pl.BlockSpec(memory_space=pltpu.SMEM)
+    shape = jax.ShapeDtypeStruct
+    got = pl.pallas_call(
+        partial(layer_kernel, depth),
+        out_shape=[shape((SEQ, WIDTH), bf16)] * 2
+        + [shape((24, WIDTH), f32)] * 4
+        + [shape((UNITS, WIDTH), f32)] * 2
+        + [shape((16, 128), f32)],
+        in_specs=[in_vmem, in_vmem, in_smem, in_vmem, in_vmem, in_vmem],
+        out_specs=[in_vmem] * 9,
+        scratch_shapes=scratch,
+        compiler_params=pltpu.CompilerParams(
+            collective_id=0, has_side_effects=True, vmem_limit_bytes=63 * 2**20
+        ),
+        name="h3_layer",
+    )(tokens, cotangent, lengths, mats, feed, small)
+    out, grad_in, g_query, g_key, g_value, g_out, g_fc1, g_fc2, g_small = got
+    return (
+        out, grad_in, g_query, g_key, g_value, g_out, g_fc1.T, g_fc2, g_small[15, :UNITS], g_small[:15, :24],
+    )
+
+
+def fits(mesh):
+    return mesh.shape["wide"] == 8 and mesh.shape["narrow"] == 4
+
+
 def solution(mesh):
     placed = (
         P(("wide", "narrow"), None),
@@ -297,7 +1179,7 @@
         P(None, ("wide", "narrow")),
     )
     return jax.shard_map(
-        on_device,
+        on_device_fast if fits(mesh) else on_device,
         mesh=mesh,
         in_specs=placed,
         out_specs=(

time: 1140 us -> 238 us (0.21); the launches traced: 1130 us -> 237 us
  waiting for transfers between devices: 592 us -> 0 us
  Pallas kernels: 0 us -> 223 us
  local copies, waits for them, and re-layouts: 192 us -> 9.79 us
  matrix products: 158 us -> 0 us
  blocking collectives: 108 us -> 0 us
  other arithmetic: 58.8 us -> 2.88 us
  between operations: 15.8 us -> 1.35 us
    unnamed x8 -> x0, waiting for transfers between devices: 428 us -> none
    pallas_call x0 -> x1, Pallas kernels: none -> 223 us  [on_device_fast(): pl.pallas_call(partial(layer_kernel, depth), out_shape=[shape((SEQ, WIDTH...]
    all_gather x6 -> x0, waiting for transfers between devices: 164 us -> none  [the longest x1 59.5 us: on_device(): lax.all_gather(w_fc1, ('wide', 'narrow'), axis=1, tiled=True)]
    dot_general x90 -> x0, matrix products: 158 us -> none  [the longest x12 20 us: head_backward(): jnp.dot(grad_scores, key_head, preferred_element_type=jnp.float32)]
    reshape x72 -> x0, local copies, waits for them, and re-layouts: 87.9 us -> none  [the longest x2 36.3 us: pack_rows(): return jnp.concatenate([matrix.reshape(shard_count, -1) for matrix in mat...]
    all_gather x1 -> x0, blocking collectives: 71 us -> none  [on_device(): lax.all_gather(vectors, ('wide', 'narrow'), axis=1, tiled=True)]
    slice x52 -> x0, local copies, waits for them, and re-layouts: 52 us -> none  [the longest x24 28.9 us: toeplitz(): kernel_row[:1]]
    unnamed x1 -> x0, blocking collectives: 37.1 us -> none
  transfers between devices with their start and end apart: 7 -> 0, of which waited for: 4 -> 0; matrix products, arithmetic and copies ran while one was open for 8% -> 0% of each run, Pallas kernels for 0% -> 0%
where the time goes in v1:
time: 238 us; the launch traced here: 237 us
  Pallas kernels  223 us (94%)
  local copies, waits for them, and re-layouts  9.79 us (4%)
  other arithmetic  2.88 us (1%)
    pallas_call x1, Pallas kernels, on_device_fast(): pl.pallas_call(partial(layer_kernel, depth), out_shape=[shape((SEQ, WIDTH...  223 us
    unnamed x31, local copies, waits for them, and re-layouts  8.62 us

profile of v1, /device:TPU:0, one launch (start us, length us, event | category | flops | bytes accessed | tf_op | source)
XLA Modules:
  0.0 237.4 jit_solution(1188568194225070773)
XLA Ops:
  0.6 0.0 copy-start.10
  1.3 0.7 pad_bitcast_fusion
  2.0 0.0 copy-done.10
  2.0 0.6 fusion.2.refs_5_
  2.6 0.0 copy-start.3
  2.6 0.0 copy-start.4
  2.6 1.5 pad_maximum_fusion.1.refs_3_
  4.1 0.0 copy-done.3
  4.1 0.0 copy-done.4
  4.1 0.7 pad_maximum_fusion.refs_4_
  4.9 223.4 %h3_layer.1 = (bf16[256,768]{1,0:T(8,128)(2,1)}, bf16[256,768]{1,0:T(8,128)(2,1)}, f32[24,768]{1,0:T(8,128)}, f32[24,768]{1,0:T(8,128)}, f32[24,768]{1,0:T(8,128...) custom-call(bf16[256,768]{1,0:T(8,128)(2,1)} %refs_0_.1, ...), custom_call_target="tpu_custom_call" | custom-call | tf_op jit(solution)/shard_map/h3_layer/pallas_call | solution.py:1143
  228.3 0.0 copy-start.9
  228.3 0.7 copy-done.9
  229.0 0.5 slice_bitcast_fusion
  229.5 0.0 copy-start
  229.5 1.8 copy.31
  231.3 0.0 copy-done
  231.3 0.0 copy-start.8
  231.3 0.0 copy-start.7
  231.3 0.0 copy-start.6
  231.3 0.7 copy.32
  232.1 0.1 copy-done.8
  232.2 0.0 copy-start.2
  232.2 0.6 copy.33
  232.9 0.0 copy-done.7
  232.9 0.6 copy.34
  233.5 0.0 copy-done.6
  233.5 0.0 copy-start.5
  233.5 0.6 copy.35
  234.1 0.3 copy-done.5
  234.4 0.6 copy.36
  235.0 0.0 copy-done.2
  235.0 0.0 copy-start.1
  235.0 0.7 copy.37
  235.8 0.4 copy-done.1
  236.1 0.7 copy.38
  236.8 0.6 copy.39
Async XLA Ops:
  0.6 1.3 copy-start.10
  2.6 1.5 copy-start.3
  2.6 1.5 copy-start.4
  228.3 0.7 copy-start.9
  229.5 1.8 copy-start
  231.3 0.9 copy-start.8
  231.3 1.5 copy-start.7
  231.3 2.2 copy-start.6
  232.2 2.8 %copy-start.2 = (f32[96,768]{1,0:T(8,128)S(1)}, f32[96,768]{1,0:T(8,128)}, u32[]{:S(2)}) copy-start(f32[96,768]{1,0:T(8,128)} %get-tuple-element.25) | copy-start | bytes 884740
  233.5 0.9 copy-start.5
  235.0 1.1 copy-start.1

commit v2 on v0

--- a/solution.py
+++ b/solution.py
@@ -1,8 +1,12 @@
+import math
 from functools import partial
+from types import SimpleNamespace
 
 import jax
 import jax.numpy as jnp
 from jax import lax
+from jax.experimental import pallas as pl
+from jax.experimental.pallas import tpu as pltpu
 from jax.sharding import PartitionSpec as P
 
 HEAD_SIZE = 64
@@ -282,6 +286,1022 @@
     )
 
 
+f32, bf16 = jnp.float32, jnp.bfloat16
+MESH = pl.DeviceIdType.MESH
+
+
+def dg(left, right, left_dim, right_dim):
+    return lax.dot_general(
+        left, right, (((left_dim,), (right_dim,)), ((), ())), preferred_element_type=f32
+    )
+
+
+def when(condition, body):
+    if condition is None:
+        body()
+    else:
+        pl.when(condition)(body)
+
+
+def both(first, second):
+    if first is None:
+        return second
+    if second is None:
+        return first
+    return jnp.logical_and(first, second)
+
+
+class Links:
+    def __init__(self, depth):
+        wide, z = lax.axis_index("wide"), lax.axis_index("narrow")
+        self.depth = depth
+        self.z, self.core = z, lax.rem(wide, 2)
+        self.x, self.y = lax.rem(lax.div(wide, 2), 2), lax.div(wide, 4)
+        self.me = self.y * 2 + self.x
+        self.xs = self.y * 2 + (1 - self.x)
+        self.ys = (1 - self.y) * 2 + self.x
+        self.ds = (1 - self.y) * 2 + (1 - self.x)
+        self.sib_dev = (self.me * 2 + (1 - self.core), z)
+        self.x_dev = (self.xs * 2 + self.core, z)
+        self.y_dev = (self.ys * 2 + self.core, z)
+        self.up_dev = (wide, z + 1)
+        self.down_dev = (wide, z - 1)
+        self.has_up = z < depth - 1
+        self.has_down = z > 0
+        self.pending = {}
+
+    def barrier(self):
+        semaphore = pltpu.get_barrier_semaphore()
+
+        def greet(device):
+            pl.semaphore_signal(semaphore, inc=1, device_id=device, device_id_type=MESH)
+
+        for device in (self.sib_dev, self.x_dev, self.y_dev):
+            greet(device)
+        pl.when(self.has_up)(lambda: greet(self.up_dev))
+        pl.when(self.has_down)(lambda: greet(self.down_dev))
+        peers = 3 + self.has_up.astype(jnp.int32) + self.has_down.astype(jnp.int32)
+        pl.semaphore_wait(semaphore, peers)
+
+    def start(self, condition, source, target, send, receive, device, group=""):
+        def build():
+            return pltpu.make_async_remote_copy(
+                src_ref=source(),
+                dst_ref=target(),
+                send_sem=send(),
+                recv_sem=receive(),
+                device_id=device,
+                device_id_type=MESH,
+            )
+
+        when(condition, lambda: build().start())
+        self.pending.setdefault(group, []).append((condition, build))
+
+    def arrive(self, target, receive):
+        pltpu.make_async_remote_copy(
+            src_ref=target,
+            dst_ref=target,
+            send_sem=receive,
+            recv_sem=receive,
+            device_id=self.sib_dev,
+            device_id_type=MESH,
+        ).wait_recv()
+
+    def drain(self, *groups):
+        for group in groups or tuple(self.pending):
+            for condition, build in self.pending.pop(group, ()):
+                when(condition, lambda build=build: build().wait_send())
+
+
+def near(k, distance):
+    if distance == 0:
+        return ((None, k.z, False),)
+    return ((k.z >= distance, k.z - distance, True), (k.z + distance < k.depth, k.z + distance, False))
+
+
+def gather_z_first(k, name, buf, index, low, rows, half, ss, rs, sib_index=None):
+    depth = k.depth
+
+    def block(yx, zs, lo=0, n=rows):
+        return buf.at[index(yx, zs), pl.ds(low + lo, n)]
+
+    def send(condition, yx, zs, lo, n, device, s, r):
+        ref = lambda: block(yx, zs, lo, n)
+        k.start(condition, ref, ref, lambda: ss.at[s], lambda: rs.at[r], device, name)
+
+    def to_sib(condition, yx, zs):
+        if sib_index is not None:
+            send(condition, yx, zs, 0, rows, k.sib_dev, 6 * depth + yx * depth + zs, 5 * depth + yx * depth + zs)
+
+    def outward(condition, zs):
+        send(condition, k.me, zs, 0, rows, k.x_dev, 2 * depth + zs, depth + zs)
+        send(condition, k.me, zs, 0, rows, k.y_dev, 3 * depth + zs, 2 * depth + zs)
+        to_sib(condition, k.me, zs)
+
+    def along(condition, zs, up, down):
+        if up:
+            send(both(condition, k.has_up), k.me, zs, 0, rows, k.up_dev, zs, zs)
+        if down:
+            send(both(condition, k.has_down), k.me, zs, 0, rows, k.down_dev, depth + zs, zs)
+
+    def take(condition, yx, zs, lo, n, r):
+        when(condition, lambda: k.arrive(block(yx, zs, lo, n), rs.at[r]))
+
+    def own():
+        along(None, k.z, True, True)
+        outward(None, k.z)
+        yield
+
+    def z_steps():
+        for d in range(1, depth):
+            for condition, zs, below in near(k, d):
+                take(condition, k.me, zs, 0, rows, zs)
+                along(condition, zs, below, not below)
+                outward(condition, zs)
+            yield
+
+    def x_steps():
+        for d in range(depth):
+            for condition, zs, _ in near(k, d):
+                take(condition, k.xs, zs, 0, rows, depth + zs)
+                send(condition, k.xs, zs, 0, half, k.y_dev, 5 * depth + zs, 4 * depth + zs)
+                to_sib(condition, k.xs, zs)
+            yield
+
+    def y_steps():
+        for d in range(depth):
+            for condition, zs, _ in near(k, d):
+                take(condition, k.ys, zs, 0, rows, 2 * depth + zs)
+                send(condition, k.ys, zs, half, rows - half, k.x_dev, 4 * depth + zs, 3 * depth + zs)
+                to_sib(condition, k.ys, zs)
+            yield
+
+    def d_steps():
+        for d in range(depth):
+            for condition, zs, _ in near(k, d):
+                take(condition, k.ds, zs, 0, half, 4 * depth + zs)
+                take(condition, k.ds, zs, half, rows - half, 3 * depth + zs)
+                to_sib(condition, k.ds, zs)
+            yield
+
+    def sib_steps():
+        for yx in range(4):
+            for zs in range(depth):
+                k.arrive(buf.at[sib_index(yx, zs), pl.ds(low, rows)], rs.at[5 * depth + yx * depth + zs])
+        yield
+
+    steps = {"0": own(), "z": z_steps(), "x": x_steps(), "y": y_steps(), "d": d_steps(), "s": sib_steps()}
+    return {name + key: step for key, step in steps.items()}
+
+
+def gather_z_last(k, name, buf, index, low, rows, half, ss, rs):
+    depth = k.depth
+    yx_of = (k.me, k.xs, k.ys, k.ds)
+
+    def block(yx, zs, lo=0, n=rows):
+        return buf.at[index(yx, zs), pl.ds(low + lo, n)]
+
+    def send(condition, yx, zs, lo, n, device, s, r):
+        ref = lambda: block(yx, zs, lo, n)
+        k.start(condition, ref, ref, lambda: ss.at[s], lambda: rs.at[r], device, name)
+
+    def along(condition, which, zs, up, down):
+        yx = yx_of[which]
+        place = which * depth + zs
+        if up:
+            send(both(condition, k.has_up), yx, zs, 0, rows, k.up_dev, 4 + place, 4 + place)
+        if down:
+            send(both(condition, k.has_down), yx, zs, 0, rows, k.down_dev, 4 + 4 * depth + place, 4 + place)
+
+    def own():
+        send(None, k.me, k.z, 0, rows, k.x_dev, 0, 0)
+        send(None, k.me, k.z, 0, rows, k.y_dev, 1, 1)
+        along(None, 0, k.z, True, True)
+        yield
+
+    def x_step():
+        k.arrive(block(k.xs, k.z), rs.at[0])
+        send(None, k.xs, k.z, 0, half, k.y_dev, 2, 2)
+        along(None, 1, k.z, True, True)
+        yield
+
+    def y_step():
+        k.arrive(block(k.ys, k.z), rs.at[1])
+        send(None, k.ys, k.z, half, rows - half, k.x_dev, 3, 3)
+        along(None, 2, k.z, True, True)
+        yield
+
+    def d_step():
+        k.arrive(block(k.ds, k.z, 0, half), rs.at[2])
+        k.arrive(block(k.ds, k.z, half, rows - half), rs.at[3])
+        along(None, 3, k.z, True, True)
+        yield
+
+    def z_steps(which):
+        for d in range(1, depth):
+            for condition, zs, below in near(k, d):
+                when(condition, lambda zs=zs: k.arrive(block(yx_of[which], zs), rs.at[4 + which * depth + zs]))
+                along(condition, which, zs, below, not below)
+            yield
+
+    steps = {"0": own(), "x": x_step(), "y": y_step(), "d": d_step()}
+    for which in range(4):
+        steps[str(4 + which)] = z_steps(which)
+    return {name + key: step for key, step in steps.items()}
+
+
+def add_into(ref, *others):
+    total = ref[...].astype(f32)
+    for other in others:
+        total = total + other[...].astype(f32)
+    ref[...] = total.astype(ref.dtype)
+
+
+def scatter_order(depth):
+    return ([0, depth - 1] + list(range(1, depth - 1)))[:depth]
+
+
+def along_z(k, zd, wave, block, from_up, from_down, rs_up, rs_down, send):
+    top, low = k.depth - 1 - wave, wave
+
+    def take(slot, semaphore):
+        k.arrive(slot, semaphore)
+        add_into(block, slot)
+
+    if zd < top:
+        if wave:
+            pl.when(k.z == top)(lambda: take(from_up, rs_up))
+        send(k.z == top, False)
+    if zd > low:
+        if wave:
+            pl.when(k.z == low)(lambda: take(from_down, rs_down))
+        send(k.z == low, True)
+
+
+def scatter_z_last(k, name, buf, index, low, rows, half, slots, ss, rs, finish):
+    depth = k.depth
+    from_x_diag, from_y_diag, from_x, from_y, from_up, from_down = slots
+    order = scatter_order(depth)
+    rest = rows - half
+
+    def block(yx, zd, lo=0, n=rows):
+        return buf.at[index(yx, zd), pl.ds(low + lo, n)]
+
+    def send(condition, source, target, device, s, r):
+        k.start(condition, source, target, lambda: ss.at[s], lambda: rs.at[r], device)
+
+    def pure_x():
+        for zd in order:
+            send(None, lambda zd=zd: block(k.xs, zd, half, rest), lambda zd=zd: from_x.at[zd, pl.ds(half, rest)], k.x_dev, 2 * depth + zd, 2 * depth + zd)
+        yield
+
+    def pure_y():
+        for zd in order:
+            send(None, lambda zd=zd: block(k.ys, zd, 0, half), lambda zd=zd: from_y.at[zd, pl.ds(0, half)], k.y_dev, 3 * depth + zd, 3 * depth + zd)
+        yield
+
+    def diagonal():
+        for zd in order:
+            send(None, lambda zd=zd: block(k.ds, zd, 0, half), lambda zd=zd: from_y_diag.at[zd], k.y_dev, zd, zd)
+            send(None, lambda zd=zd: block(k.ds, zd, half, rest), lambda zd=zd: from_x_diag.at[zd], k.x_dev, depth + zd, depth + zd)
+        yield
+
+    def y_added():
+        for zd in order:
+            k.arrive(from_y_diag.at[zd], rs.at[zd])
+            add_into(block(k.xs, zd, 0, half), from_y_diag.at[zd])
+            send(None, lambda zd=zd: block(k.xs, zd, 0, half), lambda zd=zd: from_x.at[zd, pl.ds(0, half)], k.x_dev, 4 * depth + zd, 4 * depth + zd)
+            yield
+
+    def x_added():
+        for zd in order:
+            k.arrive(from_x_diag.at[zd], rs.at[depth + zd])
+            add_into(block(k.ys, zd, half, rest), from_x_diag.at[zd])
+            send(None, lambda zd=zd: block(k.ys, zd, half, rest), lambda zd=zd: from_y.at[zd, pl.ds(half, rest)], k.y_dev, 5 * depth + zd, 5 * depth + zd)
+            yield
+
+    def wave(zd, number):
+        def send_z(condition, up):
+            place = (7 if up else 6) * depth + zd
+            slot = from_down if up else from_up
+            send(condition, lambda: block(k.me, zd), lambda: slot.at[zd], k.up_dev if up else k.down_dev, place, place)
+
+        along_z(
+            k, zd, number, block(k.me, zd), from_up.at[zd], from_down.at[zd],
+            rs.at[6 * depth + zd], rs.at[7 * depth + zd], send_z,
+        )
+
+    def collect():
+        for zd in order:
+            k.arrive(from_x.at[zd, pl.ds(half, rest)], rs.at[2 * depth + zd])
+            k.arrive(from_y.at[zd, pl.ds(0, half)], rs.at[3 * depth + zd])
+            k.arrive(from_x.at[zd, pl.ds(0, half)], rs.at[4 * depth + zd])
+            k.arrive(from_y.at[zd, pl.ds(half, rest)], rs.at[5 * depth + zd])
+            add_into(block(k.me, zd), from_x.at[zd], from_y.at[zd])
+            wave(zd, 0)
+            yield
+
+    def waves(number):
+        for zd in order:
+            if zd < depth - 1 - number or zd > number:
+                wave(zd, number)
+                yield
+
+    def end():
+        finish(block(k.me, k.z), False)
+
+        def last_up():
+            k.arrive(from_up.at[k.z], rs.at[6 * depth + k.z])
+            finish(from_up.at[k.z], True)
+
+        def last_down():
+            k.arrive(from_down.at[k.z], rs.at[7 * depth + k.z])
+            finish(from_down.at[k.z], True)
+
+        pl.when(k.has_up)(last_up)
+        pl.when(k.has_down)(last_down)
+        yield
+
+    steps = {"X": pure_x(), "Y": pure_y(), "D": diagonal(), "a": y_added(), "b": x_added(), "c": collect(), "e": end()}
+    steps |= {"v": waves(1), "w": waves(2)}
+    return {name + key: step for key, step in steps.items()}
+
+
+def scatter_z_first(k, name, buf, index, low, rows, half, slots, ss, rs, finish):
+    depth = k.depth
+    from_x_diag, from_y_diag, from_x, from_y, from_up, from_down = slots
+    yx_of = (k.me, k.xs, k.ys, k.ds)
+    rest = rows - half
+    base = 8 * depth
+
+    def block(yx, zd, lo=0, n=rows):
+        return buf.at[index(yx, zd), pl.ds(low + lo, n)]
+
+    def send(condition, source, target, device, s, r):
+        k.start(condition, source, target, lambda: ss.at[s], lambda: rs.at[r], device)
+
+    def waves(which):
+        yx = yx_of[which]
+        for number in range(depth - 1):
+            for zd in scatter_order(depth):
+                place = which * depth + zd
+
+                def send_z(condition, up, zd=zd, place=place):
+                    slot, number = (from_down, 4 * depth + place) if up else (from_up, place)
+                    send(condition, lambda: block(yx, zd), lambda: slot.at[place], k.up_dev if up else k.down_dev, number, number)
+
+                along_z(
+                    k, zd, number, block(yx, zd), from_up.at[place], from_down.at[place],
+                    rs.at[place], rs.at[4 * depth + place], send_z,
+                )
+            yield
+
+    def own(which):
+        yx = yx_of[which]
+        place = which * depth + k.z
+
+        def take(slot, semaphore):
+            k.arrive(slot, semaphore)
+            add_into(block(yx, k.z), slot)
+
+        pl.when(k.has_up)(lambda: take(from_up.at[place], rs.at[place]))
+        pl.when(k.has_down)(lambda: take(from_down.at[place], rs.at[4 * depth + place]))
+
+    def own_me():
+        own(0)
+        yield
+
+    def own_x():
+        own(1)
+        send(None, lambda: block(k.xs, k.z, half, rest), lambda: from_x.at[0, pl.ds(half, rest)], k.x_dev, base + 2, base + 2)
+        yield
+
+    def own_y():
+        own(2)
+        send(None, lambda: block(k.ys, k.z, 0, half), lambda: from_y.at[0, pl.ds(0, half)], k.y_dev, base + 3, base + 3)
+        yield
+
+    def own_d():
+        own(3)
+        send(None, lambda: block(k.ds, k.z, 0, half), lambda: from_y_diag.at[0], k.y_dev, base, base)
+        send(None, lambda: block(k.ds, k.z, half, rest), lambda: from_x_diag.at[0], k.x_dev, base + 1, base + 1)
+        yield
+
+    def y_added():
+        k.arrive(from_y_diag.at[0], rs.at[base])
+        add_into(block(k.xs, k.z, 0, half), from_y_diag.at[0])
+        send(None, lambda: block(k.xs, k.z, 0, half), lambda: from_x.at[0, pl.ds(0, half)], k.x_dev, base + 4, base + 4)
+        yield
+
+    def x_added():
+        k.arrive(from_x_diag.at[0], rs.at[base + 1])
+        add_into(block(k.ys, k.z, half, rest), from_x_diag.at[0])
+        send(None, lambda: block(k.ys, k.z, half, rest), lambda: from_y.at[0, pl.ds(half, rest)], k.y_dev, base + 5, base + 5)
+        yield
+
+    def end():
+        finish(block(k.me, k.z), False)
+        k.arrive(from_x.at[0, pl.ds(half, rest)], rs.at[base + 2])
+        k.arrive(from_x.at[0, pl.ds(0, half)], rs.at[base + 4])
+        finish(from_x.at[0], True)
+        k.arrive(from_y.at[0, pl.ds(0, half)], rs.at[base + 3])
+        k.arrive(from_y.at[0, pl.ds(half, rest)], rs.at[base + 5])
+        finish(from_y.at[0], True)
+        yield
+
+    steps = {"O": own_me(), "X": own_x(), "Y": own_y(), "D": own_d(), "a": y_added(), "b": x_added(), "e": end()}
+    steps |= {str(which): waves(which) for which in range(4)}
+    return {name + key: step for key, step in steps.items()}
+
+
+SEQ, WIDTH, UNITS = 256, 768, 96
+HEADS = WIDTH // HEAD_SIZE
+
+
+def row_loop(total, step, body):
+    def once(i, carry):
+        body(pl.multiple_of(i * step, step), step)
+        return carry
+
+    lax.fori_loop(0, total // step, once, 0)
+
+
+def lane_shift(values, offset, left):
+    extent = values.shape[1]
+    lane = lax.broadcasted_iota(jnp.int32, values.shape, 1)
+    if left:
+        return jnp.where(lane < extent - offset, pltpu.roll(values, extent - offset, 1), 0.0)
+    return jnp.where(lane >= offset, pltpu.roll(values, offset, 1), 0.0)
+
+
+def three_heads(first, body):
+    for h in range(first, first + 3):
+        body(h)
+
+
+def head_rows(h):
+    return pl.ds(pl.multiple_of(h * HEAD_SIZE, HEAD_SIZE), HEAD_SIZE)
+
+
+def scratch_of(depth):
+    devices, blocks = 8 * depth, 4 * depth
+    table = {
+        "qk": ((devices, UNITS, WIDTH), bf16),
+        "ff": ((blocks, 2 * UNITS, WIDTH), bf16),
+        "sm": ((devices, 16, 128), f32),
+        "gff": ((blocks, 2 * UNITS, WIDTH), bf16),
+        "gs": ((devices, 16, 128), f32),
+        "sr": ((blocks, UNITS, WIDTH), bf16),
+        "srs": ((blocks, 16, 128), f32),
+        "wq": ((WIDTH, WIDTH), bf16),
+        "wk": ((WIDTH, WIDTH), bf16),
+        "wv": ((WIDTH, WIDTH), bf16),
+        "wo": ((WIDTH, WIDTH), bf16),
+        "s1": ((SEQ, WIDTH), f32),
+        "i1": ((SEQ, 128), f32),
+        "nm": ((SEQ, WIDTH), bf16),
+        "hid": ((SEQ, WIDTH), f32),
+        "s2": ((SEQ, WIDTH), f32),
+        "i2": ((SEQ, 128), f32),
+        "n2": ((2 * SEQ, WIDTH), bf16),
+        "ct": ((2 * SEQ, WIDTH), bf16),
+        "outp": ((2 * SEQ, WIDTH), f32),
+        "dn2": ((2 * SEQ, WIDTH), f32),
+        "outr": ((SEQ, WIDTH), f32),
+        "dn2r": ((SEQ, WIDTH), f32),
+        "act": ((2 * SEQ, UNITS * depth), bf16),
+        "dp": ((2 * SEQ, UNITS * depth), bf16),
+        "da": ((SEQ, WIDTH), bf16),
+        "dn": ((SEQ, WIDTH), f32),
+        "nmt": ((WIDTH, SEQ), bf16),
+        "qt": ((WIDTH, SEQ), bf16),
+        "kt": ((WIDTH, SEQ), bf16),
+        "vt": ((WIDTH, SEQ), bf16),
+        "krt": ((WIDTH, SEQ), f32),
+        "mt": ((WIDTH, SEQ), bf16),
+        "dmt": ((WIDTH, SEQ), bf16),
+        "dqt": ((WIDTH, SEQ), bf16),
+        "dkt": ((WIDTH, SEQ), bf16),
+        "dvt": ((WIDTH, SEQ), bf16),
+        "kft": ((WIDTH, SEQ), bf16),
+        "vft": ((WIDTH, SEQ), bf16),
+        "ex": ((WIDTH, SEQ), f32),
+        "tt": ((HEADS, SEQ, SEQ), f32),
+        "vec": ((16, WIDTH), f32),
+        "vecc": ((WIDTH, 128), f32),
+        "colsum": ((WIDTH, 128), f32),
+        "gvec": ((16, WIDTH), f32),
+        "bias": ((4, 8, UNITS * depth), f32),
+        "gbias": ((blocks, 8, 128), f32),
+    }
+    for name, rows, half, lanes, kind in (
+        ("q", UNITS, UNITS // 2, WIDTH, bf16),
+        ("b", 128, 64, WIDTH, bf16),
+        ("t", 16, 8, 128, f32),
+    ):
+        table["r" + name + "dx"] = ((depth, rows - half, lanes), kind)
+        table["r" + name + "dy"] = ((depth, half, lanes), kind)
+        for place in ("x", "y", "u", "d"):
+            table["r" + name + place] = ((depth, rows, lanes), kind)
+    table["rcdx"] = table["rcdy"] = ((1, 32, WIDTH), bf16)
+    table["rcx"] = table["rcy"] = ((1, 64, WIDTH), bf16)
+    table["rcu"] = table["rcd"] = ((blocks, 64, WIDTH), bf16)
+    table["out"] = table["dinp"] = ((SEQ, WIDTH), bf16)
+    for name in ("gwq", "gwk", "gwv", "gwo"):
+        table[name] = ((24, WIDTH), f32)
+    table["gfc1"] = table["gfc2"] = ((UNITS, WIDTH), f32)
+    table["gsmall"] = ((16, 128), f32)
+    table["store"] = len(RESULTS)
+    for name, count in (
+        ("gq", 10 * depth), ("gb", 10 * depth), ("gt", 10 * depth), ("gc", 4 + 8 * depth),
+        ("sq", 8 * depth), ("sb", 8 * depth), ("st", 8 * depth), ("sc", 8 * depth + 6), ("e", 12),
+    ):
+        table[name + "_s"] = table[name + "_r"] = count
+    return table
+
+
+PLAN = (
+    "own_blocks", "barrier", "S0", "M0", "L0", "own_cotangent", "norm1", "Sz", "Mz", "Sx", "Sy", "Mx", "My",
+    "Lx", "Ly", "Sz", "Mz", "Sx", "Sy", "Mx", "My", "F0", "Ld", "Sz", "Mz", "Sx", "Sy", "Mx", "My", "Fz",
+    "Sx", "Sy", "Mx", "My", "Sd", "Sd", "Sd", "Sd", "Ss", "vectors", "mixer_kernels", "gain1", "Md", "Md",
+    "Md", "Md", "Fz", "L4", "L5", "Ms", "Fx", "Fy", "Fz", "L6", "L7", "unpack", "project", "Fx", "Fy",
+    "mix0", "L4", "L5", "mix1", "L6", "L7", "Fx", "Fy", "mix2", "L4", "mix3", "hidden", "Fx", "Fy", "norm2",
+    "L5", "L6", "L7", "sibling_rows", "feed0", "feed_grads0", "l0", "feed1", "feed_grads1", "fX", "l1", "l0",
+    "feed2", "feed_grads2", "fY", "l2", "l1", "l0", "Fd", "Fd", "Fd", "Fd", "feed3", "feed_swap",
+    "feed_grads3", "fD", "l3", "l2", "l1", "back2", "grad_mixed", "back4", "fa", "fb", "l2", "l3", "back5",
+    "fa", "fb", "l3", "back6", "fa", "fb", "lX", "lY", "lO", "back7", "fa", "fb", "lD", "sent", "pack",
+    "grad_normed", "fc", "fc", "la", "lb", "back1", "fc", "fc", "core_sums", "mD", "mX", "mY", "fv", "fv",
+    "fv", "fv", "flip", "kernel0", "kernel1", "fw", "fw", "kernel2", "ma", "mb", "kernel3", "vector_tiles",
+    "finish_out", "small_sums", "sD", "sX", "sY", "ma", "mb", "ma", "mb", "ma", "mb", "sa", "sb", "sa", "sb",
+    "sa", "sb", "sa", "sb", "fe", "le", "mc", "sc", "mc", "sc", "mc", "sc", "mc", "sc", "mv", "sv", "mv",
+    "sv", "mv", "sv", "mv", "sv", "mw", "sw", "mw", "sw", "me", "se", "store",
+)
+INPUTS = ("tok", "length", "cot", "iq", "ik", "iv", "io", "ifc1", "ifc2", "ibias", "ivec")
+RESULTS = ("out", "dinp", "gwq", "gwk", "gwv", "gwo", "gfc1", "gfc2", "gsmall")
+OUTPUTS = tuple("to_" + name for name in RESULTS)
+
+
+def layer_kernel(depth, *refs):
+    names = INPUTS + OUTPUTS + tuple(scratch_of(depth))
+    m = SimpleNamespace(**dict(zip(names, refs, strict=True)))
+    k = Links(depth)
+    core = k.core
+
+    def in_all(yx, zs):
+        return (yx * 2 + core) * depth + zs
+
+    def in_all_sib(yx, zs):
+        return (yx * 2 + (1 - core)) * depth + zs
+
+    def in_core(yx, zs):
+        return yx * depth + zs
+
+    def chip_rows(start, step):
+        return pl.ds(pl.multiple_of(core * SEQ + start, step), step)
+
+    def stored(name):
+        place = RESULTS.index(name)
+        return pltpu.make_async_copy(getattr(m, name), getattr(m, "to_" + name), m.store.at[place])
+
+    core_rows = pl.ds(pl.multiple_of(core * SEQ, SEQ), SEQ)
+    sib_rows = pl.ds(pl.multiple_of((1 - core) * SEQ, SEQ), SEQ)
+
+    def swap(place, source, target):
+        k.start(None, lambda: source, lambda: target, lambda: m.e_s.at[place], lambda: m.e_r.at[place], k.sib_dev)
+
+    day = lax.broadcasted_iota(jnp.int32, (1, SEQ), 1).astype(f32)
+    s_at = lax.broadcasted_iota(jnp.int32, (SEQ, SEQ), 0)
+    t_at = lax.broadcasted_iota(jnp.int32, (SEQ, SEQ), 1)
+    valid = (lax.broadcasted_iota(jnp.int32, (1, SEQ), 1) < m.length[0]).astype(f32)
+
+    def own_blocks():
+        here = in_all(k.me, k.z)
+        for place, (first, second) in enumerate(((m.iq, m.ik), (m.iv, m.io))):
+            pair = jnp.concatenate([first[...].astype(f32), second[...].astype(f32)], axis=0)
+            m.qk[here, 48 * place : 48 * place + 48] = pair.astype(bf16)
+        m.sm[here] = jnp.zeros((16, 128), f32)
+        m.sm[here, 0:15, 0:24] = m.ivec[...].astype(f32)
+        m.sm[here, 15:16, 0:UNITS] = m.ibias[...].astype(f32)
+        m.ff[in_core(k.me, k.z), 0:UNITS] = m.ifc1[...]
+        m.ff[in_core(k.me, k.z), UNITS : 2 * UNITS] = m.ifc2[...]
+
+    def own_cotangent():
+        m.ct[core_rows] = m.cot[...]
+        swap(0, m.ct.at[core_rows], m.ct.at[core_rows])
+
+    def norm1():
+        def rows_of(start, step):
+            rows = pl.ds(start, step)
+            tokens = m.tok[rows].astype(f32)
+            centred = tokens - jnp.mean(tokens, axis=1, keepdims=True)
+            inverse = lax.rsqrt(jnp.mean(centred * centred, axis=1, keepdims=True) + EPSILON)
+            m.s1[rows] = centred * inverse
+            m.i1[rows] = jnp.broadcast_to(inverse, (step, 128))
+
+        row_loop(SEQ, 32, rows_of)
+
+    def vectors():
+        total = jnp.zeros((16, WIDTH), f32)
+        for wide in range(8):
+            part = jnp.zeros((16, 128), f32)
+            for zs in range(depth):
+                tile = m.sm[wide * depth + zs]
+                part = part + (pltpu.roll(tile, 24 * zs, 1) if zs else tile)
+            padded = jnp.concatenate([part, jnp.zeros((16, WIDTH - 128), f32)], axis=1)
+            total = total + (pltpu.roll(padded, 96 * wide, 1) if wide else padded)
+        m.vec[...] = total
+        m.vecc[...] = jnp.transpose(jnp.concatenate([total, jnp.zeros((112, WIDTH), f32)], axis=0))
+        for yx in range(4):
+            line = jnp.zeros((16, UNITS * depth), f32)
+            for zs in range(depth):
+                tile = jnp.concatenate([m.sm[in_all(yx, zs)], jnp.zeros((16, UNITS * depth - 128), f32)], axis=1)
+                line = line + (pltpu.roll(tile, UNITS * zs, 1) if zs else tile)
+            m.bias[yx] = line[8:16]
+
+    def head_kernel(h, carry):
+        rows = head_rows(h)
+        decays = jnp.exp(-m.vecc[rows, 10:11] * day)
+        m.ex[rows] = decays
+        line = jnp.sum(m.vecc[rows, 9:10] * decays, axis=0, keepdims=True) * (1.0 / STATE)
+        matrix = pltpu.roll(jnp.broadcast_to(line, (SEQ, SEQ)), 0, 1, stride=1, stride_axis=0)
+        m.tt[h] = jnp.where(t_at >= s_at, matrix, 0.0)
+        return carry
+
+    def mixer_kernels():
+        lax.fori_loop(0, HEADS, head_kernel, 0)
+
+    def gain1():
+        def rows_of(start, step):
+            rows = pl.ds(start, step)
+            m.nm[rows] = (m.s1[rows] * m.vec[0:1] + m.vec[1:2]).astype(bf16)
+
+        row_loop(SEQ, 32, rows_of)
+        m.nmt[...] = jnp.transpose(m.nm[...])
+
+    def unpack_rows(w, carry):
+        rows = pl.ds(pl.multiple_of(w * 96, 96), 96)
+        for place, (first, second) in enumerate(((m.wq, m.wk), (m.wv, m.wo))):
+            pair = m.qk[pl.ds(w * depth, depth), 48 * place : 48 * place + 48, :].astype(f32)
+            first[rows] = pair[:, :24].reshape(96, WIDTH).astype(bf16)
+            second[rows] = pair[:, 24:].reshape(96, WIDTH).astype(bf16)
+        return carry
+
+    def unpack():
+        lax.fori_loop(0, 8, unpack_rows, 0)
+
+    def project():
+        m.qt[...] = jnp.transpose(dg(m.nm[...], m.wq[...], 1, 0) + m.vec[2:3]).astype(bf16)
+        m.krt[...] = jnp.transpose(dg(m.nm[...], m.wk[...], 1, 0) + m.vec[3:4])
+        m.vt[...] = (jnp.transpose(dg(m.nm[...], m.wv[...], 1, 0) + m.vec[4:5]) * valid).astype(bf16)
+
+    def mix_head(h):
+        rows = head_rows(h)
+        raw = m.krt[rows]
+        summed = raw * m.vecc[rows, 5:6]
+        for j in range(1, 4):
+            summed = summed + lane_shift(raw, j, False) * m.vecc[rows, 5 + j : 6 + j]
+        keys = (summed * valid).astype(bf16)
+        m.kt[rows] = keys
+        scores = dg(keys, m.qt[rows], 0, 0) * (1.0 / HEAD_SIZE)
+        weights = (scores * m.tt[h]).astype(bf16)
+        m.mt[rows] = (dg(m.vt[rows], weights, 1, 0) * valid).astype(bf16)
+
+    def hidden():
+        m.hid[...] = dg(m.mt[...], m.wo[...], 0, 0)
+
+    def norm2():
+        def rows_of(start, step):
+            rows = pl.ds(start, step)
+            hidden = m.tok[rows].astype(f32) + m.hid[rows] + m.vec[11:12]
+            m.hid[rows] = hidden
+            centred = hidden - jnp.mean(hidden, axis=1, keepdims=True)
+            inverse = lax.rsqrt(jnp.mean(centred * centred, axis=1, keepdims=True) + EPSILON)
+            scaled = centred * inverse
+            m.s2[rows] = scaled
+            m.i2[rows] = jnp.broadcast_to(inverse, (step, 128))
+            m.n2[chip_rows(start, step)] = (scaled * m.vec[12:13] + m.vec[13:14]).astype(bf16)
+
+        row_loop(SEQ, 32, rows_of)
+        swap(1, m.n2.at[core_rows], m.n2.at[core_rows])
+
+    def sibling_rows():
+        k.arrive(m.ct.at[sib_rows], m.e_r.at[0])
+        k.arrive(m.n2.at[sib_rows], m.e_r.at[1])
+
+    def finish_feed(ref, more):
+        value = ref[...].astype(f32)
+        for target, low, high in ((m.gfc1, 0, UNITS), (m.gfc2.at[0:32], UNITS, 128)):
+            target[...] = target[...] + value[low:high] if more else value[low:high]
+
+    def finish_last(ref, more):
+        value = ref[...].astype(f32)
+        m.gfc2[32:96] = m.gfc2[32:96] + value if more else value
+
+    def finish_mats(ref, more):
+        value = ref[...].astype(f32)
+        for place, target in enumerate((m.gwq, m.gwk, m.gwv, m.gwo)):
+            part = value[24 * place : 24 * place + 24]
+            target[...] = target[...] + part if more else part
+
+    def finish_small(ref, more):
+        m.gsmall[...] = m.gsmall[...] + ref[...] if more else ref[...]
+
+    steps = {}
+    steps |= gather_z_first(k, "S", m.sm, in_all, 0, 16, 8, m.gt_s, m.gt_r, in_all_sib)
+    steps |= gather_z_first(k, "M", m.qk, in_all, 0, UNITS, UNITS // 2, m.gq_s, m.gq_r, in_all_sib)
+    steps |= gather_z_first(k, "F", m.ff, in_core, 0, 128, 64, m.gb_s, m.gb_r)
+    steps |= gather_z_last(k, "L", m.ff, in_core, 128, 64, 32, m.gc_s, m.gc_r)
+    slots = (m.rbdx, m.rbdy, m.rbx, m.rby, m.rbu, m.rbd)
+    steps |= scatter_z_last(k, "f", m.gff, in_core, 0, 128, 64, slots, m.sb_s, m.sb_r, finish_feed)
+    slots = (m.rcdx, m.rcdy, m.rcx, m.rcy, m.rcu, m.rcd)
+    steps |= scatter_z_first(k, "l", m.gff, in_core, 128, 64, 32, slots, m.sc_s, m.sc_r, finish_last)
+    slots = (m.rqdx, m.rqdy, m.rqx, m.rqy, m.rqu, m.rqd)
+    steps |= scatter_z_last(k, "m", m.qk, in_all, 0, UNITS, UNITS // 2, slots, m.sq_s, m.sq_r, finish_mats)
+    slots = (m.rtdx, m.rtdy, m.rtx, m.rty, m.rtu, m.rtd)
+    steps |= scatter_z_last(k, "s", m.gs, in_all, 0, 16, 8, slots, m.st_s, m.st_r, finish_small)
+
+    root = math.sqrt(2.0 / math.pi)
+    chunk = UNITS * depth
+    yx_of = (k.me, k.xs, k.ys, k.ds)
+
+    def feed(which):
+        yx = yx_of[which]
+        blocks = pl.ds(yx * depth, depth)
+        fc1 = m.ff[blocks, 0:UNITS, :].reshape(chunk, WIDTH)
+        fc2 = m.ff[blocks, UNITS : 2 * UNITS, :].reshape(chunk, WIDTH)
+        for r in range(2):
+            rows = pl.ds(r * SEQ, SEQ)
+            pre = dg(m.n2[rows], fc1, 1, 1) + m.bias[yx, 7:8]
+            square = pre * pre
+            tanh = jnp.tanh(root * pre * (1.0 + 0.044715 * square))
+            half = 0.5 * (1.0 + tanh)
+            slope = half + 0.5 * pre * (1.0 - tanh * tanh) * (root * (1.0 + 3 * 0.044715 * square))
+            activated = (pre * half).astype(bf16)
+            grad_pre = (dg(m.ct[rows], fc2, 1, 1) * slope).astype(bf16)
+            m.act[rows] = activated
+            m.dp[rows] = grad_pre
+            if which == 0:
+                m.outp[rows] = dg(activated, fc2, 1, 0)
+                m.dn2[rows] = dg(grad_pre, fc1, 1, 0)
+            else:
+                m.outp[rows] += dg(activated, fc2, 1, 0)
+                m.dn2[rows] += dg(grad_pre, fc1, 1, 0)
+
+    def feed_swap():
+        swap(2, m.dn2.at[sib_rows], m.dn2r)
+        swap(3, m.outp.at[sib_rows], m.outr)
+
+    def feed_grads(which):
+        yx = yx_of[which]
+        blocks = pl.ds(yx * depth, depth)
+        m.gff[blocks, 0:UNITS] = dg(m.dp[...], m.n2[...], 0, 0).astype(bf16).reshape(depth, UNITS, WIDTH)
+        m.gff[blocks, UNITS : 2 * UNITS] = (
+            dg(m.act[...], m.ct[...], 0, 0).astype(bf16).reshape(depth, UNITS, WIDTH)
+        )
+        sums = jnp.sum(m.dp[...].astype(f32), axis=0, keepdims=True)
+        lane = lax.broadcasted_iota(jnp.int32, (1, 128), 1)
+        for zs in range(depth):
+            line = (pltpu.roll(sums, chunk - UNITS * zs, 1) if zs else sums)[:, :128]
+            m.gbias[yx * depth + zs] = jnp.broadcast_to(jnp.where(lane < UNITS, line, 0.0), (8, 128))
+
+    def back2():
+        m.gvec[...] = jnp.zeros((16, WIDTH), f32)
+        k.arrive(m.dn2r, m.e_r.at[2])
+
+        def rows_of(start, step):
+            rows = pl.ds(start, step)
+            grad_normed = m.dn2[chip_rows(start, step)] + m.dn2r[rows]
+            scaled = m.s2[rows]
+            grad_in = grad_normed * m.vec[12:13]
+            first = jnp.mean(grad_in, axis=1, keepdims=True)
+            second = jnp.mean(grad_in * scaled, axis=1, keepdims=True)
+            top = m.cot[rows].astype(f32)
+            grad_hidden = top + m.i2[rows, 0:1] * (grad_in - first - scaled * second)
+            m.s2[rows] = grad_hidden
+            rounded = grad_hidden.astype(bf16)
+            m.da[rows] = rounded
+            m.gvec[11:12] += jnp.sum(rounded.astype(f32), axis=0, keepdims=True)
+            m.gvec[12:13] += jnp.sum(grad_normed * scaled, axis=0, keepdims=True)
+            m.gvec[13:14] += jnp.sum(grad_normed, axis=0, keepdims=True)
+            m.gvec[14:15] += jnp.sum(top, axis=0, keepdims=True)
+
+        row_loop(SEQ, 32, rows_of)
+
+    def grad_mixed():
+        m.dmt[...] = (jnp.transpose(dg(m.da[...], m.wo[...], 1, 1)) * valid).astype(bf16)
+
+    def back_head(h):
+        rows = head_rows(h)
+        queries, keys, grad_mixed, kernel = m.qt[rows], m.kt[rows], m.dmt[rows], m.tt[h]
+        scores = dg(keys, queries, 0, 0) * (1.0 / HEAD_SIZE)
+        weights = (scores * kernel).astype(bf16)
+        grad_weights = dg(m.vt[rows], grad_mixed, 0, 0)
+        grad_values = (dg(grad_mixed, weights, 1, 1) * valid).astype(bf16)
+        m.dvt[rows] = grad_values
+        grad_scores = (grad_weights * kernel).astype(bf16)
+        grad_queries = (dg(keys, grad_scores, 1, 0) * (1.0 / HEAD_SIZE)).astype(bf16)
+        m.dqt[rows] = grad_queries
+        grad_keys = dg(queries, grad_scores, 1, 1) * (1.0 / HEAD_SIZE) * valid
+        raw = m.krt[rows]
+        at = lax.broadcasted_iota(jnp.int32, (HEAD_SIZE, 128), 1)
+        grad_raw = grad_keys * m.vecc[rows, 5:6]
+        sums = jnp.where(at == 5, jnp.sum(grad_keys * raw, axis=1, keepdims=True), 0.0)
+        for j in range(1, 4):
+            grad_raw = grad_raw + lane_shift(grad_keys, j, True) * m.vecc[rows, 5 + j : 6 + j]
+            tap = jnp.sum(grad_keys * lane_shift(raw, j, False), axis=1, keepdims=True)
+            sums = jnp.where(at == 5 + j, tap, sums)
+        rounded = grad_raw.astype(bf16)
+        m.dkt[rows] = rounded
+        for place, value in ((2, grad_queries), (3, rounded), (4, grad_values)):
+            sums = jnp.where(at == place, jnp.sum(value.astype(f32), axis=1, keepdims=True), sums)
+        m.colsum[rows] = sums
+
+    def pack_rows(part, carry):
+        rows = pl.ds(pl.multiple_of(part * 384, 384), 384)
+        normed = m.nmt[rows]
+        grads = (
+            dg(normed, m.dqt[...], 1, 1),
+            dg(normed, m.dkt[...], 1, 1),
+            dg(normed, m.dvt[...], 1, 1),
+            dg(m.mt[rows], m.da[...], 1, 0),
+        )
+        for place in range(2):
+            pair = [grad.reshape(4 * depth, 24, WIDTH) for grad in grads[2 * place : 2 * place + 2]]
+            m.qk[pl.ds(part * 4 * depth, 4 * depth), 48 * place : 48 * place + 48, :] = jnp.concatenate(pair, axis=1).astype(bf16)
+        return carry
+
+    def pack():
+        lax.fori_loop(0, 2, pack_rows, 0)
+        for yx in range(4):
+            swap(4 + yx, m.qk.at[pl.ds(in_all_sib(yx, 0), depth)], m.sr.at[pl.ds(yx * depth, depth)])
+
+    def grad_normed():
+        m.dn[...] = jnp.transpose(
+            dg(m.wq[...], m.dqt[...], 1, 0) + dg(m.wk[...], m.dkt[...], 1, 0) + dg(m.wv[...], m.dvt[...], 1, 0)
+        )
+
+    def back1():
+        def rows_of(start, step):
+            rows = pl.ds(start, step)
+            grad_out, scaled = m.dn[rows], m.s1[rows]
+            grad_in = grad_out * m.vec[0:1]
+            first = jnp.mean(grad_in, axis=1, keepdims=True)
+            second = jnp.mean(grad_in * scaled, axis=1, keepdims=True)
+            m.dinp[rows] = (m.s2[rows] + m.i1[rows, 0:1] * (grad_in - first - scaled * second)).astype(bf16)
+            m.gvec[0:1] += jnp.sum(grad_out * scaled, axis=0, keepdims=True)
+            m.gvec[1:2] += jnp.sum(grad_out, axis=0, keepdims=True)
+
+        row_loop(SEQ, 32, rows_of)
+        stored("dinp").start()
+
+    def core_sum(yx):
+        k.arrive(m.sr.at[pl.ds(yx * depth, depth)], m.e_r.at[4 + yx])
+
+        def block_sum(zs, carry):
+            add_into(m.qk.at[in_all(yx, zs)], m.sr.at[yx * depth + zs])
+            return carry
+
+        lax.fori_loop(0, depth, block_sum, 0)
+
+    def core_sums():
+        for yx in range(4):
+            core_sum(yx)
+
+    def flip():
+        turn = (s_at + t_at == SEQ - 1).astype(bf16)
+        m.kft[...] = dg(m.kt[...], turn, 1, 0).astype(bf16)
+        m.vft[...] = dg(m.vt[...], turn, 1, 0).astype(bf16)
+
+    def kernel_head(h):
+        rows = head_rows(h)
+        scores = dg(m.kft[rows], m.qt[rows], 0, 0) * (1.0 / HEAD_SIZE)
+        grad_weights = dg(m.vft[rows], m.dmt[rows], 0, 0)
+        product = jnp.where(s_at + t_at >= SEQ - 1, scores * grad_weights, 0.0)
+        lined = pltpu.roll(product, 1, 1, stride=1, stride_axis=0)
+        grad_kernel = jnp.sum(lined, axis=0, keepdims=True) * (1.0 / STATE)
+        part = m.ex[rows] * grad_kernel
+        at = lax.broadcasted_iota(jnp.int32, (HEAD_SIZE, 128), 1)
+        grad_rate = -m.vecc[rows, 9:10] * jnp.sum(part * day, axis=1, keepdims=True)
+        sums = jnp.where(at == 9, jnp.sum(part, axis=1, keepdims=True), m.colsum[rows])
+        m.colsum[rows] = jnp.where(at == 10, grad_rate, sums)
+
+    def vector_tiles():
+        grads = m.gvec[...] + jnp.transpose(m.colsum[...])[0:16]
+        row_at = lax.broadcasted_iota(jnp.int32, (16, 128), 0)
+        lane_at = lax.broadcasted_iota(jnp.int32, (16, 128), 1)
+        for wide in range(8):
+            turned = (pltpu.roll(grads, WIDTH - 96 * wide, 1) if wide else grads)[:, :128]
+            for zs in range(depth):
+                tile = pltpu.roll(turned, 128 - 24 * zs, 1) if zs else turned
+                tile = jnp.where((lane_at < 24) & (row_at < 15), tile, 0.0)
+                own = jnp.concatenate([jnp.zeros((8, 128), f32), m.gbias[(wide // 2) * depth + zs]], axis=0)
+                mine = (row_at == 15) & (core == wide % 2)
+                m.gs[wide * depth + zs] = jnp.where(mine, own, tile)
+        for yx in range(4):
+            swap(8 + yx, m.gs.at[pl.ds(in_all_sib(yx, 0), depth)], m.srs.at[pl.ds(yx * depth, depth)])
+
+    def small_sums():
+        for yx in range(4):
+            k.arrive(m.srs.at[pl.ds(yx * depth, depth)], m.e_r.at[8 + yx])
+            for zs in range(depth):
+                add_into(m.gs.at[in_all(yx, zs)], m.srs.at[yx * depth + zs])
+
+    def finish_out():
+        def rows_of(start, step):
+            rows = pl.ds(start, step)
+            m.out[rows] = (m.hid[rows] + (m.outp[chip_rows(start, step)] + m.outr[rows]) + m.vec[14:15]).astype(bf16)
+
+        k.arrive(m.outr, m.e_r.at[3])
+        row_loop(SEQ, 32, rows_of)
+        stored("out").start()
+
+    def store():
+        for name in RESULTS[2:]:
+            stored(name).start()
+        k.drain()
+        for name in RESULTS:
+            stored(name).wait()
+
+    compute = {
+        "own_blocks": own_blocks, "barrier": k.barrier, "own_cotangent": own_cotangent, "norm1": norm1,
+        "vectors": vectors, "mixer_kernels": mixer_kernels, "gain1": gain1, "unpack": unpack, "project": project,
+        "hidden": hidden, "norm2": norm2, "sibling_rows": sibling_rows, "feed_swap": feed_swap, "sent": partial(k.drain, "M"), "store": store,
+        "back2": back2, "grad_mixed": grad_mixed, "pack": pack, "grad_normed": grad_normed, "back1": back1,
+        "core_sums": core_sums, "flip": flip, "vector_tiles": vector_tiles, "small_sums": small_sums, "finish_out": finish_out,
+    }
+    for which in range(4):
+        compute["feed%d" % which] = partial(feed, which)
+        compute["feed_grads%d" % which] = partial(feed_grads, which)
+        compute["mix%d" % which] = partial(three_heads, 3 * which, mix_head)
+        compute["back%d" % (4 + which)] = partial(three_heads, 3 * which, back_head)
+        compute["kernel%d" % which] = partial(three_heads, 3 * which, kernel_head)
+    for step in PLAN:
+        if step in compute:
+            compute[step]()
+        else:
+            next(steps[step])
+
+
+def results_kernel(*refs):
+    count = len(RESULTS) - 1
+    sources, tile, targets, bias, vectors = refs[:count], refs[count], refs[9 : 9 + count], refs[17], refs[18]
+    held, came, left = refs[19 : 19 + count], refs[-2], refs[-1]
+    bring = [pltpu.make_async_copy(s, h, came.at[i]) for i, (s, h) in enumerate(zip(sources, held, strict=True))]
+    take = [pltpu.make_async_copy(h, t, left.at[i]) for i, (h, t) in enumerate(zip(held, targets, strict=True))]
+    for copy in bring:
+        copy.start()
+    bias[...] = tile[15:16, :UNITS]
+    vectors[...] = tile[0:15, 0:24]
+    for first, second in zip(bring, take, strict=True):
+        first.wait()
+        second.start()
+    for copy in take:
+        copy.wait()
+
+
+def on_device_fast(
+    tokens, lengths, cotangent, w_query, w_key, w_value, w_out, w_fc1, w_fc2, fc1_bias, vectors
+):
+    depth = lax.axis_size("narrow")
+    scratch = []
+    for entry in scratch_of(depth).values():
+        scratch.append(pltpu.SemaphoreType.DMA((entry,)) if isinstance(entry, int) else pltpu.VMEM(*entry))
+    in_vmem = pl.BlockSpec(memory_space=pltpu.VMEM)
+    anywhere = pl.BlockSpec(memory_space=pl.ANY)
+    in_smem = pl.BlockSpec(memory_space=pltpu.SMEM)
+    shape = jax.ShapeDtypeStruct
+    got = pl.pallas_call(
+        partial(layer_kernel, depth),
+        out_shape=[shape((SEQ, WIDTH), bf16)] * 2
+        + [shape((24, WIDTH), f32)] * 4
+        + [shape((UNITS, WIDTH), f32)] * 2
+        + [shape((16, 128), f32)],
+        in_specs=[in_vmem, in_smem] + [in_vmem] * 9,
+        out_specs=[anywhere] * 9,
+        scratch_shapes=scratch,
+        compiler_params=pltpu.CompilerParams(
+            collective_id=0, has_side_effects=True, vmem_limit_bytes=63 * 2**20
+        ),
+        name="h3_layer",
+    )(
+        tokens, lengths, cotangent, w_query, w_key, w_value, w_out, w_fc1.T, w_fc2, fc1_bias[None], vectors
+    )
+    results = pl.pallas_call(
+        results_kernel,
+        out_shape=[shape(x.shape, x.dtype) for x in got[:8]] + [shape((1, UNITS), f32), shape((15, 24), f32)],
+        in_specs=[anywhere] * 8 + [in_vmem],
+        out_specs=[anywhere] * 8 + [in_vmem] * 2,
+        scratch_shapes=[pltpu.VMEM(x.shape, x.dtype) for x in got[:8]] + [pltpu.SemaphoreType.DMA((8,))] * 2,
+        name="results",
+    )(*got)
+    out, grad_in, g_query, g_key, g_value, g_out, g_fc1, g_fc2, g_bias, g_vectors = results
+    return out, grad_in, g_query, g_key, g_value, g_out, g_fc1.T, g_fc2, g_bias.reshape(-1), g_vectors
+
+
+def fits(mesh):
+    return mesh.shape["wide"] == 8 and mesh.shape["narrow"] == 4
+
+
 def solution(mesh):
     placed = (
         P(("wide", "narrow"), None),
@@ -297,7 +1317,7 @@
         P(None, ("wide", "narrow")),
     )
     return jax.shard_map(
-        on_device,
+        on_device_fast if fits(mesh) else on_device,
         mesh=mesh,
         in_specs=placed,
         out_specs=(

time: 1140 us -> 153 us (0.13); the launches traced: 1130 us -> 153 us
  waiting for transfers between devices: 592 us -> 0 us
  local copies, waits for them, and re-layouts: 192 us -> 0 us
  matrix products: 158 us -> 0 us
  Pallas kernels: 0 us -> 151 us
  blocking collectives: 108 us -> 0 us
  other arithmetic: 58.8 us -> 0 us
  between operations: 15.8 us -> 1.48 us
    unnamed x8 -> x0, waiting for transfers between devices: 428 us -> none
    all_gather x6 -> x0, waiting for transfers between devices: 164 us -> none  [the longest x1 59.5 us: on_device(): lax.all_gather(w_fc1, ('wide', 'narrow'), axis=1, tiled=True)]
    dot_general x90 -> x0, matrix products: 158 us -> none  [the longest x12 20 us: head_backward(): jnp.dot(grad_scores, key_head, preferred_element_type=jnp.float32)]
    pallas_call x0 -> x2, Pallas kernels: none -> 151 us  [the longest x1 148 us: on_device_fast(): pl.pallas_call(partial(layer_kernel, depth), out_shape=[shape((SEQ, WIDTH...]
    reshape x72 -> x0, local copies, waits for them, and re-layouts: 87.9 us -> none  [the longest x2 36.3 us: pack_rows(): return jnp.concatenate([matrix.reshape(shard_count, -1) for matrix in mat...]
    all_gather x1 -> x0, blocking collectives: 71 us -> none  [on_device(): lax.all_gather(vectors, ('wide', 'narrow'), axis=1, tiled=True)]
    slice x52 -> x0, local copies, waits for them, and re-layouts: 52 us -> none  [the longest x24 28.9 us: toeplitz(): kernel_row[:1]]
    unnamed x1 -> x0, blocking collectives: 37.1 us -> none
  transfers between devices with their start and end apart: 7 -> 0, of which waited for: 4 -> 0; matrix products, arithmetic and copies ran while one was open for 8% -> 0% of each run, Pallas kernels for 0% -> 0%
where the time goes in v2:
time: 153 us
  Pallas kernels  151 us (99%)
    pallas_call x1, Pallas kernels, on_device_fast(): pl.pallas_call(partial(layer_kernel, depth), out_shape=[shape((SEQ, WIDTH...  148 us
    pallas_call x1, Pallas kernels, on_device_fast(): pl.pallas_call(results_kernel, out_shape=[shape(x.shape, x.dtype) for x i...  3.61 us

profile of v2, /device:TPU:0, one launch (start us, length us, event | category | flops | bytes accessed | tf_op | source)
XLA Modules:
  0.0 152.8 jit_solution(9776911110669508123)
XLA Ops:
  1.3 147.7 %h3_layer.1 = (bf16[256,768]{1,0:T(8,128)(2,1)}, bf16[256,768]{1,0:T(8,128)(2,1)}, f32[24,768]{1,0:T(8,128)}, f32[24,768]{1,0:T(8,128)}, f32[24,768]{1,0:T(8,128...) custom-call(bf16[256,768]{1,0:T(8,128)(2,1)} %refs_0_.1, ...), custom_call_target="tpu_custom_call" | custom-call | tf_op jit(solution)/shard_map/h3_layer/pallas_call | solution.py:1273
  149.0 3.6 %results.1 = (bf16[256,768]{1,0:T(8,128)(2,1)}, bf16[256,768]{1,0:T(8,128)(2,1)}, f32[24,768]{1,0:T(8,128)}, f32[24,768]{1,0:T(8,128)}, f32[24,768]{1,0:T(8,128)...) custom-call(bf16[256,768]{1,0:T(8,128)(2,1)} %get-tuple-element.29.refs, ...), custom_call_target="tpu_custom_call" | custom-call | tf_op jit(solution)/shard_map/results/pallas_call | solution.py:1289

commit v3 on v2

--- a/solution.py
+++ b/solution.py
@@ -328,7 +328,7 @@
         self.down_dev = (wide, z - 1)
         self.has_up = z < depth - 1
         self.has_down = z > 0
-        self.pending = {}
+        self.at_end = jnp.logical_or(z == 0, z == depth - 1)
 
     def barrier(self):
         semaphore = pltpu.get_barrier_semaphore()
@@ -343,19 +343,18 @@
         peers = 3 + self.has_up.astype(jnp.int32) + self.has_down.astype(jnp.int32)
         pl.semaphore_wait(semaphore, peers)
 
-    def start(self, condition, source, target, send, receive, device, group=""):
-        def build():
-            return pltpu.make_async_remote_copy(
+    def start(self, condition, source, target, send, receive, device):
+        when(
+            condition,
+            lambda: pltpu.make_async_remote_copy(
                 src_ref=source(),
                 dst_ref=target(),
-                send_sem=send(),
-                recv_sem=receive(),
+                send_sem=send,
+                recv_sem=receive,
                 device_id=device,
                 device_id_type=MESH,
-            )
-
-        when(condition, lambda: build().start())
-        self.pending.setdefault(group, []).append((condition, build))
+            ).start(),
+        )
 
     def arrive(self, target, receive):
         pltpu.make_async_remote_copy(
@@ -367,10 +366,19 @@
             device_id_type=MESH,
         ).wait_recv()
 
-    def drain(self, *groups):
-        for group in groups or tuple(self.pending):
-            for condition, build in self.pending.pop(group, ()):
-                when(condition, lambda build=build: build().wait_send())
+    def left(self, extent, semaphore):
+        pltpu.make_async_remote_copy(
+            src_ref=extent,
+            dst_ref=extent,
+            send_sem=semaphore,
+            recv_sem=semaphore,
+            device_id=self.sib_dev,
+            device_id_type=MESH,
+        ).wait_send()
+
+    def left_along(self, extent, semaphore):
+        pl.when(self.at_end)(lambda: self.left(extent(1), semaphore))
+        pl.when(jnp.logical_not(self.at_end))(lambda: self.left(extent(self.depth + 1), semaphore))
 
 
 def near(k, distance):
@@ -385,27 +393,27 @@
     def block(yx, zs, lo=0, n=rows):
         return buf.at[index(yx, zs), pl.ds(low + lo, n)]
 
-    def send(condition, yx, zs, lo, n, device, s, r):
+    def send(condition, yx, zs, lo, n, device, r, way=0):
         ref = lambda: block(yx, zs, lo, n)
-        k.start(condition, ref, ref, lambda: ss.at[s], lambda: rs.at[r], device, name)
+        k.start(condition, ref, ref, ss.at[way], rs.at[r], device)
 
     def to_sib(condition, yx, zs):
         if sib_index is not None:
-            send(condition, yx, zs, 0, rows, k.sib_dev, 6 * depth + yx * depth + zs, 5 * depth + yx * depth + zs)
+            send(condition, yx, zs, 0, rows, k.sib_dev, 4 * depth)
 
     def outward(condition, zs):
-        send(condition, k.me, zs, 0, rows, k.x_dev, 2 * depth + zs, depth + zs)
-        send(condition, k.me, zs, 0, rows, k.y_dev, 3 * depth + zs, 2 * depth + zs)
+        send(condition, k.me, zs, 0, rows, k.x_dev, depth + zs)
+        send(condition, k.me, zs, 0, rows, k.y_dev, 2 * depth + zs)
         to_sib(condition, k.me, zs)
 
     def along(condition, zs, up, down):
         if up:
-            send(both(condition, k.has_up), k.me, zs, 0, rows, k.up_dev, zs, zs)
+            send(both(condition, k.has_up), k.me, zs, 0, rows, k.up_dev, zs, 1)
         if down:
-            send(both(condition, k.has_down), k.me, zs, 0, rows, k.down_dev, depth + zs, zs)
-
-    def take(condition, yx, zs, lo, n, r):
-        when(condition, lambda: k.arrive(block(yx, zs, lo, n), rs.at[r]))
+            send(both(condition, k.has_down), k.me, zs, 0, rows, k.down_dev, zs, 1)
+
+    def take(condition, yx, zs, r):
+        when(condition, lambda: k.arrive(block(yx, zs), rs.at[r]))
 
     def own():
         along(None, k.z, True, True)
@@ -415,7 +423,7 @@
     def z_steps():
         for d in range(1, depth):
             for condition, zs, below in near(k, d):
-                take(condition, k.me, zs, 0, rows, zs)
+                take(condition, k.me, zs, zs)
                 along(condition, zs, below, not below)
                 outward(condition, zs)
             yield
@@ -423,34 +431,39 @@
     def x_steps():
         for d in range(depth):
             for condition, zs, _ in near(k, d):
-                take(condition, k.xs, zs, 0, rows, depth + zs)
-                send(condition, k.xs, zs, 0, half, k.y_dev, 5 * depth + zs, 4 * depth + zs)
+                take(condition, k.xs, zs, depth + zs)
+                send(condition, k.xs, zs, 0, half, k.y_dev, 3 * depth + zs)
                 to_sib(condition, k.xs, zs)
             yield
 
     def y_steps():
         for d in range(depth):
             for condition, zs, _ in near(k, d):
-                take(condition, k.ys, zs, 0, rows, 2 * depth + zs)
-                send(condition, k.ys, zs, half, rows - half, k.x_dev, 4 * depth + zs, 3 * depth + zs)
+                take(condition, k.ys, zs, 2 * depth + zs)
+                send(condition, k.ys, zs, half, rows - half, k.x_dev, 3 * depth + zs)
                 to_sib(condition, k.ys, zs)
             yield
 
     def d_steps():
         for d in range(depth):
             for condition, zs, _ in near(k, d):
-                take(condition, k.ds, zs, 0, half, 4 * depth + zs)
-                take(condition, k.ds, zs, half, rows - half, 3 * depth + zs)
+                take(condition, k.ds, zs, 3 * depth + zs)
                 to_sib(condition, k.ds, zs)
             yield
 
+    def extent(blocks):
+        return buf.at[pl.ds(0, blocks), pl.ds(low, rows)]
+
     def sib_steps():
-        for yx in range(4):
-            for zs in range(depth):
-                k.arrive(buf.at[sib_index(yx, zs), pl.ds(low, rows)], rs.at[5 * depth + yx * depth + zs])
-        yield
-
-    steps = {"0": own(), "z": z_steps(), "x": x_steps(), "y": y_steps(), "d": d_steps(), "s": sib_steps()}
+        k.arrive(extent(4 * depth), rs.at[4 * depth])
+        yield
+
+    def left():
+        k.left(extent((7 if sib_index is not None else 3) * depth), ss.at[0])
+        k.left_along(extent, ss.at[1])
+        yield
+
+    steps = {"0": own(), "z": z_steps(), "x": x_steps(), "y": y_steps(), "d": d_steps(), "s": sib_steps(), ".": left()}
     return {name + key: step for key, step in steps.items()}
 
 
@@ -461,50 +474,57 @@
     def block(yx, zs, lo=0, n=rows):
         return buf.at[index(yx, zs), pl.ds(low + lo, n)]
 
-    def send(condition, yx, zs, lo, n, device, s, r):
+    def send(condition, yx, zs, lo, n, device, r, way=0):
         ref = lambda: block(yx, zs, lo, n)
-        k.start(condition, ref, ref, lambda: ss.at[s], lambda: rs.at[r], device, name)
+        k.start(condition, ref, ref, ss.at[way], rs.at[r], device)
 
     def along(condition, which, zs, up, down):
-        yx = yx_of[which]
-        place = which * depth + zs
+        yx, place = yx_of[which], 3 + which * depth + zs
         if up:
-            send(both(condition, k.has_up), yx, zs, 0, rows, k.up_dev, 4 + place, 4 + place)
+            send(both(condition, k.has_up), yx, zs, 0, rows, k.up_dev, place, 1 + which)
         if down:
-            send(both(condition, k.has_down), yx, zs, 0, rows, k.down_dev, 4 + 4 * depth + place, 4 + place)
+            send(both(condition, k.has_down), yx, zs, 0, rows, k.down_dev, place, 1 + which)
 
     def own():
-        send(None, k.me, k.z, 0, rows, k.x_dev, 0, 0)
-        send(None, k.me, k.z, 0, rows, k.y_dev, 1, 1)
+        send(None, k.me, k.z, 0, rows, k.x_dev, 0)
+        send(None, k.me, k.z, 0, rows, k.y_dev, 1)
         along(None, 0, k.z, True, True)
         yield
 
     def x_step():
         k.arrive(block(k.xs, k.z), rs.at[0])
-        send(None, k.xs, k.z, 0, half, k.y_dev, 2, 2)
+        send(None, k.xs, k.z, 0, half, k.y_dev, 2)
         along(None, 1, k.z, True, True)
         yield
 
     def y_step():
         k.arrive(block(k.ys, k.z), rs.at[1])
-        send(None, k.ys, k.z, half, rows - half, k.x_dev, 3, 3)
+        send(None, k.ys, k.z, half, rows - half, k.x_dev, 2)
         along(None, 2, k.z, True, True)
         yield
 
     def d_step():
-        k.arrive(block(k.ds, k.z, 0, half), rs.at[2])
-        k.arrive(block(k.ds, k.z, half, rows - half), rs.at[3])
+        k.arrive(block(k.ds, k.z), rs.at[2])
         along(None, 3, k.z, True, True)
         yield
 
     def z_steps(which):
         for d in range(1, depth):
             for condition, zs, below in near(k, d):
-                when(condition, lambda zs=zs: k.arrive(block(yx_of[which], zs), rs.at[4 + which * depth + zs]))
+                when(condition, lambda zs=zs: k.arrive(block(yx_of[which], zs), rs.at[3 + which * depth + zs]))
                 along(condition, which, zs, below, not below)
             yield
 
-    steps = {"0": own(), "x": x_step(), "y": y_step(), "d": d_step()}
+    def extent(blocks):
+        return buf.at[pl.ds(0, blocks), pl.ds(low, rows)]
+
+    def left():
+        k.left(extent(3), ss.at[0])
+        for which in range(4):
+            k.left_along(extent, ss.at[1 + which])
+        yield
+
+    steps = {"0": own(), "x": x_step(), "y": y_step(), "d": d_step(), ".": left()}
     for which in range(4):
         steps[str(4 + which)] = z_steps(which)
     return {name + key: step for key, step in steps.items()}
@@ -540,64 +560,67 @@
 
 def scatter_z_last(k, name, buf, index, low, rows, half, slots, ss, rs, finish):
     depth = k.depth
-    from_x_diag, from_y_diag, from_x, from_y, from_up, from_down = slots
+    from_x_diag, from_y_diag, from_xy, from_up, from_down = slots
     order = scatter_order(depth)
     rest = rows - half
 
     def block(yx, zd, lo=0, n=rows):
         return buf.at[index(yx, zd), pl.ds(low + lo, n)]
 
-    def send(condition, source, target, device, s, r):
-        k.start(condition, source, target, lambda: ss.at[s], lambda: rs.at[r], device)
+    def send(condition, source, target, device, r):
+        k.start(condition, source, target, ss.at[0], rs.at[r], device)
+
+    def x_part(zd, lo, n):
+        return from_xy.at[zd, 0, pl.ds(lo, n)]
+
+    def y_part(zd, lo, n):
+        return from_xy.at[zd, 1, pl.ds(lo, n)]
 
     def pure_x():
         for zd in order:
-            send(None, lambda zd=zd: block(k.xs, zd, half, rest), lambda zd=zd: from_x.at[zd, pl.ds(half, rest)], k.x_dev, 2 * depth + zd, 2 * depth + zd)
+            send(None, lambda zd=zd: block(k.xs, zd, half, rest), lambda zd=zd: x_part(zd, half, rest), k.x_dev, 2 * depth + zd)
         yield
 
     def pure_y():
         for zd in order:
-            send(None, lambda zd=zd: block(k.ys, zd, 0, half), lambda zd=zd: from_y.at[zd, pl.ds(0, half)], k.y_dev, 3 * depth + zd, 3 * depth + zd)
+            send(None, lambda zd=zd: block(k.ys, zd, 0, half), lambda zd=zd: y_part(zd, 0, half), k.y_dev, 2 * depth + zd)
         yield
 
     def diagonal():
         for zd in order:
-            send(None, lambda zd=zd: block(k.ds, zd, 0, half), lambda zd=zd: from_y_diag.at[zd], k.y_dev, zd, zd)
-            send(None, lambda zd=zd: block(k.ds, zd, half, rest), lambda zd=zd: from_x_diag.at[zd], k.x_dev, depth + zd, depth + zd)
+            send(None, lambda zd=zd: block(k.ds, zd, 0, half), lambda zd=zd: from_y_diag.at[zd], k.y_dev, zd)
+            send(None, lambda zd=zd: block(k.ds, zd, half, rest), lambda zd=zd: from_x_diag.at[zd], k.x_dev, depth + zd)
         yield
 
     def y_added():
         for zd in order:
             k.arrive(from_y_diag.at[zd], rs.at[zd])
             add_into(block(k.xs, zd, 0, half), from_y_diag.at[zd])
-            send(None, lambda zd=zd: block(k.xs, zd, 0, half), lambda zd=zd: from_x.at[zd, pl.ds(0, half)], k.x_dev, 4 * depth + zd, 4 * depth + zd)
+            send(None, lambda zd=zd: block(k.xs, zd, 0, half), lambda zd=zd: x_part(zd, 0, half), k.x_dev, 2 * depth + zd)
             yield
 
     def x_added():
         for zd in order:
             k.arrive(from_x_diag.at[zd], rs.at[depth + zd])
             add_into(block(k.ys, zd, half, rest), from_x_diag.at[zd])
-            send(None, lambda zd=zd: block(k.ys, zd, half, rest), lambda zd=zd: from_y.at[zd, pl.ds(half, rest)], k.y_dev, 5 * depth + zd, 5 * depth + zd)
+            send(None, lambda zd=zd: block(k.ys, zd, half, rest), lambda zd=zd: y_part(zd, half, rest), k.y_dev, 2 * depth + zd)
             yield
 
     def wave(zd, number):
         def send_z(condition, up):
-            place = (7 if up else 6) * depth + zd
+            place = (4 if up else 3) * depth + zd
             slot = from_down if up else from_up
-            send(condition, lambda: block(k.me, zd), lambda: slot.at[zd], k.up_dev if up else k.down_dev, place, place)
+            send(condition, lambda: block(k.me, zd), lambda: slot.at[zd], k.up_dev if up else k.down_dev, place)
 
         along_z(
             k, zd, number, block(k.me, zd), from_up.at[zd], from_down.at[zd],
-            rs.at[6 * depth + zd], rs.at[7 * depth + zd], send_z,
+            rs.at[3 * depth + zd], rs.at[4 * depth + zd], send_z,
         )
 
     def collect():
         for zd in order:
-            k.arrive(from_x.at[zd, pl.ds(half, rest)], rs.at[2 * depth + zd])
-            k.arrive(from_y.at[zd, pl.ds(0, half)], rs.at[3 * depth + zd])
-            k.arrive(from_x.at[zd, pl.ds(0, half)], rs.at[4 * depth + zd])
-            k.arrive(from_y.at[zd, pl.ds(half, rest)], rs.at[5 * depth + zd])
-            add_into(block(k.me, zd), from_x.at[zd], from_y.at[zd])
+            k.arrive(from_xy.at[zd], rs.at[2 * depth + zd])
+            add_into(block(k.me, zd), from_xy.at[zd, 0], from_xy.at[zd, 1])
             wave(zd, 0)
             yield
 
@@ -611,25 +634,29 @@
         finish(block(k.me, k.z), False)
 
         def last_up():
-            k.arrive(from_up.at[k.z], rs.at[6 * depth + k.z])
+            k.arrive(from_up.at[k.z], rs.at[3 * depth + k.z])
             finish(from_up.at[k.z], True)
 
         def last_down():
-            k.arrive(from_down.at[k.z], rs.at[7 * depth + k.z])
+            k.arrive(from_down.at[k.z], rs.at[4 * depth + k.z])
             finish(from_down.at[k.z], True)
 
         pl.when(k.has_up)(last_up)
         pl.when(k.has_down)(last_down)
         yield
 
+    def left():
+        k.left(buf.at[pl.ds(0, 4 * depth - 1), pl.ds(low, rows)], ss.at[0])
+        yield
+
     steps = {"X": pure_x(), "Y": pure_y(), "D": diagonal(), "a": y_added(), "b": x_added(), "c": collect(), "e": end()}
-    steps |= {"v": waves(1), "w": waves(2)}
+    steps |= {"v": waves(1), "w": waves(2), ".": left()}
     return {name + key: step for key, step in steps.items()}
 
 
 def scatter_z_first(k, name, buf, index, low, rows, half, slots, ss, rs, finish):
     depth = k.depth
-    from_x_diag, from_y_diag, from_x, from_y, from_up, from_down = slots
+    from_x_diag, from_y_diag, from_xy, from_up, from_down = slots
     yx_of = (k.me, k.xs, k.ys, k.ds)
     rest = rows - half
     base = 8 * depth
@@ -637,8 +664,14 @@
     def block(yx, zd, lo=0, n=rows):
         return buf.at[index(yx, zd), pl.ds(low + lo, n)]
 
-    def send(condition, source, target, device, s, r):
-        k.start(condition, source, target, lambda: ss.at[s], lambda: rs.at[r], device)
+    def send(condition, source, target, device, r):
+        k.start(condition, source, target, ss.at[0], rs.at[r], device)
+
+    def x_part(lo, n):
+        return from_xy.at[0, 0, pl.ds(lo, n)]
+
+    def y_part(lo, n):
+        return from_xy.at[0, 1, pl.ds(lo, n)]
 
     def waves(which):
         yx = yx_of[which]
@@ -648,7 +681,7 @@
 
                 def send_z(condition, up, zd=zd, place=place):
                     slot, number = (from_down, 4 * depth + place) if up else (from_up, place)
-                    send(condition, lambda: block(yx, zd), lambda: slot.at[place], k.up_dev if up else k.down_dev, number, number)
+                    send(condition, lambda: block(yx, zd), lambda: slot.at[place], k.up_dev if up else k.down_dev, number)
 
                 along_z(
                     k, zd, number, block(yx, zd), from_up.at[place], from_down.at[place],
@@ -673,43 +706,45 @@
 
     def own_x():
         own(1)
-        send(None, lambda: block(k.xs, k.z, half, rest), lambda: from_x.at[0, pl.ds(half, rest)], k.x_dev, base + 2, base + 2)
+        send(None, lambda: block(k.xs, k.z, half, rest), lambda: x_part(half, rest), k.x_dev, base + 2)
         yield
 
     def own_y():
         own(2)
-        send(None, lambda: block(k.ys, k.z, 0, half), lambda: from_y.at[0, pl.ds(0, half)], k.y_dev, base + 3, base + 3)
+        send(None, lambda: block(k.ys, k.z, 0, half), lambda: y_part(0, half), k.y_dev, base + 2)
         yield
 
     def own_d():
         own(3)
-        send(None, lambda: block(k.ds, k.z, 0, half), lambda: from_y_diag.at[0], k.y_dev, base, base)
-        send(None, lambda: block(k.ds, k.z, half, rest), lambda: from_x_diag.at[0], k.x_dev, base + 1, base + 1)
+        send(None, lambda: block(k.ds, k.z, 0, half), lambda: from_y_diag.at[0], k.y_dev, base)
+        send(None, lambda: block(k.ds, k.z, half, rest), lambda: from_x_diag.at[0], k.x_dev, base + 1)
         yield
 
     def y_added():
         k.arrive(from_y_diag.at[0], rs.at[base])
         add_into(block(k.xs, k.z, 0, half), from_y_diag.at[0])
-        send(None, lambda: block(k.xs, k.z, 0, half), lambda: from_x.at[0, pl.ds(0, half)], k.x_dev, base + 4, base + 4)
+        send(None, lambda: block(k.xs, k.z, 0, half), lambda: x_part(0, half), k.x_dev, base + 2)
         yield
 
     def x_added():
         k.arrive(from_x_diag.at[0], rs.at[base + 1])
         add_into(block(k.ys, k.z, half, rest), from_x_diag.at[0])
-        send(None, lambda: block(k.ys, k.z, half, rest), lambda: from_y.at[0, pl.ds(half, rest)], k.y_dev, base + 5, base + 5)
+        send(None, lambda: block(k.ys, k.z, half, rest), lambda: y_part(half, rest), k.y_dev, base + 2)
         yield
 
     def end():
+        k.arrive(from_xy.at[0], rs.at[base + 2])
         finish(block(k.me, k.z), False)
-        k.arrive(from_x.at[0, pl.ds(half, rest)], rs.at[base + 2])
-        k.arrive(from_x.at[0, pl.ds(0, half)], rs.at[base + 4])
-        finish(from_x.at[0], True)
-        k.arrive(from_y.at[0, pl.ds(0, half)], rs.at[base + 3])
-        k.arrive(from_y.at[0, pl.ds(half, rest)], rs.at[base + 5])
-        finish(from_y.at[0], True)
+        finish(from_xy.at[0, 0], True)
+        finish(from_xy.at[0, 1], True)
+        yield
+
+    def left():
+        k.left(buf.at[pl.ds(0, 4 * depth - 1), pl.ds(low, rows)], ss.at[0])
         yield
 
     steps = {"O": own_me(), "X": own_x(), "Y": own_y(), "D": own_d(), "a": y_added(), "b": x_added(), "e": end()}
+    steps["."] = left()
     steps |= {str(which): waves(which) for which in range(4)}
     return {name + key: step for key, step in steps.items()}
 
@@ -801,10 +836,10 @@
     ):
         table["r" + name + "dx"] = ((depth, rows - half, lanes), kind)
         table["r" + name + "dy"] = ((depth, half, lanes), kind)
-        for place in ("x", "y", "u", "d"):
-            table["r" + name + place] = ((depth, rows, lanes), kind)
+        table["r" + name + "xy"] = ((depth, 2, rows, lanes), kind)
+        table["r" + name + "u"] = table["r" + name + "d"] = ((depth, rows, lanes), kind)
     table["rcdx"] = table["rcdy"] = ((1, 32, WIDTH), bf16)
-    table["rcx"] = table["rcy"] = ((1, 64, WIDTH), bf16)
+    table["rcxy"] = ((1, 2, 64, WIDTH), bf16)
     table["rcu"] = table["rcd"] = ((blocks, 64, WIDTH), bf16)
     table["out"] = table["dinp"] = ((SEQ, WIDTH), bf16)
     for name in ("gwq", "gwk", "gwv", "gwo"):
@@ -812,29 +847,29 @@
     table["gfc1"] = table["gfc2"] = ((UNITS, WIDTH), f32)
     table["gsmall"] = ((16, 128), f32)
     table["store"] = len(RESULTS)
-    for name, count in (
-        ("gq", 10 * depth), ("gb", 10 * depth), ("gt", 10 * depth), ("gc", 4 + 8 * depth),
-        ("sq", 8 * depth), ("sb", 8 * depth), ("st", 8 * depth), ("sc", 8 * depth + 6), ("e", 12),
+    for name, sent, came in (
+        ("gq", 2, 4 * depth + 1), ("gb", 2, 4 * depth), ("gt", 2, 4 * depth + 1), ("gc", 5, 4 * depth + 3),
+        ("sq", 1, 5 * depth), ("sb", 1, 5 * depth), ("st", 1, 5 * depth), ("sc", 1, 8 * depth + 3), ("e", 6, 6),
     ):
-        table[name + "_s"] = table[name + "_r"] = count
+        table[name + "_s"], table[name + "_r"] = sent, came
     return table
 
 
 PLAN = (
-    "own_blocks", "barrier", "S0", "M0", "L0", "own_cotangent", "norm1", "Sz", "Mz", "Sx", "Sy", "Mx", "My",
-    "Lx", "Ly", "Sz", "Mz", "Sx", "Sy", "Mx", "My", "F0", "Ld", "Sz", "Mz", "Sx", "Sy", "Mx", "My", "Fz",
-    "Sx", "Sy", "Mx", "My", "Sd", "Sd", "Sd", "Sd", "Ss", "vectors", "mixer_kernels", "gain1", "Md", "Md",
-    "Md", "Md", "Fz", "L4", "L5", "Ms", "Fx", "Fy", "Fz", "L6", "L7", "unpack", "project", "Fx", "Fy",
-    "mix0", "L4", "L5", "mix1", "L6", "L7", "Fx", "Fy", "mix2", "L4", "mix3", "hidden", "Fx", "Fy", "norm2",
-    "L5", "L6", "L7", "sibling_rows", "feed0", "feed_grads0", "l0", "feed1", "feed_grads1", "fX", "l1", "l0",
-    "feed2", "feed_grads2", "fY", "l2", "l1", "l0", "Fd", "Fd", "Fd", "Fd", "feed3", "feed_swap",
-    "feed_grads3", "fD", "l3", "l2", "l1", "back2", "grad_mixed", "back4", "fa", "fb", "l2", "l3", "back5",
-    "fa", "fb", "l3", "back6", "fa", "fb", "lX", "lY", "lO", "back7", "fa", "fb", "lD", "sent", "pack",
-    "grad_normed", "fc", "fc", "la", "lb", "back1", "fc", "fc", "core_sums", "mD", "mX", "mY", "fv", "fv",
-    "fv", "fv", "flip", "kernel0", "kernel1", "fw", "fw", "kernel2", "ma", "mb", "kernel3", "vector_tiles",
-    "finish_out", "small_sums", "sD", "sX", "sY", "ma", "mb", "ma", "mb", "ma", "mb", "sa", "sb", "sa", "sb",
-    "sa", "sb", "sa", "sb", "fe", "le", "mc", "sc", "mc", "sc", "mc", "sc", "mc", "sc", "mv", "sv", "mv",
-    "sv", "mv", "sv", "mv", "sv", "mw", "sw", "mw", "sw", "me", "se", "store",
+    "own_blocks", "barrier", "S0", "M0", "Sz", "Sx", "L0", "Sz", "Sx", "Sy", "Mz", "My", "Mx", "Sz", "Ly",
+    "Sd", "Sy", "norm1", "Mz", "My", "Mx", "Mz", "Sy", "L4", "L4", "Lx", "L4", "Sx", "own_cotangent", "Mx",
+    "My", "My", "Sx", "Md", "Sd", "Sy", "F0", "Sd", "Md", "Sd", "Mx", "Ss", "Fz", "Md", "vectors", "L5",
+    "Md", "mixer_kernels", "Fz", "Fx", "Ms", "unpack", "Fy", "L6", "L5", "gain1", "project", "mix0", "mix1",
+    "mix2", "mix3", "Fz", "hidden", "Ld", "norm2", "flip", "sibling_rows", "Fy", "feed0", "Fx",
+    "feed_grads0", "L6", "Fx", "L5", "Fy", "Fx", "l0", "feed1", "Fy", "L7", "feed_grads1", "fX", "l1", "Fd",
+    "L6", "feed2", "feed_grads2", "Fd", "L7", "fY", "l2", "L7", "Fd", "Fd", "feed3", "feed_grads3", "l1",
+    "fD", "feed_swap", "back2", "grad_mixed", "back4", "back5", "l1", "l2", "back6", "M.", "fb", "fa", "fa",
+    "back7", "l3", "pack", "fb", "fb", "l3", "fa", "kernel1", "core_sums", "fc", "mD", "kernel2", "fc", "fa",
+    "fb", "grad_normed", "mb", "l0", "mb", "finish_out", "fc", "fv", "l3", "mY", "l2", "fv", "mb", "back1",
+    "kernel0", "ma", "kernel3", "vector_tiles", "small_sums", "fc", "ma", "fv", "fw", "mX", "fw", "fv", "ma",
+    "sD", "sY", "mc", "ma", "l0", "mv", "mc", "mb", "mv", "mc", "lO", "sX", "sa", "mw", "sa", "sb", "sb",
+    "sb", "sb", "lD", "fe", "sc", "lY", "sc", "mw", "sa", "sv", "sw", "sv", "mv", "mc", "lX", "sa", "sc",
+    "la", "sw", "lb", "sc", "sv", "mv", "sv", "le", "me", "se", "store",
 )
 INPUTS = ("tok", "length", "cot", "iq", "ik", "iv", "io", "ifc1", "ifc2", "ibias", "ivec")
 RESULTS = ("out", "dinp", "gwq", "gwk", "gwv", "gwo", "gfc1", "gfc2", "gsmall")
@@ -867,7 +902,7 @@
     sib_rows = pl.ds(pl.multiple_of((1 - core) * SEQ, SEQ), SEQ)
 
     def swap(place, source, target):
-        k.start(None, lambda: source, lambda: target, lambda: m.e_s.at[place], lambda: m.e_r.at[place], k.sib_dev)
+        k.start(None, lambda: source, lambda: target, m.e_s.at[place], m.e_r.at[place], k.sib_dev)
 
     day = lax.broadcasted_iota(jnp.int32, (1, SEQ), 1).astype(f32)
     s_at = lax.broadcasted_iota(jnp.int32, (SEQ, SEQ), 0)
@@ -1011,13 +1046,13 @@
     steps |= gather_z_first(k, "M", m.qk, in_all, 0, UNITS, UNITS // 2, m.gq_s, m.gq_r, in_all_sib)
     steps |= gather_z_first(k, "F", m.ff, in_core, 0, 128, 64, m.gb_s, m.gb_r)
     steps |= gather_z_last(k, "L", m.ff, in_core, 128, 64, 32, m.gc_s, m.gc_r)
-    slots = (m.rbdx, m.rbdy, m.rbx, m.rby, m.rbu, m.rbd)
+    slots = (m.rbdx, m.rbdy, m.rbxy, m.rbu, m.rbd)
     steps |= scatter_z_last(k, "f", m.gff, in_core, 0, 128, 64, slots, m.sb_s, m.sb_r, finish_feed)
-    slots = (m.rcdx, m.rcdy, m.rcx, m.rcy, m.rcu, m.rcd)
+    slots = (m.rcdx, m.rcdy, m.rcxy, m.rcu, m.rcd)
     steps |= scatter_z_first(k, "l", m.gff, in_core, 128, 64, 32, slots, m.sc_s, m.sc_r, finish_last)
-    slots = (m.rqdx, m.rqdy, m.rqx, m.rqy, m.rqu, m.rqd)
+    slots = (m.rqdx, m.rqdy, m.rqxy, m.rqu, m.rqd)
     steps |= scatter_z_last(k, "m", m.qk, in_all, 0, UNITS, UNITS // 2, slots, m.sq_s, m.sq_r, finish_mats)
-    slots = (m.rtdx, m.rtdy, m.rtx, m.rty, m.rtu, m.rtd)
+    slots = (m.rtdx, m.rtdy, m.rtxy, m.rtu, m.rtd)
     steps |= scatter_z_last(k, "s", m.gs, in_all, 0, 16, 8, slots, m.st_s, m.st_r, finish_small)
 
     root = math.sqrt(2.0 / math.pi)
@@ -1133,7 +1168,7 @@
     def pack():
         lax.fori_loop(0, 2, pack_rows, 0)
         for yx in range(4):
-            swap(4 + yx, m.qk.at[pl.ds(in_all_sib(yx, 0), depth)], m.sr.at[pl.ds(yx * depth, depth)])
+            swap(4, m.qk.at[pl.ds(in_all_sib(yx, 0), depth)], m.sr.at[pl.ds(yx * depth, depth)])
 
     def grad_normed():
         m.dn[...] = jnp.transpose(
@@ -1154,18 +1189,15 @@
         row_loop(SEQ, 32, rows_of)
         stored("dinp").start()
 
-    def core_sum(yx):
-        k.arrive(m.sr.at[pl.ds(yx * depth, depth)], m.e_r.at[4 + yx])
-
-        def block_sum(zs, carry):
-            add_into(m.qk.at[in_all(yx, zs)], m.sr.at[yx * depth + zs])
+    def core_sums():
+        k.arrive(m.sr, m.e_r.at[4])
+
+        def block_sum(place, carry):
+            yx, zs = lax.div(place, depth), lax.rem(place, depth)
+            add_into(m.qk.at[in_all(yx, zs)], m.sr.at[place])
             return carry
 
-        lax.fori_loop(0, depth, block_sum, 0)
-
-    def core_sums():
-        for yx in range(4):
-            core_sum(yx)
+        lax.fori_loop(0, 4 * depth, block_sum, 0)
 
     def flip():
         turn = (s_at + t_at == SEQ - 1).astype(bf16)
@@ -1198,11 +1230,11 @@
                 mine = (row_at == 15) & (core == wide % 2)
                 m.gs[wide * depth + zs] = jnp.where(mine, own, tile)
         for yx in range(4):
-            swap(8 + yx, m.gs.at[pl.ds(in_all_sib(yx, 0), depth)], m.srs.at[pl.ds(yx * depth, depth)])
+            swap(5, m.gs.at[pl.ds(in_all_sib(yx, 0), depth)], m.srs.at[pl.ds(yx * depth, depth)])
 
     def small_sums():
+        k.arrive(m.srs, m.e_r.at[5])
         for yx in range(4):
-            k.arrive(m.srs.at[pl.ds(yx * depth, depth)], m.e_r.at[8 + yx])
             for zs in range(depth):
                 add_into(m.gs.at[in_all(yx, zs)], m.srs.at[yx * depth + zs])
 
@@ -1218,14 +1250,17 @@
     def store():
         for name in RESULTS[2:]:
             stored(name).start()
-        k.drain()
+        for group in "SFLflms":
+            next(steps[group + "."])
+        for place, extent in enumerate((m.ct.at[core_rows], m.n2.at[core_rows], m.dn2r, m.outr, m.sr, m.srs)):
+            k.left(extent, m.e_s.at[place])
         for name in RESULTS:
             stored(name).wait()
 
     compute = {
         "own_blocks": own_blocks, "barrier": k.barrier, "own_cotangent": own_cotangent, "norm1": norm1,
         "vectors": vectors, "mixer_kernels": mixer_kernels, "gain1": gain1, "unpack": unpack, "project": project,
-        "hidden": hidden, "norm2": norm2, "sibling_rows": sibling_rows, "feed_swap": feed_swap, "sent": partial(k.drain, "M"), "store": store,
+        "hidden": hidden, "norm2": norm2, "sibling_rows": sibling_rows, "feed_swap": feed_swap, "store": store,
         "back2": back2, "grad_mixed": grad_mixed, "pack": pack, "grad_normed": grad_normed, "back1": back1,
         "core_sums": core_sums, "flip": flip, "vector_tiles": vector_tiles, "small_sums": small_sums, "finish_out": finish_out,
     }
@@ -1243,20 +1278,11 @@
 
 
 def results_kernel(*refs):
-    count = len(RESULTS) - 1
-    sources, tile, targets, bias, vectors = refs[:count], refs[count], refs[9 : 9 + count], refs[17], refs[18]
-    held, came, left = refs[19 : 19 + count], refs[-2], refs[-1]
-    bring = [pltpu.make_async_copy(s, h, came.at[i]) for i, (s, h) in enumerate(zip(sources, held, strict=True))]
-    take = [pltpu.make_async_copy(h, t, left.at[i]) for i, (h, t) in enumerate(zip(held, targets, strict=True))]
-    for copy in bring:
-        copy.start()
+    sources, tile, targets, bias, vectors = refs[:8], refs[8], refs[9:17], refs[17], refs[18]
+    for source, target in zip(sources, targets, strict=True):
+        target[...] = source[...]
     bias[...] = tile[15:16, :UNITS]
     vectors[...] = tile[0:15, 0:24]
-    for first, second in zip(bring, take, strict=True):
-        first.wait()
-        second.start()
-    for copy in take:
-        copy.wait()
 
 
 def on_device_fast(
@@ -1289,9 +1315,8 @@
     results = pl.pallas_call(
         results_kernel,
         out_shape=[shape(x.shape, x.dtype) for x in got[:8]] + [shape((1, UNITS), f32), shape((15, 24), f32)],
-        in_specs=[anywhere] * 8 + [in_vmem],
-        out_specs=[anywhere] * 8 + [in_vmem] * 2,
-        scratch_shapes=[pltpu.VMEM(x.shape, x.dtype) for x in got[:8]] + [pltpu.SemaphoreType.DMA((8,))] * 2,
+        in_specs=[in_vmem] * 9,
+        out_specs=[in_vmem] * 10,
         name="results",
     )(*got)
     out, grad_in, g_query, g_key, g_value, g_out, g_fc1, g_fc2, g_bias, g_vectors = results

time: 153 us -> 129 us (0.84); the launches traced: 153 us -> 126 us
  Pallas kernels: 151 us -> 125 us
    pallas_call x1, Pallas kernels: 148 us -> 122 us  [on_device_fast(): pl.pallas_call(partial(layer_kernel, depth), out_shape=[shape((SEQ, WIDTH...]
where the time goes in v3:
time: 129 us; the launch traced here: 126 us
  Pallas kernels  125 us (97%)
  between operations  1.42 us (1%)
    pallas_call x1, Pallas kernels, on_device_fast(): pl.pallas_call(partial(layer_kernel, depth), out_shape=[shape((SEQ, WIDTH...  122 us
    pallas_call x1, Pallas kernels, on_device_fast(): pl.pallas_call(results_kernel, out_shape=[shape(x.shape, x.dtype) for x i...  2.62 us

profile of v3, /device:TPU:0, one launch (start us, length us, event | category | flops | bytes accessed | tf_op | source)
XLA Modules:
  0.0 126.4 jit_solution(919799133882177032)
XLA Ops:
  1.3 122.3 %h3_layer.1 = (bf16[256,768]{1,0:T(8,128)(2,1)}, bf16[256,768]{1,0:T(8,128)(2,1)}, f32[24,768]{1,0:T(8,128)}, f32[24,768]{1,0:T(8,128)}, f32[24,768]{1,0:T(8,128...) custom-call(bf16[256,768]{1,0:T(8,128)(2,1)} %refs_0_.1, ...), custom_call_target="tpu_custom_call" | custom-call | tf_op jit(solution)/shard_map/h3_layer/pallas_call | solution.py:1299
  123.6 2.6 %results.1 = (bf16[256,768]{1,0:T(8,128)(2,1)}, bf16[256,768]{1,0:T(8,128)(2,1)}, f32[24,768]{1,0:T(8,128)}, f32[24,768]{1,0:T(8,128)}, f32[24,768]{1,0:T(8,128)...) custom-call(bf16[256,768]{1,0:T(8,128)(2,1)} %get-tuple-element.29.refs, ...), custom_call_target="tpu_custom_call" | custom-call | tf_op jit(solution)/shard_map/results/pallas_call | solution.py:1315

commit v4 on v3

--- a/solution.py
+++ b/solution.py
@@ -467,66 +467,98 @@
     return {name + key: step for key, step in steps.items()}
 
 
-def gather_z_last(k, name, buf, index, low, rows, half, ss, rs):
+def gather_pair_z_first(k, name, buf, index, low, rows, ss, rs):
     depth = k.depth
-    yx_of = (k.me, k.xs, k.ys, k.ds)
-
-    def block(yx, zs, lo=0, n=rows):
-        return buf.at[index(yx, zs), pl.ds(low + lo, n)]
-
-    def send(condition, yx, zs, lo, n, device, r, way=0):
-        ref = lambda: block(yx, zs, lo, n)
+
+    def block(yx, zs):
+        return buf.at[index(yx, zs), pl.ds(low, rows)]
+
+    def extent(blocks):
+        return buf.at[pl.ds(0, blocks), pl.ds(low, rows)]
+
+    def send(condition, zs, device, r, way):
+        ref = lambda: block(k.me, zs)
         k.start(condition, ref, ref, ss.at[way], rs.at[r], device)
 
+    def along(condition, zs, up, down):
+        if up:
+            send(both(condition, k.has_up), zs, k.up_dev, zs, 1)
+        if down:
+            send(both(condition, k.has_down), zs, k.down_dev, zs, 1)
+
+    def own():
+        along(None, k.z, True, True)
+        send(None, k.z, k.y_dev, depth + k.z, 0)
+        yield
+
+    def z_steps():
+        for d in range(1, depth):
+            for condition, zs, below in near(k, d):
+                when(condition, lambda zs=zs: k.arrive(block(k.me, zs), rs.at[zs]))
+                along(condition, zs, below, not below)
+                send(condition, zs, k.y_dev, depth + zs, 0)
+            yield
+
+    def y_steps():
+        for d in range(depth):
+            for condition, zs, _ in near(k, d):
+                when(condition, lambda zs=zs: k.arrive(block(k.ys, zs), rs.at[depth + zs]))
+            yield
+
+    def left():
+        k.left(extent(depth), ss.at[0])
+        k.left_along(extent, ss.at[1])
+        yield
+
+    steps = {"0": own(), "z": z_steps(), "y": y_steps(), ".": left()}
+    return {name + key: step for key, step in steps.items()}
+
+
+def gather_pair_z_last(k, name, buf, index, low, rows, ss, rs):
+    depth = k.depth
+    yx_of = (k.me, k.ys)
+
+    def block(yx, zs):
+        return buf.at[index(yx, zs), pl.ds(low, rows)]
+
+    def extent(blocks):
+        return buf.at[pl.ds(0, blocks), pl.ds(low, rows)]
+
+    def send(condition, yx, zs, device, r, way):
+        ref = lambda: block(yx, zs)
+        k.start(condition, ref, ref, ss.at[way], rs.at[r], device)
+
     def along(condition, which, zs, up, down):
-        yx, place = yx_of[which], 3 + which * depth + zs
+        place = 1 + which * depth + zs
         if up:
-            send(both(condition, k.has_up), yx, zs, 0, rows, k.up_dev, place, 1 + which)
+            send(both(condition, k.has_up), yx_of[which], zs, k.up_dev, place, 1 + which)
         if down:
-            send(both(condition, k.has_down), yx, zs, 0, rows, k.down_dev, place, 1 + which)
+            send(both(condition, k.has_down), yx_of[which], zs, k.down_dev, place, 1 + which)
 
     def own():
-        send(None, k.me, k.z, 0, rows, k.x_dev, 0)
-        send(None, k.me, k.z, 0, rows, k.y_dev, 1)
+        send(None, k.me, k.z, k.y_dev, 0, 0)
         along(None, 0, k.z, True, True)
         yield
 
-    def x_step():
-        k.arrive(block(k.xs, k.z), rs.at[0])
-        send(None, k.xs, k.z, 0, half, k.y_dev, 2)
+    def y_step():
+        k.arrive(block(k.ys, k.z), rs.at[0])
         along(None, 1, k.z, True, True)
-        yield
-
-    def y_step():
-        k.arrive(block(k.ys, k.z), rs.at[1])
-        send(None, k.ys, k.z, half, rows - half, k.x_dev, 2)
-        along(None, 2, k.z, True, True)
-        yield
-
-    def d_step():
-        k.arrive(block(k.ds, k.z), rs.at[2])
-        along(None, 3, k.z, True, True)
         yield
 
     def z_steps(which):
         for d in range(1, depth):
             for condition, zs, below in near(k, d):
-                when(condition, lambda zs=zs: k.arrive(block(yx_of[which], zs), rs.at[3 + which * depth + zs]))
+                when(condition, lambda zs=zs: k.arrive(block(yx_of[which], zs), rs.at[1 + which * depth + zs]))
                 along(condition, which, zs, below, not below)
             yield
 
-    def extent(blocks):
-        return buf.at[pl.ds(0, blocks), pl.ds(low, rows)]
-
     def left():
-        k.left(extent(3), ss.at[0])
-        for which in range(4):
+        k.left(extent(1), ss.at[0])
+        for which in range(2):
             k.left_along(extent, ss.at[1 + which])
         yield
 
-    steps = {"0": own(), "x": x_step(), "y": y_step(), "d": d_step(), ".": left()}
-    for which in range(4):
-        steps[str(4 + which)] = z_steps(which)
+    steps = {"0": own(), "y": y_step(), "4": z_steps(0), "5": z_steps(1), ".": left()}
     return {name + key: step for key, step in steps.items()}
 
 
@@ -579,18 +611,18 @@
     def pure_x():
         for zd in order:
             send(None, lambda zd=zd: block(k.xs, zd, half, rest), lambda zd=zd: x_part(zd, half, rest), k.x_dev, 2 * depth + zd)
-        yield
+            yield
 
     def pure_y():
         for zd in order:
             send(None, lambda zd=zd: block(k.ys, zd, 0, half), lambda zd=zd: y_part(zd, 0, half), k.y_dev, 2 * depth + zd)
-        yield
+            yield
 
     def diagonal():
         for zd in order:
             send(None, lambda zd=zd: block(k.ds, zd, 0, half), lambda zd=zd: from_y_diag.at[zd], k.y_dev, zd)
             send(None, lambda zd=zd: block(k.ds, zd, half, rest), lambda zd=zd: from_x_diag.at[zd], k.x_dev, depth + zd)
-        yield
+            yield
 
     def y_added():
         for zd in order:
@@ -654,24 +686,79 @@
     return {name + key: step for key, step in steps.items()}
 
 
-def scatter_z_first(k, name, buf, index, low, rows, half, slots, ss, rs, finish):
+def scatter_pair_z_last(k, name, buf, index, low, rows, slots, ss, rs, finish):
     depth = k.depth
-    from_x_diag, from_y_diag, from_xy, from_up, from_down = slots
-    yx_of = (k.me, k.xs, k.ys, k.ds)
-    rest = rows - half
-    base = 8 * depth
-
-    def block(yx, zd, lo=0, n=rows):
-        return buf.at[index(yx, zd), pl.ds(low + lo, n)]
+    from_y, from_up, from_down = slots
+    order = scatter_order(depth)
+
+    def block(yx, zd):
+        return buf.at[index(yx, zd), pl.ds(low, rows)]
 
     def send(condition, source, target, device, r):
         k.start(condition, source, target, ss.at[0], rs.at[r], device)
 
-    def x_part(lo, n):
-        return from_xy.at[0, 0, pl.ds(lo, n)]
-
-    def y_part(lo, n):
-        return from_xy.at[0, 1, pl.ds(lo, n)]
+    def pure_y():
+        for zd in order:
+            send(None, lambda zd=zd: block(k.ys, zd), lambda zd=zd: from_y.at[zd], k.y_dev, zd)
+            yield
+
+    def wave(zd, number):
+        def send_z(condition, up):
+            slot = from_down if up else from_up
+            place = (2 if up else 1) * depth + zd
+            send(condition, lambda: block(k.me, zd), lambda: slot.at[zd], k.up_dev if up else k.down_dev, place)
+
+        along_z(
+            k, zd, number, block(k.me, zd), from_up.at[zd], from_down.at[zd],
+            rs.at[depth + zd], rs.at[2 * depth + zd], send_z,
+        )
+
+    def collect():
+        for zd in order:
+            k.arrive(from_y.at[zd], rs.at[zd])
+            add_into(block(k.me, zd), from_y.at[zd])
+            wave(zd, 0)
+            yield
+
+    def waves(number):
+        for zd in order:
+            if zd < depth - 1 - number or zd > number:
+                wave(zd, number)
+                yield
+
+    def end():
+        finish(block(k.me, k.z), False)
+
+        def last_up():
+            k.arrive(from_up.at[k.z], rs.at[depth + k.z])
+            finish(from_up.at[k.z], True)
+
+        def last_down():
+            k.arrive(from_down.at[k.z], rs.at[2 * depth + k.z])
+            finish(from_down.at[k.z], True)
+
+        pl.when(k.has_up)(last_up)
+        pl.when(k.has_down)(last_down)
+        yield
+
+    def left():
+        k.left(buf.at[pl.ds(0, 2 * depth - 1), pl.ds(low, rows)], ss.at[0])
+        yield
+
+    steps = {"Y": pure_y(), "c": collect(), "v": waves(1), "w": waves(2), "e": end(), ".": left()}
+    return {name + key: step for key, step in steps.items()}
+
+
+def scatter_pair_z_first(k, name, buf, index, low, rows, slots, ss, rs, finish):
+    depth = k.depth
+    from_y, from_up, from_down = slots
+    yx_of = (k.me, k.ys)
+
+    def block(yx, zd):
+        return buf.at[index(yx, zd), pl.ds(low, rows)]
+
+    def send(condition, source, target, device, r):
+        k.start(condition, source, target, ss.at[0], rs.at[r], device)
 
     def waves(which):
         yx = yx_of[which]
@@ -680,12 +767,12 @@
                 place = which * depth + zd
 
                 def send_z(condition, up, zd=zd, place=place):
-                    slot, number = (from_down, 4 * depth + place) if up else (from_up, place)
+                    slot, number = (from_down, 2 * depth + place) if up else (from_up, place)
                     send(condition, lambda: block(yx, zd), lambda: slot.at[place], k.up_dev if up else k.down_dev, number)
 
                 along_z(
                     k, zd, number, block(yx, zd), from_up.at[place], from_down.at[place],
-                    rs.at[place], rs.at[4 * depth + place], send_z,
+                    rs.at[place], rs.at[2 * depth + place], send_z,
                 )
             yield
 
@@ -698,54 +785,28 @@
             add_into(block(yx, k.z), slot)
 
         pl.when(k.has_up)(lambda: take(from_up.at[place], rs.at[place]))
-        pl.when(k.has_down)(lambda: take(from_down.at[place], rs.at[4 * depth + place]))
+        pl.when(k.has_down)(lambda: take(from_down.at[place], rs.at[2 * depth + place]))
 
     def own_me():
         own(0)
         yield
 
-    def own_x():
+    def own_y():
         own(1)
-        send(None, lambda: block(k.xs, k.z, half, rest), lambda: x_part(half, rest), k.x_dev, base + 2)
-        yield
-
-    def own_y():
-        own(2)
-        send(None, lambda: block(k.ys, k.z, 0, half), lambda: y_part(0, half), k.y_dev, base + 2)
-        yield
-
-    def own_d():
-        own(3)
-        send(None, lambda: block(k.ds, k.z, 0, half), lambda: from_y_diag.at[0], k.y_dev, base)
-        send(None, lambda: block(k.ds, k.z, half, rest), lambda: from_x_diag.at[0], k.x_dev, base + 1)
-        yield
-
-    def y_added():
-        k.arrive(from_y_diag.at[0], rs.at[base])
-        add_into(block(k.xs, k.z, 0, half), from_y_diag.at[0])
-        send(None, lambda: block(k.xs, k.z, 0, half), lambda: x_part(0, half), k.x_dev, base + 2)
-        yield
-
-    def x_added():
-        k.arrive(from_x_diag.at[0], rs.at[base + 1])
-        add_into(block(k.ys, k.z, half, rest), from_x_diag.at[0])
-        send(None, lambda: block(k.ys, k.z, half, rest), lambda: y_part(half, rest), k.y_dev, base + 2)
+        send(None, lambda: block(k.ys, k.z), lambda: from_y.at[0], k.y_dev, 4 * depth)
         yield
 
     def end():
-        k.arrive(from_xy.at[0], rs.at[base + 2])
+        k.arrive(from_y.at[0], rs.at[4 * depth])
         finish(block(k.me, k.z), False)
-        finish(from_xy.at[0, 0], True)
-        finish(from_xy.at[0, 1], True)
+        finish(from_y.at[0], True)
         yield
 
     def left():
-        k.left(buf.at[pl.ds(0, 4 * depth - 1), pl.ds(low, rows)], ss.at[0])
-        yield
-
-    steps = {"O": own_me(), "X": own_x(), "Y": own_y(), "D": own_d(), "a": y_added(), "b": x_added(), "e": end()}
-    steps["."] = left()
-    steps |= {str(which): waves(which) for which in range(4)}
+        k.left(buf.at[pl.ds(0, 2 * depth - 1), pl.ds(low, rows)], ss.at[0])
+        yield
+
+    steps = {"0": waves(0), "1": waves(1), "O": own_me(), "Y": own_y(), "e": end(), ".": left()}
     return {name + key: step for key, step in steps.items()}
 
 
@@ -753,9 +814,9 @@
 HEADS = WIDTH // HEAD_SIZE
 
 
-def row_loop(total, step, body):
+def row_loop(total, step, body, first=0):
     def once(i, carry):
-        body(pl.multiple_of(i * step, step), step)
+        body(pl.multiple_of(first + i * step, step), step)
         return carry
 
     lax.fori_loop(0, total // step, once, 0)
@@ -779,12 +840,12 @@
 
 
 def scratch_of(depth):
-    devices, blocks = 8 * depth, 4 * depth
+    devices, blocks, half = 8 * depth, 4 * depth, 2 * depth
     table = {
         "qk": ((devices, UNITS, WIDTH), bf16),
-        "ff": ((blocks, 2 * UNITS, WIDTH), bf16),
+        "ff": ((half, 2 * UNITS, WIDTH), bf16),
         "sm": ((devices, 16, 128), f32),
-        "gff": ((blocks, 2 * UNITS, WIDTH), bf16),
+        "gff": ((half, 2 * UNITS, WIDTH), bf16),
         "gs": ((devices, 16, 128), f32),
         "sr": ((blocks, UNITS, WIDTH), bf16),
         "srs": ((blocks, 16, 128), f32),
@@ -798,15 +859,20 @@
         "hid": ((SEQ, WIDTH), f32),
         "s2": ((SEQ, WIDTH), f32),
         "i2": ((SEQ, 128), f32),
-        "n2": ((2 * SEQ, WIDTH), bf16),
-        "ct": ((2 * SEQ, WIDTH), bf16),
-        "outp": ((2 * SEQ, WIDTH), f32),
-        "dn2": ((2 * SEQ, WIDTH), f32),
-        "outr": ((SEQ, WIDTH), f32),
-        "dn2r": ((SEQ, WIDTH), f32),
-        "act": ((2 * SEQ, UNITS * depth), bf16),
-        "dp": ((2 * SEQ, UNITS * depth), bf16),
+        "n2": ((4 * SEQ, WIDTH), bf16),
+        "ct": ((4 * SEQ, WIDTH), bf16),
+        "outp": ((4 * SEQ, WIDTH), f32),
+        "dn2": ((4 * SEQ, WIDTH), f32),
+        "outs": ((SEQ, WIDTH), f32),
+        "dn2s": ((SEQ, WIDTH), f32),
+        "outb": ((SEQ, WIDTH), f32),
+        "dn2b": ((SEQ, WIDTH), f32),
+        "outx": ((2, SEQ, WIDTH), bf16),
+        "dn2x": ((2, SEQ, WIDTH), bf16),
+        "act": ((2, 4 * SEQ, UNITS * depth), bf16),
+        "dp": ((2, 4 * SEQ, UNITS * depth), bf16),
         "da": ((SEQ, WIDTH), bf16),
+        "dk": ((WIDTH, SEQ), f32),
         "dn": ((SEQ, WIDTH), f32),
         "nmt": ((WIDTH, SEQ), bf16),
         "qt": ((WIDTH, SEQ), bf16),
@@ -826,21 +892,16 @@
         "vecc": ((WIDTH, 128), f32),
         "colsum": ((WIDTH, 128), f32),
         "gvec": ((16, WIDTH), f32),
-        "bias": ((4, 8, UNITS * depth), f32),
-        "gbias": ((blocks, 8, 128), f32),
+        "bias": ((2, 8, UNITS * depth), f32),
+        "gbias": ((half, 8, 128), f32),
     }
-    for name, rows, half, lanes, kind in (
-        ("q", UNITS, UNITS // 2, WIDTH, bf16),
-        ("b", 128, 64, WIDTH, bf16),
-        ("t", 16, 8, 128, f32),
-    ):
-        table["r" + name + "dx"] = ((depth, rows - half, lanes), kind)
-        table["r" + name + "dy"] = ((depth, half, lanes), kind)
+    for name, rows, lanes, kind in (("q", UNITS, WIDTH, bf16), ("t", 16, 128, f32)):
+        table["r" + name + "dx"] = table["r" + name + "dy"] = ((depth, rows // 2, lanes), kind)
         table["r" + name + "xy"] = ((depth, 2, rows, lanes), kind)
         table["r" + name + "u"] = table["r" + name + "d"] = ((depth, rows, lanes), kind)
-    table["rcdx"] = table["rcdy"] = ((1, 32, WIDTH), bf16)
-    table["rcxy"] = ((1, 2, 64, WIDTH), bf16)
-    table["rcu"] = table["rcd"] = ((blocks, 64, WIDTH), bf16)
+    table["rby"] = table["rbu"] = table["rbd"] = ((depth, 128, WIDTH), bf16)
+    table["rcy"] = ((1, 64, WIDTH), bf16)
+    table["rcu"] = table["rcd"] = ((half, 64, WIDTH), bf16)
     table["out"] = table["dinp"] = ((SEQ, WIDTH), bf16)
     for name in ("gwq", "gwk", "gwv", "gwo"):
         table[name] = ((24, WIDTH), f32)
@@ -848,28 +909,30 @@
     table["gsmall"] = ((16, 128), f32)
     table["store"] = len(RESULTS)
     for name, sent, came in (
-        ("gq", 2, 4 * depth + 1), ("gb", 2, 4 * depth), ("gt", 2, 4 * depth + 1), ("gc", 5, 4 * depth + 3),
-        ("sq", 1, 5 * depth), ("sb", 1, 5 * depth), ("st", 1, 5 * depth), ("sc", 1, 8 * depth + 3), ("e", 6, 6),
+        ("gq", 2, 4 * depth + 1), ("gb", 2, 2 * depth), ("gt", 2, 4 * depth + 1), ("gc", 3, 2 * depth + 1),
+        ("sq", 1, 5 * depth), ("sb", 1, 3 * depth), ("st", 1, 5 * depth), ("sc", 1, 4 * depth + 1), ("e", 21, 21),
     ):
         table[name + "_s"], table[name + "_r"] = sent, came
     return table
 
 
 PLAN = (
-    "own_blocks", "barrier", "S0", "M0", "Sz", "Sx", "L0", "Sz", "Sx", "Sy", "Mz", "My", "Mx", "Sz", "Ly",
-    "Sd", "Sy", "norm1", "Mz", "My", "Mx", "Mz", "Sy", "L4", "L4", "Lx", "L4", "Sx", "own_cotangent", "Mx",
-    "My", "My", "Sx", "Md", "Sd", "Sy", "F0", "Sd", "Md", "Sd", "Mx", "Ss", "Fz", "Md", "vectors", "L5",
-    "Md", "mixer_kernels", "Fz", "Fx", "Ms", "unpack", "Fy", "L6", "L5", "gain1", "project", "mix0", "mix1",
-    "mix2", "mix3", "Fz", "hidden", "Ld", "norm2", "flip", "sibling_rows", "Fy", "feed0", "Fx",
-    "feed_grads0", "L6", "Fx", "L5", "Fy", "Fx", "l0", "feed1", "Fy", "L7", "feed_grads1", "fX", "l1", "Fd",
-    "L6", "feed2", "feed_grads2", "Fd", "L7", "fY", "l2", "L7", "Fd", "Fd", "feed3", "feed_grads3", "l1",
-    "fD", "feed_swap", "back2", "grad_mixed", "back4", "back5", "l1", "l2", "back6", "M.", "fb", "fa", "fa",
-    "back7", "l3", "pack", "fb", "fb", "l3", "fa", "kernel1", "core_sums", "fc", "mD", "kernel2", "fc", "fa",
-    "fb", "grad_normed", "mb", "l0", "mb", "finish_out", "fc", "fv", "l3", "mY", "l2", "fv", "mb", "back1",
-    "kernel0", "ma", "kernel3", "vector_tiles", "small_sums", "fc", "ma", "fv", "fw", "mX", "fw", "fv", "ma",
-    "sD", "sY", "mc", "ma", "l0", "mv", "mc", "mb", "mv", "mc", "lO", "sX", "sa", "mw", "sa", "sb", "sb",
-    "sb", "sb", "lD", "fe", "sc", "lY", "sc", "mw", "sa", "sv", "sw", "sv", "mv", "mc", "lX", "sa", "sc",
-    "la", "sw", "lb", "sc", "sv", "mv", "sv", "le", "me", "se", "store",
+    "own_blocks", "barrier", "S0", "M0", "Sx", "Sz", "L0", "Sy", "Sy", "Sz", "Sx", "Mz", "Sx", "Sd", "Sz",
+    "My", "Sx", "Mx", "Sy", "Mz", "norm1", "Sy", "Sd", "Mz", "L4", "My", "Mx", "Mx", "Mx", "F0", "Ly", "My",
+    "Sd", "Sd", "Ss", "vectors", "My", "own_cotangent", "mixer_kernels", "gain1", "Md", "Md", "Fz", "Md",
+    "Md", "L4", "Ms", "unpack", "project", "mix0", "mix1", "mix2", "Fz", "mix3", "hidden", "norm2", "Fz",
+    "Fy", "M.", "sibling_rows", "L5", "pass_ct", "L4", "feed0o", "pass_n2_0", "feed0x0", "Fy", "L5",
+    "diagonal_rows0", "feed0s", "feed0d0", "pass_n2_1", "L5", "feed0x1", "Fy", "diagonal_rows1", "feed0d1",
+    "Fy", "feed1d0", "to_diagonal0", "feed1x0", "feed1x1", "feed1s", "to_x0", "feed1o", "feed1d1",
+    "feed_grads1", "fY", "flip", "to_diagonal1", "l1", "fY", "fY", "fY", "feed_grads0", "out_to_diagonal",
+    "to_sibling", "l0", "to_x1", "out_to_x", "back2_0", "back2_1", "grad_mixed", "back4", "back5", "back6",
+    "fc", "back7", "pack0", "pack1", "fc", "fc", "core_sum0", "l0", "mD", "grad_normed", "finish_out",
+    "core_sum1", "mD", "mb", "mY", "back1", "core_sum2", "l1", "mX", "fv", "kernel0", "core_sum3", "l1",
+    "ma", "l0", "fc", "kernel3", "fv", "fv", "ma", "mb", "mY", "mX", "kernel1", "mD", "kernel2", "fv", "mc",
+    "vector_tiles", "small_sums", "fw", "sD", "sX", "mY", "sD", "mb", "mX", "mD", "mc", "sY", "mv", "mv",
+    "sa", "sa", "ma", "fw", "sb", "sY", "mb", "sX", "sb", "mY", "sD", "mX", "mw", "mc", "sc", "sY", "lO",
+    "sb", "ma", "mw", "sX", "sc", "sD", "fe", "lY", "sX", "sv", "sY", "sv", "mv", "mc", "sa", "sa", "sc",
+    "sb", "sw", "sw", "le", "mv", "sv", "sc", "me", "sv", "se", "store",
 )
 INPUTS = ("tok", "length", "cot", "iq", "ik", "iv", "io", "ifc1", "ifc2", "ibias", "ivec")
 RESULTS = ("out", "dinp", "gwq", "gwk", "gwv", "gwo", "gfc1", "gfc2", "gsmall")
@@ -888,21 +951,20 @@
     def in_all_sib(yx, zs):
         return (yx * 2 + (1 - core)) * depth + zs
 
-    def in_core(yx, zs):
-        return yx * depth + zs
-
-    def chip_rows(start, step):
-        return pl.ds(pl.multiple_of(core * SEQ + start, step), step)
+    def in_pair(yx, zs):
+        return lax.div(yx, 2) * depth + zs
+
+    places = {"o": k.x * 2 + core, "s": k.x * 2 + 1 - core, "x": (1 - k.x) * 2 + core, "d": (1 - k.x) * 2 + 1 - core}
+
+    def rows_at(who, start=0, step=SEQ):
+        return pl.ds(pl.multiple_of(places[who] * SEQ + start, step), step)
 
     def stored(name):
         place = RESULTS.index(name)
         return pltpu.make_async_copy(getattr(m, name), getattr(m, "to_" + name), m.store.at[place])
 
-    core_rows = pl.ds(pl.multiple_of(core * SEQ, SEQ), SEQ)
-    sib_rows = pl.ds(pl.multiple_of((1 - core) * SEQ, SEQ), SEQ)
-
-    def swap(place, source, target):
-        k.start(None, lambda: source, lambda: target, m.e_s.at[place], m.e_r.at[place], k.sib_dev)
+    def swap(place, source, target, device=None):
+        k.start(None, lambda: source, lambda: target, m.e_s.at[place], m.e_r.at[place], device or k.sib_dev)
 
     day = lax.broadcasted_iota(jnp.int32, (1, SEQ), 1).astype(f32)
     s_at = lax.broadcasted_iota(jnp.int32, (SEQ, SEQ), 0)
@@ -917,12 +979,22 @@
         m.sm[here] = jnp.zeros((16, 128), f32)
         m.sm[here, 0:15, 0:24] = m.ivec[...].astype(f32)
         m.sm[here, 15:16, 0:UNITS] = m.ibias[...].astype(f32)
-        m.ff[in_core(k.me, k.z), 0:UNITS] = m.ifc1[...]
-        m.ff[in_core(k.me, k.z), UNITS : 2 * UNITS] = m.ifc2[...]
+        m.ff[in_pair(k.me, k.z), 0:UNITS] = m.ifc1[...]
+        m.ff[in_pair(k.me, k.z), UNITS : 2 * UNITS] = m.ifc2[...]
+
+    def half_at(who, half):
+        return rows_at(who, half * (SEQ // 2), SEQ // 2)
 
     def own_cotangent():
-        m.ct[core_rows] = m.cot[...]
-        swap(0, m.ct.at[core_rows], m.ct.at[core_rows])
+        m.ct[rows_at("o")] = m.cot[...]
+        ref = m.ct.at[rows_at("o")]
+        swap(0, ref, ref)
+        swap(1, ref, ref, k.x_dev)
+
+    def pass_ct():
+        ref = m.ct.at[rows_at("x")]
+        k.arrive(ref, m.e_r.at[1])
+        swap(2, ref, ref)
 
     def norm1():
         def rows_of(start, step):
@@ -946,12 +1018,13 @@
             total = total + (pltpu.roll(padded, 96 * wide, 1) if wide else padded)
         m.vec[...] = total
         m.vecc[...] = jnp.transpose(jnp.concatenate([total, jnp.zeros((112, WIDTH), f32)], axis=0))
-        for yx in range(4):
+        for y in range(2):
             line = jnp.zeros((16, UNITS * depth), f32)
             for zs in range(depth):
-                tile = jnp.concatenate([m.sm[in_all(yx, zs)], jnp.zeros((16, UNITS * depth - 128), f32)], axis=1)
+                tile = m.sm[in_all(y * 2 + k.x, zs)]
+                tile = jnp.concatenate([tile, jnp.zeros((16, UNITS * depth - 128), f32)], axis=1)
                 line = line + (pltpu.roll(tile, UNITS * zs, 1) if zs else tile)
-            m.bias[yx] = line[8:16]
+            m.bias[y] = line[8:16]
 
     def head_kernel(h, carry):
         rows = head_rows(h)
@@ -1014,14 +1087,28 @@
             scaled = centred * inverse
             m.s2[rows] = scaled
             m.i2[rows] = jnp.broadcast_to(inverse, (step, 128))
-            m.n2[chip_rows(start, step)] = (scaled * m.vec[12:13] + m.vec[13:14]).astype(bf16)
+            m.n2[rows_at("o", start, step)] = (scaled * m.vec[12:13] + m.vec[13:14]).astype(bf16)
 
         row_loop(SEQ, 32, rows_of)
-        swap(1, m.n2.at[core_rows], m.n2.at[core_rows])
+        ref = m.n2.at[rows_at("o")]
+        swap(3, ref, ref)
+        for half in range(2):
+            ref = m.n2.at[half_at("o", half)]
+            swap(4 + half, ref, ref, k.x_dev)
+
+    def pass_n2(half):
+        ref = m.n2.at[half_at("x", half)]
+        k.arrive(ref, m.e_r.at[4 + half])
+        swap(6 + half, ref, ref)
 
     def sibling_rows():
-        k.arrive(m.ct.at[sib_rows], m.e_r.at[0])
-        k.arrive(m.n2.at[sib_rows], m.e_r.at[1])
+        k.arrive(m.ct.at[rows_at("s")], m.e_r.at[0])
+        k.arrive(m.n2.at[rows_at("s")], m.e_r.at[3])
+
+    def diagonal_rows(half):
+        if half == 0:
+            k.arrive(m.ct.at[rows_at("d")], m.e_r.at[2])
+        k.arrive(m.n2.at[half_at("d", half)], m.e_r.at[6 + half])
 
     def finish_feed(ref, more):
         value = ref[...].astype(f32)
@@ -1044,12 +1131,12 @@
     steps = {}
     steps |= gather_z_first(k, "S", m.sm, in_all, 0, 16, 8, m.gt_s, m.gt_r, in_all_sib)
     steps |= gather_z_first(k, "M", m.qk, in_all, 0, UNITS, UNITS // 2, m.gq_s, m.gq_r, in_all_sib)
-    steps |= gather_z_first(k, "F", m.ff, in_core, 0, 128, 64, m.gb_s, m.gb_r)
-    steps |= gather_z_last(k, "L", m.ff, in_core, 128, 64, 32, m.gc_s, m.gc_r)
-    slots = (m.rbdx, m.rbdy, m.rbxy, m.rbu, m.rbd)
-    steps |= scatter_z_last(k, "f", m.gff, in_core, 0, 128, 64, slots, m.sb_s, m.sb_r, finish_feed)
-    slots = (m.rcdx, m.rcdy, m.rcxy, m.rcu, m.rcd)
-    steps |= scatter_z_first(k, "l", m.gff, in_core, 128, 64, 32, slots, m.sc_s, m.sc_r, finish_last)
+    steps |= gather_pair_z_first(k, "F", m.ff, in_pair, 0, 128, m.gb_s, m.gb_r)
+    steps |= gather_pair_z_last(k, "L", m.ff, in_pair, 128, 64, m.gc_s, m.gc_r)
+    slots = (m.rby, m.rbu, m.rbd)
+    steps |= scatter_pair_z_last(k, "f", m.gff, in_pair, 0, 128, slots, m.sb_s, m.sb_r, finish_feed)
+    slots = (m.rcy, m.rcu, m.rcd)
+    steps |= scatter_pair_z_first(k, "l", m.gff, in_pair, 128, 64, slots, m.sc_s, m.sc_r, finish_last)
     slots = (m.rqdx, m.rqdy, m.rqxy, m.rqu, m.rqd)
     steps |= scatter_z_last(k, "m", m.qk, in_all, 0, UNITS, UNITS // 2, slots, m.sq_s, m.sq_r, finish_mats)
     slots = (m.rtdx, m.rtdy, m.rtxy, m.rtu, m.rtd)
@@ -1057,55 +1144,75 @@
 
     root = math.sqrt(2.0 / math.pi)
     chunk = UNITS * depth
-    yx_of = (k.me, k.xs, k.ys, k.ds)
-
-    def feed(which):
-        yx = yx_of[which]
-        blocks = pl.ds(yx * depth, depth)
+    ys = (k.y, 1 - k.y)
+
+    def feed(which, who, half=None):
+        blocks = pl.ds(ys[which] * depth, depth)
+        rows = rows_at(who) if half is None else half_at(who, half)
         fc1 = m.ff[blocks, 0:UNITS, :].reshape(chunk, WIDTH)
         fc2 = m.ff[blocks, UNITS : 2 * UNITS, :].reshape(chunk, WIDTH)
-        for r in range(2):
-            rows = pl.ds(r * SEQ, SEQ)
-            pre = dg(m.n2[rows], fc1, 1, 1) + m.bias[yx, 7:8]
-            square = pre * pre
-            tanh = jnp.tanh(root * pre * (1.0 + 0.044715 * square))
-            half = 0.5 * (1.0 + tanh)
-            slope = half + 0.5 * pre * (1.0 - tanh * tanh) * (root * (1.0 + 3 * 0.044715 * square))
-            activated = (pre * half).astype(bf16)
-            grad_pre = (dg(m.ct[rows], fc2, 1, 1) * slope).astype(bf16)
-            m.act[rows] = activated
-            m.dp[rows] = grad_pre
-            if which == 0:
-                m.outp[rows] = dg(activated, fc2, 1, 0)
-                m.dn2[rows] = dg(grad_pre, fc1, 1, 0)
-            else:
-                m.outp[rows] += dg(activated, fc2, 1, 0)
-                m.dn2[rows] += dg(grad_pre, fc1, 1, 0)
-
-    def feed_swap():
-        swap(2, m.dn2.at[sib_rows], m.dn2r)
-        swap(3, m.outp.at[sib_rows], m.outr)
+        pre = dg(m.n2[rows], fc1, 1, 1) + m.bias[ys[which], 7:8]
+        square = pre * pre
+        tanh = jnp.tanh(root * pre * (1.0 + 0.044715 * square))
+        half = 0.5 * (1.0 + tanh)
+        slope = half + 0.5 * pre * (1.0 - tanh * tanh) * (root * (1.0 + 3 * 0.044715 * square))
+        activated = (pre * half).astype(bf16)
+        grad_pre = (dg(m.ct[rows], fc2, 1, 1) * slope).astype(bf16)
+        m.act[which, rows] = activated
+        m.dp[which, rows] = grad_pre
+        if which == 0:
+            m.outp[rows] = dg(activated, fc2, 1, 0)
+            m.dn2[rows] = dg(grad_pre, fc1, 1, 0)
+        else:
+            m.outp[rows] += dg(activated, fc2, 1, 0)
+            m.dn2[rows] += dg(grad_pre, fc1, 1, 0)
+
+    def to_sibling():
+        swap(8, m.dn2.at[rows_at("s")], m.dn2s)
+        swap(9, m.outp.at[rows_at("s")], m.outs)
+
+    def half_rows(half):
+        return pl.ds(half * (SEQ // 2), SEQ // 2)
+
+    def to_diagonal(half):
+        swap(10 + half, m.dn2.at[half_at("d", half)], m.dn2b.at[half_rows(half)])
+
+    def to_x(half):
+        rows = half_rows(half)
+        k.arrive(m.dn2b.at[rows], m.e_r.at[10 + half])
+        m.dn2x[0, rows] = (m.dn2[half_at("x", half)] + m.dn2b[rows]).astype(bf16)
+        swap(13 + half, m.dn2x.at[0, rows], m.dn2x.at[1, rows], k.x_dev)
+
+    def out_to_diagonal():
+        swap(12, m.outp.at[rows_at("d")], m.outb)
+
+    def out_to_x():
+        k.arrive(m.outb, m.e_r.at[12])
+        m.outx[0] = (m.outp[rows_at("x")] + m.outb[...]).astype(bf16)
+        swap(15, m.outx.at[0], m.outx.at[1], k.x_dev)
 
     def feed_grads(which):
-        yx = yx_of[which]
-        blocks = pl.ds(yx * depth, depth)
-        m.gff[blocks, 0:UNITS] = dg(m.dp[...], m.n2[...], 0, 0).astype(bf16).reshape(depth, UNITS, WIDTH)
+        blocks = pl.ds(ys[which] * depth, depth)
+        pre = m.dp[which]
+        m.gff[blocks, 0:UNITS] = dg(pre, m.n2[...], 0, 0).astype(bf16).reshape(depth, UNITS, WIDTH)
         m.gff[blocks, UNITS : 2 * UNITS] = (
-            dg(m.act[...], m.ct[...], 0, 0).astype(bf16).reshape(depth, UNITS, WIDTH)
+            dg(m.act[which], m.ct[...], 0, 0).astype(bf16).reshape(depth, UNITS, WIDTH)
         )
-        sums = jnp.sum(m.dp[...].astype(f32), axis=0, keepdims=True)
+        sums = jnp.sum(pre.astype(f32), axis=0, keepdims=True)
         lane = lax.broadcasted_iota(jnp.int32, (1, 128), 1)
         for zs in range(depth):
             line = (pltpu.roll(sums, chunk - UNITS * zs, 1) if zs else sums)[:, :128]
-            m.gbias[yx * depth + zs] = jnp.broadcast_to(jnp.where(lane < UNITS, line, 0.0), (8, 128))
-
-    def back2():
-        m.gvec[...] = jnp.zeros((16, WIDTH), f32)
-        k.arrive(m.dn2r, m.e_r.at[2])
+            m.gbias[ys[which] * depth + zs] = jnp.broadcast_to(jnp.where(lane < UNITS, line, 0.0), (8, 128))
+
+    def back2(half):
+        if half == 0:
+            m.gvec[...] = jnp.zeros((16, WIDTH), f32)
+            k.arrive(m.dn2s, m.e_r.at[8])
+        k.arrive(m.dn2x.at[1, half_rows(half)], m.e_r.at[13 + half])
 
         def rows_of(start, step):
             rows = pl.ds(start, step)
-            grad_normed = m.dn2[chip_rows(start, step)] + m.dn2r[rows]
+            grad_normed = m.dn2[rows_at("o", start, step)] + m.dn2s[rows] + m.dn2x[1, rows].astype(f32)
             scaled = m.s2[rows]
             grad_in = grad_normed * m.vec[12:13]
             first = jnp.mean(grad_in, axis=1, keepdims=True)
@@ -1120,7 +1227,7 @@
             m.gvec[13:14] += jnp.sum(grad_normed, axis=0, keepdims=True)
             m.gvec[14:15] += jnp.sum(top, axis=0, keepdims=True)
 
-        row_loop(SEQ, 32, rows_of)
+        row_loop(SEQ // 2, 32, rows_of, half * (SEQ // 2))
 
     def grad_mixed():
         m.dmt[...] = (jnp.transpose(dg(m.da[...], m.wo[...], 1, 1)) * valid).astype(bf16)
@@ -1137,21 +1244,13 @@
         grad_queries = (dg(keys, grad_scores, 1, 0) * (1.0 / HEAD_SIZE)).astype(bf16)
         m.dqt[rows] = grad_queries
         grad_keys = dg(queries, grad_scores, 1, 1) * (1.0 / HEAD_SIZE) * valid
-        raw = m.krt[rows]
-        at = lax.broadcasted_iota(jnp.int32, (HEAD_SIZE, 128), 1)
+        m.dk[rows] = grad_keys
         grad_raw = grad_keys * m.vecc[rows, 5:6]
-        sums = jnp.where(at == 5, jnp.sum(grad_keys * raw, axis=1, keepdims=True), 0.0)
         for j in range(1, 4):
             grad_raw = grad_raw + lane_shift(grad_keys, j, True) * m.vecc[rows, 5 + j : 6 + j]
-            tap = jnp.sum(grad_keys * lane_shift(raw, j, False), axis=1, keepdims=True)
-            sums = jnp.where(at == 5 + j, tap, sums)
-        rounded = grad_raw.astype(bf16)
-        m.dkt[rows] = rounded
-        for place, value in ((2, grad_queries), (3, rounded), (4, grad_values)):
-            sums = jnp.where(at == place, jnp.sum(value.astype(f32), axis=1, keepdims=True), sums)
-        m.colsum[rows] = sums
-
-    def pack_rows(part, carry):
+        m.dkt[rows] = grad_raw.astype(bf16)
+
+    def pack_rows(part):
         rows = pl.ds(pl.multiple_of(part * 384, 384), 384)
         normed = m.nmt[rows]
         grads = (
@@ -1163,12 +1262,12 @@
         for place in range(2):
             pair = [grad.reshape(4 * depth, 24, WIDTH) for grad in grads[2 * place : 2 * place + 2]]
             m.qk[pl.ds(part * 4 * depth, 4 * depth), 48 * place : 48 * place + 48, :] = jnp.concatenate(pair, axis=1).astype(bf16)
-        return carry
-
-    def pack():
-        lax.fori_loop(0, 2, pack_rows, 0)
-        for yx in range(4):
-            swap(4, m.qk.at[pl.ds(in_all_sib(yx, 0), depth)], m.sr.at[pl.ds(yx * depth, depth)])
+
+    def pack(which):
+        pack_rows(ys[1 - which])
+        for place in (2 * which, 2 * which + 1):
+            yx = (k.ds, k.ys, k.xs, k.me)[place]
+            swap(16 + place, m.qk.at[pl.ds(in_all_sib(yx, 0), depth)], m.sr.at[pl.ds(yx * depth, depth)])
 
     def grad_normed():
         m.dn[...] = jnp.transpose(
@@ -1189,15 +1288,11 @@
         row_loop(SEQ, 32, rows_of)
         stored("dinp").start()
 
-    def core_sums():
-        k.arrive(m.sr, m.e_r.at[4])
-
-        def block_sum(place, carry):
-            yx, zs = lax.div(place, depth), lax.rem(place, depth)
-            add_into(m.qk.at[in_all(yx, zs)], m.sr.at[place])
-            return carry
-
-        lax.fori_loop(0, 4 * depth, block_sum, 0)
+    def core_sum(place):
+        yx = (k.ds, k.ys, k.xs, k.me)[place]
+        k.arrive(m.sr.at[pl.ds(yx * depth, depth)], m.e_r.at[16 + place])
+        for zs in range(depth):
+            add_into(m.qk.at[in_all(yx, zs)], m.sr.at[yx * depth + zs])
 
     def flip():
         turn = (s_at + t_at == SEQ - 1).astype(bf16)
@@ -1214,8 +1309,15 @@
         part = m.ex[rows] * grad_kernel
         at = lax.broadcasted_iota(jnp.int32, (HEAD_SIZE, 128), 1)
         grad_rate = -m.vecc[rows, 9:10] * jnp.sum(part * day, axis=1, keepdims=True)
-        sums = jnp.where(at == 9, jnp.sum(part, axis=1, keepdims=True), m.colsum[rows])
-        m.colsum[rows] = jnp.where(at == 10, grad_rate, sums)
+        sums = jnp.where(at == 9, jnp.sum(part, axis=1, keepdims=True), 0.0)
+        sums = jnp.where(at == 10, grad_rate, sums)
+        raw, grad_keys = m.krt[rows], m.dk[rows]
+        for j in range(4):
+            tap = jnp.sum(grad_keys * (lane_shift(raw, j, False) if j else raw), axis=1, keepdims=True)
+            sums = jnp.where(at == 5 + j, tap, sums)
+        for place, value in ((2, m.dqt), (3, m.dkt), (4, m.dvt)):
+            sums = jnp.where(at == place, jnp.sum(value[rows].astype(f32), axis=1, keepdims=True), sums)
+        m.colsum[rows] = sums
 
     def vector_tiles():
         grads = m.gvec[...] + jnp.transpose(m.colsum[...])[0:16]
@@ -1226,14 +1328,14 @@
             for zs in range(depth):
                 tile = pltpu.roll(turned, 128 - 24 * zs, 1) if zs else turned
                 tile = jnp.where((lane_at < 24) & (row_at < 15), tile, 0.0)
-                own = jnp.concatenate([jnp.zeros((8, 128), f32), m.gbias[(wide // 2) * depth + zs]], axis=0)
-                mine = (row_at == 15) & (core == wide % 2)
+                own = jnp.concatenate([jnp.zeros((8, 128), f32), m.gbias[(wide // 4) * depth + zs]], axis=0)
+                mine = (row_at == 15) & (core == wide % 2) & (k.x == wide // 2 % 2)
                 m.gs[wide * depth + zs] = jnp.where(mine, own, tile)
         for yx in range(4):
-            swap(5, m.gs.at[pl.ds(in_all_sib(yx, 0), depth)], m.srs.at[pl.ds(yx * depth, depth)])
+            swap(20, m.gs.at[pl.ds(in_all_sib(yx, 0), depth)], m.srs.at[pl.ds(yx * depth, depth)])
 
     def small_sums():
-        k.arrive(m.srs, m.e_r.at[5])
+        k.arrive(m.srs, m.e_r.at[20])
         for yx in range(4):
             for zs in range(depth):
                 add_into(m.gs.at[in_all(yx, zs)], m.srs.at[yx * depth + zs])
@@ -1241,9 +1343,11 @@
     def finish_out():
         def rows_of(start, step):
             rows = pl.ds(start, step)
-            m.out[rows] = (m.hid[rows] + (m.outp[chip_rows(start, step)] + m.outr[rows]) + m.vec[14:15]).astype(bf16)
-
-        k.arrive(m.outr, m.e_r.at[3])
+            others = m.outs[rows] + m.outx[1, rows].astype(f32)
+            m.out[rows] = (m.hid[rows] + (m.outp[rows_at("o", start, step)] + others) + m.vec[14:15]).astype(bf16)
+
+        k.arrive(m.outs, m.e_r.at[9])
+        k.arrive(m.outx.at[1], m.e_r.at[15])
         row_loop(SEQ, 32, rows_of)
         stored("out").start()
 
@@ -1252,24 +1356,41 @@
             stored(name).start()
         for group in "SFLflms":
             next(steps[group + "."])
-        for place, extent in enumerate((m.ct.at[core_rows], m.n2.at[core_rows], m.dn2r, m.outr, m.sr, m.srs)):
+        own, half = m.ct.at[rows_at("o")], m.ct.at[half_at("o", 0)]
+        half_f32, own_f32, blocks = m.outb.at[half_rows(0)], m.outb, m.sr.at[pl.ds(0, depth)]
+        extents = [own] * 4 + [half] * 4 + [own_f32] * 2 + [half_f32] * 2 + [own_f32] + [half] * 2 + [own] + [blocks] * 4
+        extents.append(m.srs)
+        for place, extent in enumerate(extents):
             k.left(extent, m.e_s.at[place])
         for name in RESULTS:
             stored(name).wait()
 
     compute = {
-        "own_blocks": own_blocks, "barrier": k.barrier, "own_cotangent": own_cotangent, "norm1": norm1,
+        "own_blocks": own_blocks, "barrier": k.barrier, "own_cotangent": own_cotangent, "norm1": norm1, "pass_ct": pass_ct,
         "vectors": vectors, "mixer_kernels": mixer_kernels, "gain1": gain1, "unpack": unpack, "project": project,
-        "hidden": hidden, "norm2": norm2, "sibling_rows": sibling_rows, "feed_swap": feed_swap, "store": store,
-        "back2": back2, "grad_mixed": grad_mixed, "pack": pack, "grad_normed": grad_normed, "back1": back1,
-        "core_sums": core_sums, "flip": flip, "vector_tiles": vector_tiles, "small_sums": small_sums, "finish_out": finish_out,
+        "hidden": hidden, "norm2": norm2, "sibling_rows": sibling_rows, "to_sibling": to_sibling,
+        "out_to_diagonal": out_to_diagonal, "out_to_x": out_to_x, "grad_mixed": grad_mixed, "grad_normed": grad_normed,
+        "back1": back1, "flip": flip, "vector_tiles": vector_tiles, "small_sums": small_sums, "finish_out": finish_out,
+        "store": store,
     }
+    for which in range(2):
+        for who in "os":
+            compute["feed%d%s" % (which, who)] = partial(feed, which, who)
+        for who in "xd":
+            for half in range(2):
+                compute["feed%d%s%d" % (which, who, half)] = partial(feed, which, who, half)
+        compute["feed_grads%d" % which] = partial(feed_grads, which)
+        compute["pass_n2_%d" % which] = partial(pass_n2, which)
+        compute["diagonal_rows%d" % which] = partial(diagonal_rows, which)
+        compute["to_diagonal%d" % which] = partial(to_diagonal, which)
+        compute["to_x%d" % which] = partial(to_x, which)
+        compute["back2_%d" % which] = partial(back2, which)
+        compute["pack%d" % which] = partial(pack, which)
     for which in range(4):
-        compute["feed%d" % which] = partial(feed, which)
-        compute["feed_grads%d" % which] = partial(feed_grads, which)
         compute["mix%d" % which] = partial(three_heads, 3 * which, mix_head)
         compute["back%d" % (4 + which)] = partial(three_heads, 3 * which, back_head)
         compute["kernel%d" % which] = partial(three_heads, 3 * which, kernel_head)
+        compute["core_sum%d" % which] = partial(core_sum, which)
     for step in PLAN:
         if step in compute:
             compute[step]()

time: 129 us -> 116 us (0.90)
  Pallas kernels: 125 us -> 113 us
    pallas_call x1, Pallas kernels: 122 us -> 111 us  [on_device_fast(): pl.pallas_call(partial(layer_kernel, depth), out_shape=[shape((SEQ, WIDTH...]
where the time goes in v4:
time: 116 us; the launch traced here: 115 us
  Pallas kernels  113 us (97%)
  between operations  1.42 us (1%)
    pallas_call x1, Pallas kernels, on_device_fast(): pl.pallas_call(partial(layer_kernel, depth), out_shape=[shape((SEQ, WIDTH...  111 us
    pallas_call x1, Pallas kernels, on_device_fast(): pl.pallas_call(results_kernel, out_shape=[shape(x.shape, x.dtype) for x i...  2.62 us

profile of v4, /device:TPU:0, one launch (start us, length us, event | category | flops | bytes accessed | tf_op | source)
XLA Modules:
  0.0 114.5 jit_solution(894356845826653892)
XLA Ops:
  1.3 110.5 %h3_layer.1 = (bf16[256,768]{1,0:T(8,128)(2,1)}, bf16[256,768]{1,0:T(8,128)(2,1)}, f32[24,768]{1,0:T(8,128)}, f32[24,768]{1,0:T(8,128)}, f32[24,768]{1,0:T(8,128...) custom-call(bf16[256,768]{1,0:T(8,128)(2,1)} %refs_0_.1, ...), custom_call_target="tpu_custom_call" | custom-call | tf_op jit(solution)/shard_map/h3_layer/pallas_call | solution.py:1420
  111.8 2.6 %results.1 = (bf16[256,768]{1,0:T(8,128)(2,1)}, bf16[256,768]{1,0:T(8,128)(2,1)}, f32[24,768]{1,0:T(8,128)}, f32[24,768]{1,0:T(8,128)}, f32[24,768]{1,0:T(8,128)...) custom-call(bf16[256,768]{1,0:T(8,128)(2,1)} %get-tuple-element.29.refs, ...), custom_call_target="tpu_custom_call" | custom-call | tf_op jit(solution)/shard_map/results/pallas_call | solution.py:1436

commit v5 on v4

--- a/solution.py
+++ b/solution.py
@@ -381,36 +381,42 @@
         pl.when(jnp.logical_not(self.at_end))(lambda: self.left(extent(self.depth + 1), semaphore))
 
 
+def halved(ref, piece):
+    rows, lanes = ref.shape[-2:]
+    if lanes == 128:
+        return ref.at[pl.ds(piece * (rows // 2), rows // 2)]
+    return ref.at[:, pl.ds(piece * (lanes // 2), lanes // 2)]
+
+
 def near(k, distance):
     if distance == 0:
         return ((None, k.z, False),)
     return ((k.z >= distance, k.z - distance, True), (k.z + distance < k.depth, k.z + distance, False))
 
 
-def gather_z_first(k, name, buf, index, low, rows, half, ss, rs, sib_index=None):
+def gather_z_first(k, name, buf, index, low, rows, ss, rs):
     depth = k.depth
 
-    def block(yx, zs, lo=0, n=rows):
-        return buf.at[index(yx, zs), pl.ds(low + lo, n)]
-
-    def send(condition, yx, zs, lo, n, device, r, way=0):
-        ref = lambda: block(yx, zs, lo, n)
+    def block(yx, zs):
+        return buf.at[index(yx, zs), pl.ds(low, rows)]
+
+    def send(condition, yx, zs, device, r, way=0, piece=None):
+        ref = lambda: block(yx, zs) if piece is None else halved(block(yx, zs), piece)
         k.start(condition, ref, ref, ss.at[way], rs.at[r], device)
 
     def to_sib(condition, yx, zs):
-        if sib_index is not None:
-            send(condition, yx, zs, 0, rows, k.sib_dev, 4 * depth)
+        send(condition, yx, zs, k.sib_dev, 4 * depth)
 
     def outward(condition, zs):
-        send(condition, k.me, zs, 0, rows, k.x_dev, depth + zs)
-        send(condition, k.me, zs, 0, rows, k.y_dev, 2 * depth + zs)
+        send(condition, k.me, zs, k.x_dev, depth + zs)
+        send(condition, k.me, zs, k.y_dev, 2 * depth + zs)
         to_sib(condition, k.me, zs)
 
     def along(condition, zs, up, down):
         if up:
-            send(both(condition, k.has_up), k.me, zs, 0, rows, k.up_dev, zs, 1)
+            send(both(condition, k.has_up), k.me, zs, k.up_dev, zs, 1)
         if down:
-            send(both(condition, k.has_down), k.me, zs, 0, rows, k.down_dev, zs, 1)
+            send(both(condition, k.has_down), k.me, zs, k.down_dev, zs, 1)
 
     def take(condition, yx, zs, r):
         when(condition, lambda: k.arrive(block(yx, zs), rs.at[r]))
@@ -432,7 +438,7 @@
         for d in range(depth):
             for condition, zs, _ in near(k, d):
                 take(condition, k.xs, zs, depth + zs)
-                send(condition, k.xs, zs, 0, half, k.y_dev, 3 * depth + zs)
+                send(condition, k.xs, zs, k.y_dev, 3 * depth + zs, piece=0)
                 to_sib(condition, k.xs, zs)
             yield
 
@@ -440,7 +446,7 @@
         for d in range(depth):
             for condition, zs, _ in near(k, d):
                 take(condition, k.ys, zs, 2 * depth + zs)
-                send(condition, k.ys, zs, half, rows - half, k.x_dev, 3 * depth + zs)
+                send(condition, k.ys, zs, k.x_dev, 3 * depth + zs, piece=1)
                 to_sib(condition, k.ys, zs)
             yield
 
@@ -459,7 +465,7 @@
         yield
 
     def left():
-        k.left(extent((7 if sib_index is not None else 3) * depth), ss.at[0])
+        k.left(extent(7 * depth), ss.at[0])
         k.left_along(extent, ss.at[1])
         yield
 
@@ -590,52 +596,54 @@
         send(k.z == low, True)
 
 
-def scatter_z_last(k, name, buf, index, low, rows, half, slots, ss, rs, finish):
+def scatter_z_last(k, name, buf, index, low, rows, slots, ss, rs, finish):
     depth = k.depth
     from_x_diag, from_y_diag, from_xy, from_up, from_down = slots
     order = scatter_order(depth)
-    rest = rows - half
-
-    def block(yx, zd, lo=0, n=rows):
-        return buf.at[index(yx, zd), pl.ds(low + lo, n)]
+
+    def block(yx, zd):
+        return buf.at[index(yx, zd), pl.ds(low, rows)]
+
+    def half(yx, zd, piece):
+        return halved(block(yx, zd), piece)
 
     def send(condition, source, target, device, r):
         k.start(condition, source, target, ss.at[0], rs.at[r], device)
 
-    def x_part(zd, lo, n):
-        return from_xy.at[zd, 0, pl.ds(lo, n)]
-
-    def y_part(zd, lo, n):
-        return from_xy.at[zd, 1, pl.ds(lo, n)]
+    def x_part(zd, piece):
+        return halved(from_xy.at[zd, 0], piece)
+
+    def y_part(zd, piece):
+        return halved(from_xy.at[zd, 1], piece)
 
     def pure_x():
         for zd in order:
-            send(None, lambda zd=zd: block(k.xs, zd, half, rest), lambda zd=zd: x_part(zd, half, rest), k.x_dev, 2 * depth + zd)
+            send(None, lambda zd=zd: half(k.xs, zd, 1), lambda zd=zd: x_part(zd, 1), k.x_dev, 2 * depth + zd)
             yield
 
     def pure_y():
         for zd in order:
-            send(None, lambda zd=zd: block(k.ys, zd, 0, half), lambda zd=zd: y_part(zd, 0, half), k.y_dev, 2 * depth + zd)
+            send(None, lambda zd=zd: half(k.ys, zd, 0), lambda zd=zd: y_part(zd, 0), k.y_dev, 2 * depth + zd)
             yield
 
     def diagonal():
         for zd in order:
-            send(None, lambda zd=zd: block(k.ds, zd, 0, half), lambda zd=zd: from_y_diag.at[zd], k.y_dev, zd)
-            send(None, lambda zd=zd: block(k.ds, zd, half, rest), lambda zd=zd: from_x_diag.at[zd], k.x_dev, depth + zd)
+            send(None, lambda zd=zd: half(k.ds, zd, 0), lambda zd=zd: from_y_diag.at[zd], k.y_dev, zd)
+            send(None, lambda zd=zd: half(k.ds, zd, 1), lambda zd=zd: from_x_diag.at[zd], k.x_dev, depth + zd)
             yield
 
     def y_added():
         for zd in order:
             k.arrive(from_y_diag.at[zd], rs.at[zd])
-            add_into(block(k.xs, zd, 0, half), from_y_diag.at[zd])
-            send(None, lambda zd=zd: block(k.xs, zd, 0, half), lambda zd=zd: x_part(zd, 0, half), k.x_dev, 2 * depth + zd)
+            add_into(half(k.xs, zd, 0), from_y_diag.at[zd])
+            send(None, lambda zd=zd: half(k.xs, zd, 0), lambda zd=zd: x_part(zd, 0), k.x_dev, 2 * depth + zd)
             yield
 
     def x_added():
         for zd in order:
             k.arrive(from_x_diag.at[zd], rs.at[depth + zd])
-            add_into(block(k.ys, zd, half, rest), from_x_diag.at[zd])
-            send(None, lambda zd=zd: block(k.ys, zd, half, rest), lambda zd=zd: y_part(zd, half, rest), k.y_dev, 2 * depth + zd)
+            add_into(half(k.ys, zd, 1), from_x_diag.at[zd])
+            send(None, lambda zd=zd: half(k.ys, zd, 1), lambda zd=zd: y_part(zd, 1), k.y_dev, 2 * depth + zd)
             yield
 
     def wave(zd, number):
@@ -812,6 +820,7 @@
 
 SEQ, WIDTH, UNITS = 256, 768, 96
 HEADS = WIDTH // HEAD_SIZE
+FIRST = 112
 
 
 def row_loop(total, step, body, first=0):
@@ -828,6 +837,11 @@
     if left:
         return jnp.where(lane < extent - offset, pltpu.roll(values, extent - offset, 1), 0.0)
     return jnp.where(lane >= offset, pltpu.roll(values, offset, 1), 0.0)
+
+
+def six_heads(first, body):
+    for h in range(first, first + 6):
+        body(h)
 
 
 def three_heads(first, body):
@@ -878,6 +892,7 @@
         "qt": ((WIDTH, SEQ), bf16),
         "kt": ((WIDTH, SEQ), bf16),
         "vt": ((WIDTH, SEQ), bf16),
+        "wt": ((HEADS, SEQ, SEQ), bf16),
         "krt": ((WIDTH, SEQ), f32),
         "mt": ((WIDTH, SEQ), bf16),
         "dmt": ((WIDTH, SEQ), bf16),
@@ -895,48 +910,47 @@
         "bias": ((2, 8, UNITS * depth), f32),
         "gbias": ((half, 8, 128), f32),
     }
-    for name, rows, lanes, kind in (("q", UNITS, WIDTH, bf16), ("t", 16, 128, f32)):
-        table["r" + name + "dx"] = table["r" + name + "dy"] = ((depth, rows // 2, lanes), kind)
+    for name, rows, lanes, kind in (("q", 48, WIDTH, bf16), ("v", 48, WIDTH, bf16), ("t", 16, 128, f32)):
+        part = (rows, lanes // 2) if lanes == WIDTH else (rows // 2, lanes)
+        table["r" + name + "dx"] = table["r" + name + "dy"] = ((depth,) + part, kind)
         table["r" + name + "xy"] = ((depth, 2, rows, lanes), kind)
         table["r" + name + "u"] = table["r" + name + "d"] = ((depth, rows, lanes), kind)
-    table["rby"] = table["rbu"] = table["rbd"] = ((depth, 128, WIDTH), bf16)
-    table["rcy"] = ((1, 64, WIDTH), bf16)
-    table["rcu"] = table["rcd"] = ((half, 64, WIDTH), bf16)
-    table["out"] = table["dinp"] = ((SEQ, WIDTH), bf16)
-    for name in ("gwq", "gwk", "gwv", "gwo"):
-        table[name] = ((24, WIDTH), f32)
-    table["gfc1"] = table["gfc2"] = ((UNITS, WIDTH), f32)
-    table["gsmall"] = ((16, 128), f32)
-    table["store"] = len(RESULTS)
+    table["rby"] = table["rbu"] = table["rbd"] = ((depth, FIRST, WIDTH), bf16)
+    table["rcy"] = ((1, 2 * UNITS - FIRST, WIDTH), bf16)
+    table["rcu"] = table["rcd"] = ((half, 2 * UNITS - FIRST, WIDTH), bf16)
     for name, sent, came in (
-        ("gq", 2, 4 * depth + 1), ("gb", 2, 2 * depth), ("gt", 2, 4 * depth + 1), ("gc", 3, 2 * depth + 1),
-        ("sq", 1, 5 * depth), ("sb", 1, 3 * depth), ("st", 1, 5 * depth), ("sc", 1, 4 * depth + 1), ("e", 21, 21),
+        ("gq", 2, 4 * depth + 1), ("gv", 2, 4 * depth + 1), ("gb", 2, 2 * depth), ("gt", 2, 4 * depth + 1), ("gc", 3, 2 * depth + 1),
+        ("sq", 1, 5 * depth), ("sv", 1, 5 * depth), ("sb", 1, 3 * depth), ("st", 1, 5 * depth), ("sc", 1, 4 * depth + 1), ("e", 3, 25),
     ):
         table[name + "_s"], table[name + "_r"] = sent, came
     return table
 
 
 PLAN = (
-    "own_blocks", "barrier", "S0", "M0", "Sx", "Sz", "L0", "Sy", "Sy", "Sz", "Sx", "Mz", "Sx", "Sd", "Sz",
-    "My", "Sx", "Mx", "Sy", "Mz", "norm1", "Sy", "Sd", "Mz", "L4", "My", "Mx", "Mx", "Mx", "F0", "Ly", "My",
-    "Sd", "Sd", "Ss", "vectors", "My", "own_cotangent", "mixer_kernels", "gain1", "Md", "Md", "Fz", "Md",
-    "Md", "L4", "Ms", "unpack", "project", "mix0", "mix1", "mix2", "Fz", "mix3", "hidden", "norm2", "Fz",
-    "Fy", "M.", "sibling_rows", "L5", "pass_ct", "L4", "feed0o", "pass_n2_0", "feed0x0", "Fy", "L5",
-    "diagonal_rows0", "feed0s", "feed0d0", "pass_n2_1", "L5", "feed0x1", "Fy", "diagonal_rows1", "feed0d1",
-    "Fy", "feed1d0", "to_diagonal0", "feed1x0", "feed1x1", "feed1s", "to_x0", "feed1o", "feed1d1",
-    "feed_grads1", "fY", "flip", "to_diagonal1", "l1", "fY", "fY", "fY", "feed_grads0", "out_to_diagonal",
-    "to_sibling", "l0", "to_x1", "out_to_x", "back2_0", "back2_1", "grad_mixed", "back4", "back5", "back6",
-    "fc", "back7", "pack0", "pack1", "fc", "fc", "core_sum0", "l0", "mD", "grad_normed", "finish_out",
-    "core_sum1", "mD", "mb", "mY", "back1", "core_sum2", "l1", "mX", "fv", "kernel0", "core_sum3", "l1",
-    "ma", "l0", "fc", "kernel3", "fv", "fv", "ma", "mb", "mY", "mX", "kernel1", "mD", "kernel2", "fv", "mc",
-    "vector_tiles", "small_sums", "fw", "sD", "sX", "mY", "sD", "mb", "mX", "mD", "mc", "sY", "mv", "mv",
-    "sa", "sa", "ma", "fw", "sb", "sY", "mb", "sX", "sb", "mY", "sD", "mX", "mw", "mc", "sc", "sY", "lO",
-    "sb", "ma", "mw", "sX", "sc", "sD", "fe", "lY", "sX", "sv", "sY", "sv", "mv", "mc", "sa", "sa", "sc",
-    "sb", "sw", "sw", "le", "mv", "sv", "sc", "me", "sv", "se", "store",
+    "own_blocks", "barrier", "S0", "Q0", "V0", "Sz", "Qy", "L0", "Sz", "Qx", "Sx", "Sy", "Qz", "Sy", "Vz",
+    "Qz", "Sx", "Vy", "Sz", "Qx", "Qz", "Sx", "Ly", "Vz", "Qy", "Sy", "L4", "Qx", "Sx", "Vx", "Qy", "Qx",
+    "Sy", "Sd", "Qd", "Qy", "Vz", "Vy", "Vx", "Vx", "F0", "Sd", "Qd", "Sd", "norm1", "Sd", "Ss", "vectors",
+    "Qd", "gain1", "Vy", "Qd", "L4", "Vy", "Vd", "own_cotangent", "Qs", "Vx", "unpack0", "project_qk", "Fz",
+    "mixer_kernels", "Vd", "score0", "Vd", "score1", "score2", "Vd", "Fy", "score3", "Fz", "Vs", "unpack1",
+    "project_v", "L5", "mix0", "mix1", "hidden", "norm2", "L4", "Fz", "feed0o", "sibling_rows", "feed0s",
+    "pass_ct", "L5", "flip", "Fy", "pass_n2_0", "Q.", "feed0x0", "diagonal_rows0", "Fy", "feed0d0", "L5",
+    "Fy", "feed1d0", "to_diagonal0", "feed1o", "V.", "feed1x0", "pass_n2_1", "feed1s", "to_x0", "feed0x1",
+    "diagonal_rows1", "feed0d1", "feed1d1", "to_diagonal1", "feed1x1", "feed_grads1", "fY", "l1",
+    "out_to_diagonal", "to_x1", "to_sibling", "feed_grads0", "out_to_x", "fY", "back2_0", "fc", "fY", "l0",
+    "back2_1", "grad_mixed", "back_v0", "back_v1", "pack_vo0", "back4", "sum_vo0", "pack_vo1", "sum_vo1",
+    "vD", "fY", "back5", "sum_vo2", "back6", "l1", "back7", "va", "fc", "vX", "vD", "pack_qk0", "vD",
+    "grad_normed", "sum_qk0", "qD", "fv", "back1", "l1", "qD", "l0", "sum_qk1", "fc", "vX", "pack_qk1", "vX",
+    "qY", "vY", "kernel3", "sum_qk2", "sum_vo3", "qb", "vY", "qX", "qD", "qa", "vb", "qb", "qa", "va", "fc",
+    "vb", "kernel0", "sum_qk3", "fv", "vX", "qY", "va", "kernel1", "vD", "fw", "l0", "vb", "qX", "vY", "fv",
+    "kernel2", "qc", "vector_tiles", "vc", "fv", "vc", "qa", "small_sums", "sD", "fw", "sX", "sD", "qb",
+    "qX", "sY", "qv", "sD", "sY", "qc", "sX", "qD", "sb", "sa", "vc", "vv", "sa", "sb", "qY", "vb", "vY",
+    "vv", "va", "sc", "qb", "qa", "sc", "qY", "qv", "qc", "sv", "sD", "qX", "sY", "qw", "vv", "vw", "vw",
+    "sv", "qv", "sX", "vc", "sY", "sw", "fe", "sb", "sb", "lY", "sa", "qw", "sX", "qc", "finish_out", "lO",
+    "sa", "vv", "sw", "qv", "sc", "sv", "sc", "ve", "le", "sv", "qe", "se", "store",
 )
 INPUTS = ("tok", "length", "cot", "iq", "ik", "iv", "io", "ifc1", "ifc2", "ibias", "ivec")
 RESULTS = ("out", "dinp", "gwq", "gwk", "gwv", "gwo", "gfc1", "gfc2", "gsmall")
-OUTPUTS = tuple("to_" + name for name in RESULTS)
+OUTPUTS = RESULTS
 
 
 def layer_kernel(depth, *refs):
@@ -959,12 +973,11 @@
     def rows_at(who, start=0, step=SEQ):
         return pl.ds(pl.multiple_of(places[who] * SEQ + start, step), step)
 
-    def stored(name):
-        place = RESULTS.index(name)
-        return pltpu.make_async_copy(getattr(m, name), getattr(m, "to_" + name), m.store.at[place])
+    def sent_by(place):
+        return 2 if place == 24 else 1 if place in (9, 10, 11, 12) or place >= 16 else 0
 
     def swap(place, source, target, device=None):
-        k.start(None, lambda: source, lambda: target, m.e_s.at[place], m.e_r.at[place], device or k.sib_dev)
+        k.start(None, lambda: source, lambda: target, m.e_s.at[sent_by(place)], m.e_r.at[place], device or k.sib_dev)
 
     day = lax.broadcasted_iota(jnp.int32, (1, SEQ), 1).astype(f32)
     s_at = lax.broadcasted_iota(jnp.int32, (SEQ, SEQ), 0)
@@ -1046,23 +1059,26 @@
         row_loop(SEQ, 32, rows_of)
         m.nmt[...] = jnp.transpose(m.nm[...])
 
-    def unpack_rows(w, carry):
-        rows = pl.ds(pl.multiple_of(w * 96, 96), 96)
-        for place, (first, second) in enumerate(((m.wq, m.wk), (m.wv, m.wo))):
+    def unpack(place):
+        first, second = ((m.wq, m.wk), (m.wv, m.wo))[place]
+
+        def rows_of(w, carry):
+            rows = pl.ds(pl.multiple_of(w * 96, 96), 96)
             pair = m.qk[pl.ds(w * depth, depth), 48 * place : 48 * place + 48, :].astype(f32)
             first[rows] = pair[:, :24].reshape(96, WIDTH).astype(bf16)
             second[rows] = pair[:, 24:].reshape(96, WIDTH).astype(bf16)
-        return carry
-
-    def unpack():
-        lax.fori_loop(0, 8, unpack_rows, 0)
-
-    def project():
+            return carry
+
+        lax.fori_loop(0, 8, rows_of, 0)
+
+    def project_qk():
         m.qt[...] = jnp.transpose(dg(m.nm[...], m.wq[...], 1, 0) + m.vec[2:3]).astype(bf16)
         m.krt[...] = jnp.transpose(dg(m.nm[...], m.wk[...], 1, 0) + m.vec[3:4])
+
+    def project_v():
         m.vt[...] = (jnp.transpose(dg(m.nm[...], m.wv[...], 1, 0) + m.vec[4:5]) * valid).astype(bf16)
 
-    def mix_head(h):
+    def score_head(h):
         rows = head_rows(h)
         raw = m.krt[rows]
         summed = raw * m.vecc[rows, 5:6]
@@ -1071,8 +1087,11 @@
         keys = (summed * valid).astype(bf16)
         m.kt[rows] = keys
         scores = dg(keys, m.qt[rows], 0, 0) * (1.0 / HEAD_SIZE)
-        weights = (scores * m.tt[h]).astype(bf16)
-        m.mt[rows] = (dg(m.vt[rows], weights, 1, 0) * valid).astype(bf16)
+        m.wt[h] = (scores * m.tt[h]).astype(bf16)
+
+    def mix_head(h):
+        rows = head_rows(h)
+        m.mt[rows] = (dg(m.vt[rows], m.wt[h], 1, 0) * valid).astype(bf16)
 
     def hidden():
         m.hid[...] = dg(m.mt[...], m.wo[...], 0, 0)
@@ -1110,37 +1129,39 @@
             k.arrive(m.ct.at[rows_at("d")], m.e_r.at[2])
         k.arrive(m.n2.at[half_at("d", half)], m.e_r.at[6 + half])
 
-    def finish_feed(ref, more):
-        value = ref[...].astype(f32)
-        for target, low, high in ((m.gfc1, 0, UNITS), (m.gfc2.at[0:32], UNITS, 128)):
-            target[...] = target[...] + value[low:high] if more else value[low:high]
-
-    def finish_last(ref, more):
-        value = ref[...].astype(f32)
-        m.gfc2[32:96] = m.gfc2[32:96] + value if more else value
-
-    def finish_mats(ref, more):
-        value = ref[...].astype(f32)
-        for place, target in enumerate((m.gwq, m.gwk, m.gwv, m.gwo)):
-            part = value[24 * place : 24 * place + 24]
-            target[...] = target[...] + part if more else part
+    def finish_rows(pieces):
+        def finish(ref, more):
+            value = ref[...].astype(f32)
+            for target, (low, high), (first, last) in pieces:
+                part = value[first:last]
+                target[low:high] = target[low:high] + part if more else part
+
+        return finish
+
+    finish_feed = finish_rows(((m.gfc1, (0, UNITS), (0, UNITS)), (m.gfc2, (0, FIRST - UNITS), (UNITS, FIRST))))
+    finish_last = finish_rows(((m.gfc2, (FIRST - UNITS, UNITS), (0, 2 * UNITS - FIRST)),))
+    finish_qk = finish_rows(((m.gwq, (0, 24), (0, 24)), (m.gwk, (0, 24), (24, 48))))
+    finish_vo = finish_rows(((m.gwv, (0, 24), (0, 24)), (m.gwo, (0, 24), (24, 48))))
 
     def finish_small(ref, more):
         m.gsmall[...] = m.gsmall[...] + ref[...] if more else ref[...]
 
     steps = {}
-    steps |= gather_z_first(k, "S", m.sm, in_all, 0, 16, 8, m.gt_s, m.gt_r, in_all_sib)
-    steps |= gather_z_first(k, "M", m.qk, in_all, 0, UNITS, UNITS // 2, m.gq_s, m.gq_r, in_all_sib)
-    steps |= gather_pair_z_first(k, "F", m.ff, in_pair, 0, 128, m.gb_s, m.gb_r)
-    steps |= gather_pair_z_last(k, "L", m.ff, in_pair, 128, 64, m.gc_s, m.gc_r)
+    steps |= gather_z_first(k, "S", m.sm, in_all, 0, 16, m.gt_s, m.gt_r)
+    steps |= gather_z_first(k, "Q", m.qk, in_all, 0, 48, m.gq_s, m.gq_r)
+    steps |= gather_z_first(k, "V", m.qk, in_all, 48, 48, m.gv_s, m.gv_r)
+    steps |= gather_pair_z_first(k, "F", m.ff, in_pair, 0, FIRST, m.gb_s, m.gb_r)
+    steps |= gather_pair_z_last(k, "L", m.ff, in_pair, FIRST, 2 * UNITS - FIRST, m.gc_s, m.gc_r)
     slots = (m.rby, m.rbu, m.rbd)
-    steps |= scatter_pair_z_last(k, "f", m.gff, in_pair, 0, 128, slots, m.sb_s, m.sb_r, finish_feed)
+    steps |= scatter_pair_z_last(k, "f", m.gff, in_pair, 0, FIRST, slots, m.sb_s, m.sb_r, finish_feed)
     slots = (m.rcy, m.rcu, m.rcd)
-    steps |= scatter_pair_z_first(k, "l", m.gff, in_pair, 128, 64, slots, m.sc_s, m.sc_r, finish_last)
+    steps |= scatter_pair_z_first(k, "l", m.gff, in_pair, FIRST, 2 * UNITS - FIRST, slots, m.sc_s, m.sc_r, finish_last)
     slots = (m.rqdx, m.rqdy, m.rqxy, m.rqu, m.rqd)
-    steps |= scatter_z_last(k, "m", m.qk, in_all, 0, UNITS, UNITS // 2, slots, m.sq_s, m.sq_r, finish_mats)
+    steps |= scatter_z_last(k, "q", m.qk, in_all, 0, 48, slots, m.sq_s, m.sq_r, finish_qk)
+    slots = (m.rvdx, m.rvdy, m.rvxy, m.rvu, m.rvd)
+    steps |= scatter_z_last(k, "v", m.qk, in_all, 48, 48, slots, m.sv_s, m.sv_r, finish_vo)
     slots = (m.rtdx, m.rtdy, m.rtxy, m.rtu, m.rtd)
-    steps |= scatter_z_last(k, "s", m.gs, in_all, 0, 16, 8, slots, m.st_s, m.st_r, finish_small)
+    steps |= scatter_z_last(k, "s", m.gs, in_all, 0, 16, slots, m.st_s, m.st_r, finish_small)
 
     root = math.sqrt(2.0 / math.pi)
     chunk = UNITS * depth
@@ -1232,42 +1253,35 @@
     def grad_mixed():
         m.dmt[...] = (jnp.transpose(dg(m.da[...], m.wo[...], 1, 1)) * valid).astype(bf16)
 
+    def back_v_head(h):
+        rows = head_rows(h)
+        m.dvt[rows] = (dg(m.dmt[rows], m.wt[h], 1, 1) * valid).astype(bf16)
+
     def back_head(h):
         rows = head_rows(h)
-        queries, keys, grad_mixed, kernel = m.qt[rows], m.kt[rows], m.dmt[rows], m.tt[h]
-        scores = dg(keys, queries, 0, 0) * (1.0 / HEAD_SIZE)
-        weights = (scores * kernel).astype(bf16)
-        grad_weights = dg(m.vt[rows], grad_mixed, 0, 0)
-        grad_values = (dg(grad_mixed, weights, 1, 1) * valid).astype(bf16)
-        m.dvt[rows] = grad_values
-        grad_scores = (grad_weights * kernel).astype(bf16)
-        grad_queries = (dg(keys, grad_scores, 1, 0) * (1.0 / HEAD_SIZE)).astype(bf16)
-        m.dqt[rows] = grad_queries
-        grad_keys = dg(queries, grad_scores, 1, 1) * (1.0 / HEAD_SIZE) * valid
+        grad_scores = (dg(m.vt[rows], m.dmt[rows], 0, 0) * m.tt[h]).astype(bf16)
+        m.dqt[rows] = (dg(m.kt[rows], grad_scores, 1, 0) * (1.0 / HEAD_SIZE)).astype(bf16)
+        grad_keys = dg(m.qt[rows], grad_scores, 1, 1) * (1.0 / HEAD_SIZE) * valid
         m.dk[rows] = grad_keys
         grad_raw = grad_keys * m.vecc[rows, 5:6]
         for j in range(1, 4):
             grad_raw = grad_raw + lane_shift(grad_keys, j, True) * m.vecc[rows, 5 + j : 6 + j]
         m.dkt[rows] = grad_raw.astype(bf16)
 
-    def pack_rows(part):
-        rows = pl.ds(pl.multiple_of(part * 384, 384), 384)
-        normed = m.nmt[rows]
-        grads = (
-            dg(normed, m.dqt[...], 1, 1),
-            dg(normed, m.dkt[...], 1, 1),
-            dg(normed, m.dvt[...], 1, 1),
-            dg(m.mt[rows], m.da[...], 1, 0),
-        )
-        for place in range(2):
-            pair = [grad.reshape(4 * depth, 24, WIDTH) for grad in grads[2 * place : 2 * place + 2]]
-            m.qk[pl.ds(part * 4 * depth, 4 * depth), 48 * place : 48 * place + 48, :] = jnp.concatenate(pair, axis=1).astype(bf16)
-
-    def pack(which):
-        pack_rows(ys[1 - which])
+    def pack(pair, which):
+        y = ys[1 - which]
+        rows = pl.ds(pl.multiple_of(y * 384, 384), 384)
+        if pair == 0:
+            grads = (dg(m.nmt[rows], m.dqt[...], 1, 1), dg(m.nmt[rows], m.dkt[...], 1, 1))
+        else:
+            grads = (dg(m.nmt[rows], m.dvt[...], 1, 1), dg(m.mt[rows], m.da[...], 1, 0))
+        both_grads = jnp.concatenate([grad.reshape(4 * depth, 24, WIDTH) for grad in grads], axis=1)
+        low = pl.ds(48 * pair, 48)
+        m.qk[pl.ds(y * 4 * depth, 4 * depth), low, :] = both_grads.astype(bf16)
         for place in (2 * which, 2 * which + 1):
             yx = (k.ds, k.ys, k.xs, k.me)[place]
-            swap(16 + place, m.qk.at[pl.ds(in_all_sib(yx, 0), depth)], m.sr.at[pl.ds(yx * depth, depth)])
+            source, target = pl.ds(in_all_sib(yx, 0), depth), pl.ds(yx * depth, depth)
+            swap(16 + 4 * pair + place, m.qk.at[source, low], m.sr.at[target, low])
 
     def grad_normed():
         m.dn[...] = jnp.transpose(
@@ -1286,13 +1300,12 @@
             m.gvec[1:2] += jnp.sum(grad_out, axis=0, keepdims=True)
 
         row_loop(SEQ, 32, rows_of)
-        stored("dinp").start()
-
-    def core_sum(place):
-        yx = (k.ds, k.ys, k.xs, k.me)[place]
-        k.arrive(m.sr.at[pl.ds(yx * depth, depth)], m.e_r.at[16 + place])
+
+    def core_sum(pair, place):
+        yx, low = (k.ds, k.ys, k.xs, k.me)[place], pl.ds(48 * pair, 48)
+        k.arrive(m.sr.at[pl.ds(yx * depth, depth), low], m.e_r.at[16 + 4 * pair + place])
         for zs in range(depth):
-            add_into(m.qk.at[in_all(yx, zs)], m.sr.at[yx * depth + zs])
+            add_into(m.qk.at[in_all(yx, zs), low], m.sr.at[yx * depth + zs, low])
 
     def flip():
         turn = (s_at + t_at == SEQ - 1).astype(bf16)
@@ -1332,10 +1345,10 @@
                 mine = (row_at == 15) & (core == wide % 2) & (k.x == wide // 2 % 2)
                 m.gs[wide * depth + zs] = jnp.where(mine, own, tile)
         for yx in range(4):
-            swap(20, m.gs.at[pl.ds(in_all_sib(yx, 0), depth)], m.srs.at[pl.ds(yx * depth, depth)])
+            swap(24, m.gs.at[pl.ds(in_all_sib(yx, 0), depth)], m.srs.at[pl.ds(yx * depth, depth)])
 
     def small_sums():
-        k.arrive(m.srs, m.e_r.at[20])
+        k.arrive(m.srs, m.e_r.at[24])
         for yx in range(4):
             for zs in range(depth):
                 add_into(m.gs.at[in_all(yx, zs)], m.srs.at[yx * depth + zs])
@@ -1349,31 +1362,26 @@
         k.arrive(m.outs, m.e_r.at[9])
         k.arrive(m.outx.at[1], m.e_r.at[15])
         row_loop(SEQ, 32, rows_of)
-        stored("out").start()
-
-    def store():
-        for name in RESULTS[2:]:
-            stored(name).start()
-        for group in "SFLflms":
+
+    def all_sent():
+        for group in "SFLflqvs":
             next(steps[group + "."])
-        own, half = m.ct.at[rows_at("o")], m.ct.at[half_at("o", 0)]
-        half_f32, own_f32, blocks = m.outb.at[half_rows(0)], m.outb, m.sr.at[pl.ds(0, depth)]
-        extents = [own] * 4 + [half] * 4 + [own_f32] * 2 + [half_f32] * 2 + [own_f32] + [half] * 2 + [own] + [blocks] * 4
-        extents.append(m.srs)
+        extents = (m.qk.at[:, pl.ds(0, 80)], m.qk, m.srs)
         for place, extent in enumerate(extents):
             k.left(extent, m.e_s.at[place])
-        for name in RESULTS:
-            stored(name).wait()
 
     compute = {
         "own_blocks": own_blocks, "barrier": k.barrier, "own_cotangent": own_cotangent, "norm1": norm1, "pass_ct": pass_ct,
-        "vectors": vectors, "mixer_kernels": mixer_kernels, "gain1": gain1, "unpack": unpack, "project": project,
+        "vectors": vectors, "mixer_kernels": mixer_kernels, "gain1": gain1, "project_qk": project_qk, "project_v": project_v,
         "hidden": hidden, "norm2": norm2, "sibling_rows": sibling_rows, "to_sibling": to_sibling,
         "out_to_diagonal": out_to_diagonal, "out_to_x": out_to_x, "grad_mixed": grad_mixed, "grad_normed": grad_normed,
         "back1": back1, "flip": flip, "vector_tiles": vector_tiles, "small_sums": small_sums, "finish_out": finish_out,
-        "store": store,
+        "store": all_sent,
     }
     for which in range(2):
+        compute["unpack%d" % which] = partial(unpack, which)
+        compute["mix%d" % which] = partial(six_heads, 6 * which, mix_head)
+        compute["back_v%d" % which] = partial(six_heads, 6 * which, back_v_head)
         for who in "os":
             compute["feed%d%s" % (which, who)] = partial(feed, which, who)
         for who in "xd":
@@ -1385,12 +1393,14 @@
         compute["to_diagonal%d" % which] = partial(to_diagonal, which)
         compute["to_x%d" % which] = partial(to_x, which)
         compute["back2_%d" % which] = partial(back2, which)
-        compute["pack%d" % which] = partial(pack, which)
+        compute["pack_qk%d" % which] = partial(pack, 0, which)
+        compute["pack_vo%d" % which] = partial(pack, 1, which)
     for which in range(4):
-        compute["mix%d" % which] = partial(three_heads, 3 * which, mix_head)
+        compute["score%d" % which] = partial(three_heads, 3 * which, score_head)
         compute["back%d" % (4 + which)] = partial(three_heads, 3 * which, back_head)
         compute["kernel%d" % which] = partial(three_heads, 3 * which, kernel_head)
-        compute["core_sum%d" % which] = partial(core_sum, which)
+        compute["sum_qk%d" % which] = partial(core_sum, 0, which)
+        compute["sum_vo%d" % which] = partial(core_sum, 1, which)
     for step in PLAN:
         if step in compute:
             compute[step]()
@@ -1414,20 +1424,19 @@
     for entry in scratch_of(depth).values():
         scratch.append(pltpu.SemaphoreType.DMA((entry,)) if isinstance(entry, int) else pltpu.VMEM(*entry))
     in_vmem = pl.BlockSpec(memory_space=pltpu.VMEM)
-    anywhere = pl.BlockSpec(memory_space=pl.ANY)
     in_smem = pl.BlockSpec(memory_space=pltpu.SMEM)
     shape = jax.ShapeDtypeStruct
     got = pl.pallas_call(
         partial(layer_kernel, depth),
-        out_shape=[shape((SEQ, WIDTH), bf16)] * 2
-        + [shape((24, WIDTH), f32)] * 4
-        + [shape((UNITS, WIDTH), f32)] * 2
-        + [shape((16, 128), f32)],
+        out_shape=[pltpu.VMEM((SEQ, WIDTH), bf16)] * 2
+        + [pltpu.VMEM((24, WIDTH), f32)] * 4
+        + [pltpu.VMEM((UNITS, WIDTH), f32)] * 2
+        + [pltpu.VMEM((16, 128), f32)],
         in_specs=[in_vmem, in_smem] + [in_vmem] * 9,
-        out_specs=[anywhere] * 9,
+        out_specs=[in_vmem] * 9,
         scratch_shapes=scratch,
         compiler_params=pltpu.CompilerParams(
-            collective_id=0, has_side_effects=True, vmem_limit_bytes=63 * 2**20
+            collective_id=0, has_side_effects=True, vmem_limit_bytes=61 * 2**20
         ),
         name="h3_layer",
     )(
@@ -1439,7 +1448,7 @@
         in_specs=[in_vmem] * 9,
         out_specs=[in_vmem] * 10,
         name="results",
-    )(*got)
+    )(*[pltpu.with_memory_space_constraint(x, pltpu.VMEM) for x in got])
     out, grad_in, g_query, g_key, g_value, g_out, g_fc1, g_fc2, g_bias, g_vectors = results
     return out, grad_in, g_query, g_key, g_value, g_out, g_fc1.T, g_fc2, g_bias.reshape(-1), g_vectors
 

time: 116 us -> 104 us (0.90)
  Pallas kernels: 113 us -> 101 us
    pallas_call x1, Pallas kernels: 111 us -> 99.9 us  [on_device_fast(): pl.pallas_call(partial(layer_kernel, depth), out_shape=[pltpu.VMEM((SEQ,...]
    pallas_call x1, Pallas kernels: 2.62 us -> 1.29 us  [on_device_fast(): pl.pallas_call(results_kernel, out_shape=[shape(x.shape, x.dtype) for x i...]
where the time goes in v5:
time: 104 us; the launch traced here: 102 us
  Pallas kernels  101 us (97%)
  between operations  1.3 us (1%)
    pallas_call x1, Pallas kernels, on_device_fast(): pl.pallas_call(partial(layer_kernel, depth), out_shape=[pltpu.VMEM((SEQ,...  99.9 us

profile of v5, /device:TPU:0, one launch (start us, length us, event | category | flops | bytes accessed | tf_op | source)
XLA Modules:
  0.0 102.4 jit_solution(12916473208061753817)
XLA Ops:
  1.3 99.9 %h3_layer.1 = (bf16[256,768]{1,0:T(8,128)(2,1)S(1)}, bf16[256,768]{1,0:T(8,128)(2,1)S(1)}, f32[24,768]{1,0:T(8,128)S(1)}, f32[24,768]{1,0:T(8,128)S(1)}, f32[24,...) custom-call(bf16[256,768]{1,0:T(8,128)(2,1)} %refs_0_.1, ...), custom_call_target="tpu_custom_call" | custom-call | tf_op jit(solution)/shard_map/h3_layer/pallas_call | solution.py:1429
  101.2 1.3 %results.1 = (bf16[256,768]{1,0:T(8,128)(2,1)}, bf16[256,768]{1,0:T(8,128)(2,1)}, f32[24,768]{1,0:T(8,128)}, f32[24,768]{1,0:T(8,128)}, f32[24,768]{1,0:T(8,128)...) custom-call(bf16[256,768]{1,0:T(8,128)(2,1)S(1)} %get-tuple-element.29., ...), custom_call_target="tpu_custom_call" | custom-call | tf_op jit(solution)/shard_map/results/pallas_call | solution.py:1445

commit v6 on v5

--- a/solution.py
+++ b/solution.py
@@ -825,10 +825,11 @@
 
 def row_loop(total, step, body, first=0):
     def once(i, carry):
-        body(pl.multiple_of(first + i * step, step), step)
+        for part in range(4):
+            body(pl.multiple_of(first + (i * 4 + part) * step, step), step)
         return carry
 
-    lax.fori_loop(0, total // step, once, 0)
+    lax.fori_loop(0, total // (step * 4), once, 0)
 
 
 def lane_shift(values, offset, left):
@@ -839,13 +840,8 @@
     return jnp.where(lane >= offset, pltpu.roll(values, offset, 1), 0.0)
 
 
-def six_heads(first, body):
-    for h in range(first, first + 6):
-        body(h)
-
-
-def three_heads(first, body):
-    for h in range(first, first + 3):
+def heads(which, body):
+    for h in which:
         body(h)
 
 
@@ -918,6 +914,12 @@
     table["rby"] = table["rbu"] = table["rbd"] = ((depth, FIRST, WIDTH), bf16)
     table["rcy"] = ((1, 2 * UNITS - FIRST, WIDTH), bf16)
     table["rcu"] = table["rcd"] = ((half, 2 * UNITS - FIRST, WIDTH), bf16)
+    table["tok"] = table["cot"] = ((SEQ, WIDTH), bf16)
+    for name in ("iq", "ik", "iv", "io"):
+        table[name] = ((24, WIDTH), bf16)
+    table["ifc1"] = table["ifc2"] = ((UNITS, WIDTH), bf16)
+    table["ibias"], table["ivec"] = ((1, UNITS), bf16), ((15, 24), bf16)
+    table["load"] = len(OPERANDS)
     for name, sent, came in (
         ("gq", 2, 4 * depth + 1), ("gv", 2, 4 * depth + 1), ("gb", 2, 2 * depth), ("gt", 2, 4 * depth + 1), ("gc", 3, 2 * depth + 1),
         ("sq", 1, 5 * depth), ("sv", 1, 5 * depth), ("sb", 1, 3 * depth), ("st", 1, 5 * depth), ("sc", 1, 4 * depth + 1), ("e", 3, 25),
@@ -927,28 +929,29 @@
 
 
 PLAN = (
-    "own_blocks", "barrier", "S0", "Q0", "V0", "Sz", "Qy", "L0", "Sz", "Qx", "Sx", "Sy", "Qz", "Sy", "Vz",
-    "Qz", "Sx", "Vy", "Sz", "Qx", "Qz", "Sx", "Ly", "Vz", "Qy", "Sy", "L4", "Qx", "Sx", "Vx", "Qy", "Qx",
-    "Sy", "Sd", "Qd", "Qy", "Vz", "Vy", "Vx", "Vx", "F0", "Sd", "Qd", "Sd", "norm1", "Sd", "Ss", "vectors",
-    "Qd", "gain1", "Vy", "Qd", "L4", "Vy", "Vd", "own_cotangent", "Qs", "Vx", "unpack0", "project_qk", "Fz",
-    "mixer_kernels", "Vd", "score0", "Vd", "score1", "score2", "Vd", "Fy", "score3", "Fz", "Vs", "unpack1",
-    "project_v", "L5", "mix0", "mix1", "hidden", "norm2", "L4", "Fz", "feed0o", "sibling_rows", "feed0s",
-    "pass_ct", "L5", "flip", "Fy", "pass_n2_0", "Q.", "feed0x0", "diagonal_rows0", "Fy", "feed0d0", "L5",
-    "Fy", "feed1d0", "to_diagonal0", "feed1o", "V.", "feed1x0", "pass_n2_1", "feed1s", "to_x0", "feed0x1",
-    "diagonal_rows1", "feed0d1", "feed1d1", "to_diagonal1", "feed1x1", "feed_grads1", "fY", "l1",
-    "out_to_diagonal", "to_x1", "to_sibling", "feed_grads0", "out_to_x", "fY", "back2_0", "fc", "fY", "l0",
-    "back2_1", "grad_mixed", "back_v0", "back_v1", "pack_vo0", "back4", "sum_vo0", "pack_vo1", "sum_vo1",
-    "vD", "fY", "back5", "sum_vo2", "back6", "l1", "back7", "va", "fc", "vX", "vD", "pack_qk0", "vD",
-    "grad_normed", "sum_qk0", "qD", "fv", "back1", "l1", "qD", "l0", "sum_qk1", "fc", "vX", "pack_qk1", "vX",
-    "qY", "vY", "kernel3", "sum_qk2", "sum_vo3", "qb", "vY", "qX", "qD", "qa", "vb", "qb", "qa", "va", "fc",
-    "vb", "kernel0", "sum_qk3", "fv", "vX", "qY", "va", "kernel1", "vD", "fw", "l0", "vb", "qX", "vY", "fv",
-    "kernel2", "qc", "vector_tiles", "vc", "fv", "vc", "qa", "small_sums", "sD", "fw", "sX", "sD", "qb",
-    "qX", "sY", "qv", "sD", "sY", "qc", "sX", "qD", "sb", "sa", "vc", "vv", "sa", "sb", "qY", "vb", "vY",
-    "vv", "va", "sc", "qb", "qa", "sc", "qY", "qv", "qc", "sv", "sD", "qX", "sY", "qw", "vv", "vw", "vw",
-    "sv", "qv", "sX", "vc", "sY", "sw", "fe", "sb", "sb", "lY", "sa", "qw", "sX", "qc", "finish_out", "lO",
-    "sa", "vv", "sw", "qv", "sc", "sv", "sc", "ve", "le", "sv", "qe", "se", "store",
+    "load", "barrier", "own_blocks", "S0", "Q0", "V0", "Sy", "Sz", "Sx", "L0", "Sy", "Vx", "Sz", "Vz", "Qz",
+    "Vz", "Sd", "Sx", "Sz", "Sx", "Qz", "Vz", "Sy", "Ly", "L4", "Qz", "Sx", "Vx", "Vx", "Vx", "Vy", "Qx",
+    "norm1", "Qy", "Qx", "Sy", "Sd", "Qx", "Vy", "Qx", "Vy", "Vy", "Sd", "F0", "Vd", "Qy", "Qy", "Sd", "Ss",
+    "Vd", "Vd", "L4", "Vd", "Qy", "own_cotangent", "vectors", "gain1", "Vs", "unpack1", "project_v", "Fz",
+    "Qd", "Qd", "Qd", "Qd", "mixer_kernels", "Qs", "unpack0", "project_qk", "L4", "score0", "mix0", "Fz",
+    "score1", "L5", "mix1", "hidden", "norm2", "Fz", "pass_ct", "sibling_rows", "Fy", "feed0s", "feed0o",
+    "Q.", "L5", "pass_n2_0", "feed0x0", "Fy", "diagonal_rows0", "feed0d0", "L5", "Fy", "Fy", "feed1d0",
+    "feed1x0", "to_diagonal0", "feed1s", "pass_n2_1", "feed1o", "to_x0", "feed0x1", "diagonal_rows1",
+    "feed0d1", "feed1d1", "to_diagonal1", "feed1x1", "V.", "feed_grads1", "fY", "out_to_diagonal", "l1",
+    "to_x1", "feed_grads0", "fY", "to_sibling", "back2_0", "out_to_x", "fY", "flip", "fc", "l0", "back2_1",
+    "grad_mixed", "back_v0", "back_v1", "pack_vo0", "fY", "pack_vo1", "back_qk0", "back_qk1", "sum_vo2",
+    "sum_vo0", "vD", "l1", "pack_qk0", "pack_qk1", "vX", "grad_normed", "fc", "sum_qk0", "sum_vo1", "qD",
+    "sum_qk2", "sum_qk1", "vY", "qX", "vD", "vX", "sum_vo3", "fc", "vb", "qY", "qY", "back1", "vY", "qX",
+    "fv", "kernel1", "qD", "qb", "va", "l0", "vX", "kernel2", "vD", "qa", "vD", "l1", "va", "kernel3", "qD",
+    "fc", "fw", "vb", "fv", "vX", "kernel0", "vector_tiles", "vb", "small_sums", "sD", "vc", "vY", "sD",
+    "sY", "va", "qa", "fv", "qb", "vc", "va", "sY", "sum_qk3", "sD", "sD", "sb", "sX", "vY", "sX", "sa",
+    "qc", "vb", "sY", "fv", "qD", "sb", "fw", "sX", "qX", "vc", "qX", "vv", "sa", "sa", "sX", "l0", "qb",
+    "qc", "sc", "sb", "qY", "sY", "qa", "sa", "vv", "qv", "vc", "qb", "vw", "sc", "vv", "sb", "qv", "sv",
+    "qa", "qY", "qw", "sc", "qc", "sv", "lY", "vv", "vw", "sw", "sv", "qw", "qv", "sw", "ve", "lO",
+    "finish_out", "fe", "sc", "sv", "qc", "se", "qv", "le", "qe", "store",
 )
-INPUTS = ("tok", "length", "cot", "iq", "ik", "iv", "io", "ifc1", "ifc2", "ibias", "ivec")
+OPERANDS = ("tok", "cot", "iq", "ik", "iv", "io", "ifc1", "ifc2", "ibias", "ivec")
+INPUTS = ("length",) + tuple("from_" + name for name in OPERANDS)
 RESULTS = ("out", "dinp", "gwq", "gwk", "gwv", "gwo", "gfc1", "gfc2", "gsmall")
 OUTPUTS = RESULTS
 
@@ -984,7 +987,17 @@
     t_at = lax.broadcasted_iota(jnp.int32, (SEQ, SEQ), 1)
     valid = (lax.broadcasted_iota(jnp.int32, (1, SEQ), 1) < m.length[0]).astype(f32)
 
+    def loaded(name):
+        place = OPERANDS.index(name)
+        return pltpu.make_async_copy(getattr(m, "from_" + name), getattr(m, name), m.load.at[place])
+
+    def load():
+        for name in OPERANDS[2:] + OPERANDS[:2]:
+            loaded(name).start()
+
     def own_blocks():
+        for name in OPERANDS[2:]:
+            loaded(name).wait()
         here = in_all(k.me, k.z)
         for place, (first, second) in enumerate(((m.iq, m.ik), (m.iv, m.io))):
             pair = jnp.concatenate([first[...].astype(f32), second[...].astype(f32)], axis=0)
@@ -999,6 +1012,7 @@
         return rows_at(who, half * (SEQ // 2), SEQ // 2)
 
     def own_cotangent():
+        loaded("cot").wait()
         m.ct[rows_at("o")] = m.cot[...]
         ref = m.ct.at[rows_at("o")]
         swap(0, ref, ref)
@@ -1010,6 +1024,8 @@
         swap(2, ref, ref)
 
     def norm1():
+        loaded("tok").wait()
+
         def rows_of(start, step):
             rows = pl.ds(start, step)
             tokens = m.tok[rows].astype(f32)
@@ -1039,17 +1055,21 @@
                 line = line + (pltpu.roll(tile, UNITS * zs, 1) if zs else tile)
             m.bias[y] = line[8:16]
 
-    def head_kernel(h, carry):
+    def head_kernel(h):
         rows = head_rows(h)
         decays = jnp.exp(-m.vecc[rows, 10:11] * day)
         m.ex[rows] = decays
         line = jnp.sum(m.vecc[rows, 9:10] * decays, axis=0, keepdims=True) * (1.0 / STATE)
         matrix = pltpu.roll(jnp.broadcast_to(line, (SEQ, SEQ)), 0, 1, stride=1, stride_axis=0)
         m.tt[h] = jnp.where(t_at >= s_at, matrix, 0.0)
-        return carry
 
     def mixer_kernels():
-        lax.fori_loop(0, HEADS, head_kernel, 0)
+        def four_heads(i, carry):
+            for part in range(4):
+                head_kernel(4 * i + part)
+            return carry
+
+        lax.fori_loop(0, HEADS // 4, four_heads, 0)
 
     def gain1():
         def rows_of(start, step):
@@ -1069,7 +1089,7 @@
             second[rows] = pair[:, 24:].reshape(96, WIDTH).astype(bf16)
             return carry
 
-        lax.fori_loop(0, 8, rows_of, 0)
+        lax.fori_loop(0, 8, rows_of, 0, unroll=4)
 
     def project_qk():
         m.qt[...] = jnp.transpose(dg(m.nm[...], m.wq[...], 1, 0) + m.vec[2:3]).astype(bf16)
@@ -1371,7 +1391,7 @@
             k.left(extent, m.e_s.at[place])
 
     compute = {
-        "own_blocks": own_blocks, "barrier": k.barrier, "own_cotangent": own_cotangent, "norm1": norm1, "pass_ct": pass_ct,
+        "load": load, "own_blocks": own_blocks, "barrier": k.barrier, "own_cotangent": own_cotangent, "norm1": norm1, "pass_ct": pass_ct,
         "vectors": vectors, "mixer_kernels": mixer_kernels, "gain1": gain1, "project_qk": project_qk, "project_v": project_v,
         "hidden": hidden, "norm2": norm2, "sibling_rows": sibling_rows, "to_sibling": to_sibling,
         "out_to_diagonal": out_to_diagonal, "out_to_x": out_to_x, "grad_mixed": grad_mixed, "grad_normed": grad_normed,
@@ -1380,8 +1400,10 @@
     }
     for which in range(2):
         compute["unpack%d" % which] = partial(unpack, which)
-        compute["mix%d" % which] = partial(six_heads, 6 * which, mix_head)
-        compute["back_v%d" % which] = partial(six_heads, 6 * which, back_v_head)
+        compute["score%d" % which] = partial(heads, range(6 * which, 6 * which + 6), score_head)
+        compute["mix%d" % which] = partial(heads, range(6 * which, 6 * which + 6), mix_head)
+        compute["back_qk%d" % which] = partial(heads, range(6 * which, 6 * which + 6), back_head)
+        compute["back_v%d" % which] = partial(heads, range(6 * which, 6 * which + 6), back_v_head)
         for who in "os":
             compute["feed%d%s" % (which, who)] = partial(feed, which, who)
         for who in "xd":
@@ -1396,9 +1418,7 @@
         compute["pack_qk%d" % which] = partial(pack, 0, which)
         compute["pack_vo%d" % which] = partial(pack, 1, which)
     for which in range(4):
-        compute["score%d" % which] = partial(three_heads, 3 * which, score_head)
-        compute["back%d" % (4 + which)] = partial(three_heads, 3 * which, back_head)
-        compute["kernel%d" % which] = partial(three_heads, 3 * which, kernel_head)
+        compute["kernel%d" % which] = partial(heads, range(3 * which, 3 * which + 3), kernel_head)
         compute["sum_qk%d" % which] = partial(core_sum, 0, which)
         compute["sum_vo%d" % which] = partial(core_sum, 1, which)
     for step in PLAN:
@@ -1432,7 +1452,7 @@
         + [pltpu.VMEM((24, WIDTH), f32)] * 4
         + [pltpu.VMEM((UNITS, WIDTH), f32)] * 2
         + [pltpu.VMEM((16, 128), f32)],
-        in_specs=[in_vmem, in_smem] + [in_vmem] * 9,
+        in_specs=[in_smem] + [pl.BlockSpec(memory_space=pl.ANY)] * 10,
         out_specs=[in_vmem] * 9,
         scratch_shapes=scratch,
         compiler_params=pltpu.CompilerParams(
@@ -1440,7 +1460,7 @@
         ),
         name="h3_layer",
     )(
-        tokens, lengths, cotangent, w_query, w_key, w_value, w_out, w_fc1.T, w_fc2, fc1_bias[None], vectors
+        lengths, tokens, cotangent, w_query, w_key, w_value, w_out, w_fc1.T, w_fc2, fc1_bias[None], vectors
     )
     results = pl.pallas_call(
         results_kernel,

time: 104 us -> 101 us (0.971)
  Pallas kernels: 101 us -> 97.8 us
    pallas_call x1, Pallas kernels: 99.9 us -> 96.5 us  [on_device_fast(): pl.pallas_call(partial(layer_kernel, depth), out_shape=[pltpu.VMEM((SEQ,...]
where the time goes in v6:
time: 101 us; the launch traced here: 99.1 us
  Pallas kernels  97.8 us (97%)
  between operations  1.3 us (1%)
    pallas_call x1, Pallas kernels, on_device_fast(): pl.pallas_call(partial(layer_kernel, depth), out_shape=[pltpu.VMEM((SEQ,...  96.5 us

profile of v6, /device:TPU:0, one launch (start us, length us, event | category | flops | bytes accessed | tf_op | source)
XLA Modules:
  0.0 99.1 jit_solution(16508012286109882476)
XLA Ops:
  1.3 96.5 %h3_layer.1 = (bf16[256,768]{1,0:T(8,128)(2,1)S(1)}, bf16[256,768]{1,0:T(8,128)(2,1)S(1)}, f32[24,768]{1,0:T(8,128)S(1)}, f32[24,768]{1,0:T(8,128)S(1)}, f32[24,...) custom-call(s32[1]{0:T(128)S(6)} %copy.21.refs_0_, ...), custom_call_target="tpu_custom_call" | custom-call | tf_op jit(solution)/shard_map/h3_layer/pallas_call | solution.py:1449
  97.8 1.3 %results.1 = (bf16[256,768]{1,0:T(8,128)(2,1)}, bf16[256,768]{1,0:T(8,128)(2,1)}, f32[24,768]{1,0:T(8,128)}, f32[24,768]{1,0:T(8,128)}, f32[24,768]{1,0:T(8,128)...) custom-call(bf16[256,768]{1,0:T(8,128)(2,1)S(1)} %get-tuple-element.29., ...), custom_call_target="tpu_custom_call" | custom-call | tf_op jit(solution)/shard_map/results/pallas_call | solution.py:1465

commit v7 on v6

--- a/solution.py
+++ b/solution.py
@@ -599,7 +599,7 @@
 def scatter_z_last(k, name, buf, index, low, rows, slots, ss, rs, finish):
     depth = k.depth
     from_x_diag, from_y_diag, from_xy, from_up, from_down = slots
-    order = scatter_order(depth)
+    distances = range(depth - 1, -1, -1)
 
     def block(yx, zd):
         return buf.at[index(yx, zd), pl.ds(low, rows)]
@@ -617,58 +617,78 @@
         return halved(from_xy.at[zd, 1], piece)
 
     def pure_x():
-        for zd in order:
-            send(None, lambda zd=zd: half(k.xs, zd, 1), lambda zd=zd: x_part(zd, 1), k.x_dev, 2 * depth + zd)
+        for d in distances:
+            for condition, zd, _ in near(k, d):
+                send(condition, lambda zd=zd: half(k.xs, zd, 1), lambda zd=zd: x_part(zd, 1), k.x_dev, 2 * depth + zd)
             yield
 
     def pure_y():
-        for zd in order:
-            send(None, lambda zd=zd: half(k.ys, zd, 0), lambda zd=zd: y_part(zd, 0), k.y_dev, 2 * depth + zd)
+        for d in distances:
+            for condition, zd, _ in near(k, d):
+                send(condition, lambda zd=zd: half(k.ys, zd, 0), lambda zd=zd: y_part(zd, 0), k.y_dev, 2 * depth + zd)
             yield
 
     def diagonal():
-        for zd in order:
-            send(None, lambda zd=zd: half(k.ds, zd, 0), lambda zd=zd: from_y_diag.at[zd], k.y_dev, zd)
-            send(None, lambda zd=zd: half(k.ds, zd, 1), lambda zd=zd: from_x_diag.at[zd], k.x_dev, depth + zd)
+        for d in distances:
+            for condition, zd, _ in near(k, d):
+                send(condition, lambda zd=zd: half(k.ds, zd, 0), lambda zd=zd: from_y_diag.at[zd], k.y_dev, zd)
+                send(condition, lambda zd=zd: half(k.ds, zd, 1), lambda zd=zd: from_x_diag.at[zd], k.x_dev, depth + zd)
             yield
 
     def y_added():
-        for zd in order:
-            k.arrive(from_y_diag.at[zd], rs.at[zd])
-            add_into(half(k.xs, zd, 0), from_y_diag.at[zd])
-            send(None, lambda zd=zd: half(k.xs, zd, 0), lambda zd=zd: x_part(zd, 0), k.x_dev, 2 * depth + zd)
+        for d in distances:
+            for condition, zd, _ in near(k, d):
+
+                def take(zd=zd):
+                    k.arrive(from_y_diag.at[zd], rs.at[zd])
+                    add_into(half(k.xs, zd, 0), from_y_diag.at[zd])
+
+                when(condition, take)
+                send(condition, lambda zd=zd: half(k.xs, zd, 0), lambda zd=zd: x_part(zd, 0), k.x_dev, 2 * depth + zd)
             yield
 
     def x_added():
-        for zd in order:
-            k.arrive(from_x_diag.at[zd], rs.at[depth + zd])
-            add_into(half(k.ys, zd, 1), from_x_diag.at[zd])
-            send(None, lambda zd=zd: half(k.ys, zd, 1), lambda zd=zd: y_part(zd, 1), k.y_dev, 2 * depth + zd)
-            yield
-
-    def wave(zd, number):
-        def send_z(condition, up):
-            place = (4 if up else 3) * depth + zd
-            slot = from_down if up else from_up
-            send(condition, lambda: block(k.me, zd), lambda: slot.at[zd], k.up_dev if up else k.down_dev, place)
-
-        along_z(
-            k, zd, number, block(k.me, zd), from_up.at[zd], from_down.at[zd],
-            rs.at[3 * depth + zd], rs.at[4 * depth + zd], send_z,
-        )
+        for d in distances:
+            for condition, zd, _ in near(k, d):
+
+                def take(zd=zd):
+                    k.arrive(from_x_diag.at[zd], rs.at[depth + zd])
+                    add_into(half(k.ys, zd, 1), from_x_diag.at[zd])
+
+                when(condition, take)
+                send(condition, lambda zd=zd: half(k.ys, zd, 1), lambda zd=zd: y_part(zd, 1), k.y_dev, 2 * depth + zd)
+            yield
+
+    def send_z(condition, zd, down):
+        place, slot = (3 * depth + zd, from_up) if down else (4 * depth + zd, from_down)
+        send(condition, lambda: block(k.me, zd), lambda: slot.at[zd], k.down_dev if down else k.up_dev, place)
 
     def collect():
-        for zd in order:
-            k.arrive(from_xy.at[zd], rs.at[2 * depth + zd])
-            add_into(block(k.me, zd), from_xy.at[zd, 0], from_xy.at[zd, 1])
-            wave(zd, 0)
-            yield
-
-    def waves(number):
-        for zd in order:
-            if zd < depth - 1 - number or zd > number:
-                wave(zd, number)
-                yield
+        for d in distances:
+            for condition, zd, below in near(k, d):
+
+                def take(zd=zd):
+                    k.arrive(from_xy.at[zd], rs.at[2 * depth + zd])
+                    add_into(block(k.me, zd), from_xy.at[zd, 0], from_xy.at[zd, 1])
+
+                when(condition, take)
+                if d:
+                    send_z(both(condition, jnp.logical_not(k.has_up if below else k.has_down)), zd, below)
+            yield
+
+    def between():
+        for d in range(depth - 2, 0, -1):
+            for condition, zd, below in near(k, d):
+                condition = both(condition, k.has_up if below else k.has_down)
+                slot, semaphore = (from_up, rs.at[3 * depth + zd]) if below else (from_down, rs.at[4 * depth + zd])
+
+                def take(zd=zd, slot=slot, semaphore=semaphore):
+                    k.arrive(slot.at[zd], semaphore)
+                    add_into(block(k.me, zd), slot.at[zd])
+
+                pl.when(condition)(take)
+                send_z(condition, zd, below)
+            yield
 
     def end():
         finish(block(k.me, k.z), False)
@@ -690,14 +710,14 @@
         yield
 
     steps = {"X": pure_x(), "Y": pure_y(), "D": diagonal(), "a": y_added(), "b": x_added(), "c": collect(), "e": end()}
-    steps |= {"v": waves(1), "w": waves(2), ".": left()}
+    steps |= {"v": between(), ".": left()}
     return {name + key: step for key, step in steps.items()}
 
 
 def scatter_pair_z_last(k, name, buf, index, low, rows, slots, ss, rs, finish):
     depth = k.depth
     from_y, from_up, from_down = slots
-    order = scatter_order(depth)
+    distances = range(depth - 1, -1, -1)
 
     def block(yx, zd):
         return buf.at[index(yx, zd), pl.ds(low, rows)]
@@ -706,33 +726,41 @@
         k.start(condition, source, target, ss.at[0], rs.at[r], device)
 
     def pure_y():
-        for zd in order:
-            send(None, lambda zd=zd: block(k.ys, zd), lambda zd=zd: from_y.at[zd], k.y_dev, zd)
-            yield
-
-    def wave(zd, number):
-        def send_z(condition, up):
-            slot = from_down if up else from_up
-            place = (2 if up else 1) * depth + zd
-            send(condition, lambda: block(k.me, zd), lambda: slot.at[zd], k.up_dev if up else k.down_dev, place)
-
-        along_z(
-            k, zd, number, block(k.me, zd), from_up.at[zd], from_down.at[zd],
-            rs.at[depth + zd], rs.at[2 * depth + zd], send_z,
-        )
+        for d in distances:
+            for condition, zd, _ in near(k, d):
+                send(condition, lambda zd=zd: block(k.ys, zd), lambda zd=zd: from_y.at[zd], k.y_dev, zd)
+            yield
+
+    def send_z(condition, zd, down):
+        place, slot = (depth + zd, from_up) if down else (2 * depth + zd, from_down)
+        send(condition, lambda: block(k.me, zd), lambda: slot.at[zd], k.down_dev if down else k.up_dev, place)
 
     def collect():
-        for zd in order:
-            k.arrive(from_y.at[zd], rs.at[zd])
-            add_into(block(k.me, zd), from_y.at[zd])
-            wave(zd, 0)
-            yield
-
-    def waves(number):
-        for zd in order:
-            if zd < depth - 1 - number or zd > number:
-                wave(zd, number)
-                yield
+        for d in distances:
+            for condition, zd, below in near(k, d):
+
+                def take(zd=zd):
+                    k.arrive(from_y.at[zd], rs.at[zd])
+                    add_into(block(k.me, zd), from_y.at[zd])
+
+                when(condition, take)
+                if d:
+                    send_z(both(condition, jnp.logical_not(k.has_up if below else k.has_down)), zd, below)
+            yield
+
+    def between():
+        for d in range(depth - 2, 0, -1):
+            for condition, zd, below in near(k, d):
+                condition = both(condition, k.has_up if below else k.has_down)
+                slot, semaphore = (from_up, rs.at[depth + zd]) if below else (from_down, rs.at[2 * depth + zd])
+
+                def take(zd=zd, slot=slot, semaphore=semaphore):
+                    k.arrive(slot.at[zd], semaphore)
+                    add_into(block(k.me, zd), slot.at[zd])
+
+                pl.when(condition)(take)
+                send_z(condition, zd, below)
+            yield
 
     def end():
         finish(block(k.me, k.z), False)
@@ -753,7 +781,7 @@
         k.left(buf.at[pl.ds(0, 2 * depth - 1), pl.ds(low, rows)], ss.at[0])
         yield
 
-    steps = {"Y": pure_y(), "c": collect(), "v": waves(1), "w": waves(2), "e": end(), ".": left()}
+    steps = {"Y": pure_y(), "c": collect(), "v": between(), "e": end(), ".": left()}
     return {name + key: step for key, step in steps.items()}
 
 
@@ -929,26 +957,16 @@
 
 
 PLAN = (
-    "load", "barrier", "own_blocks", "S0", "Q0", "V0", "Sy", "Sz", "Sx", "L0", "Sy", "Vx", "Sz", "Vz", "Qz",
-    "Vz", "Sd", "Sx", "Sz", "Sx", "Qz", "Vz", "Sy", "Ly", "L4", "Qz", "Sx", "Vx", "Vx", "Vx", "Vy", "Qx",
-    "norm1", "Qy", "Qx", "Sy", "Sd", "Qx", "Vy", "Qx", "Vy", "Vy", "Sd", "F0", "Vd", "Qy", "Qy", "Sd", "Ss",
-    "Vd", "Vd", "L4", "Vd", "Qy", "own_cotangent", "vectors", "gain1", "Vs", "unpack1", "project_v", "Fz",
-    "Qd", "Qd", "Qd", "Qd", "mixer_kernels", "Qs", "unpack0", "project_qk", "L4", "score0", "mix0", "Fz",
-    "score1", "L5", "mix1", "hidden", "norm2", "Fz", "pass_ct", "sibling_rows", "Fy", "feed0s", "feed0o",
-    "Q.", "L5", "pass_n2_0", "feed0x0", "Fy", "diagonal_rows0", "feed0d0", "L5", "Fy", "Fy", "feed1d0",
-    "feed1x0", "to_diagonal0", "feed1s", "pass_n2_1", "feed1o", "to_x0", "feed0x1", "diagonal_rows1",
-    "feed0d1", "feed1d1", "to_diagonal1", "feed1x1", "V.", "feed_grads1", "fY", "out_to_diagonal", "l1",
-    "to_x1", "feed_grads0", "fY", "to_sibling", "back2_0", "out_to_x", "fY", "flip", "fc", "l0", "back2_1",
-    "grad_mixed", "back_v0", "back_v1", "pack_vo0", "fY", "pack_vo1", "back_qk0", "back_qk1", "sum_vo2",
-    "sum_vo0", "vD", "l1", "pack_qk0", "pack_qk1", "vX", "grad_normed", "fc", "sum_qk0", "sum_vo1", "qD",
-    "sum_qk2", "sum_qk1", "vY", "qX", "vD", "vX", "sum_vo3", "fc", "vb", "qY", "qY", "back1", "vY", "qX",
-    "fv", "kernel1", "qD", "qb", "va", "l0", "vX", "kernel2", "vD", "qa", "vD", "l1", "va", "kernel3", "qD",
-    "fc", "fw", "vb", "fv", "vX", "kernel0", "vector_tiles", "vb", "small_sums", "sD", "vc", "vY", "sD",
-    "sY", "va", "qa", "fv", "qb", "vc", "va", "sY", "sum_qk3", "sD", "sD", "sb", "sX", "vY", "sX", "sa",
-    "qc", "vb", "sY", "fv", "qD", "sb", "fw", "sX", "qX", "vc", "qX", "vv", "sa", "sa", "sX", "l0", "qb",
-    "qc", "sc", "sb", "qY", "sY", "qa", "sa", "vv", "qv", "vc", "qb", "vw", "sc", "vv", "sb", "qv", "sv",
-    "qa", "qY", "qw", "sc", "qc", "sv", "lY", "vv", "vw", "sw", "sv", "qw", "qv", "sw", "ve", "lO",
-    "finish_out", "fe", "sc", "sv", "qc", "se", "qv", "le", "qe", "store",
+    0, 2, 1, 69, 83, 76, 70, 71, 86, 72, 94, 84, 70, 77, 85, 79, 84, 71, 86, 71, 77, 70, 96, 84, 72, 85, 77,
+    73, 95, 71, 72, 79, 85, 78, 78, 78, 87, 78, 85, 90, 96, 73, 72, 87, 73, 86, 79, 79, 73, 74, 86, 6, 3, 80,
+    7, 80, 87, 91, 80, 80, 4, 8, 87, 81, 25, 96, 9, 88, 41, 10, 26, 42, 91, 27, 43, 11, 12, 97, 13, 92, 91, 5,
+    30, 97, 34, 35, 31, 92, 92, 89, 97, 92, 47, 36, 50, 46, 37, 51, 32, 48, 52, 49, 99, 82, 15, 99, 105, 14,
+    53, 33, 99, 16, 99, 104, 20, 38, 54, 17, 29, 45, 40, 28, 44, 39, 56, 105, 59, 121, 60, 58, 100, 112, 121,
+    112, 55, 62, 61, 121, 65, 123, 121, 120, 112, 119, 114, 100, 18, 120, 104, 114, 64, 112, 122, 111, 57,
+    111, 66, 110, 110, 68, 113, 101, 119, 124, 122, 123, 113, 111, 113, 100, 119, 19, 123, 63, 21, 105, 104,
+    67, 22, 130, 130, 128, 115, 120, 124, 122, 130, 126, 128, 129, 120, 131, 101, 23, 129, 119, 132, 122, 132,
+    128, 131, 110, 129, 123, 114, 115, 131, 130, 113, 117, 107, 133, 124, 100, 133, 126, 132, 115, 111, 102,
+    106, 124, 114, 135, 129, 117, 110, 133, 128, 135, 132, 131, 125, 108, 115, 116, 133, 134, 24,
 )
 OPERANDS = ("tok", "cot", "iq", "ik", "iv", "io", "ifc1", "ifc2", "ibias", "ivec")
 INPUTS = ("length",) + tuple("from_" + name for name in OPERANDS)
@@ -971,10 +989,13 @@
     def in_pair(yx, zs):
         return lax.div(yx, 2) * depth + zs
 
-    places = {"o": k.x * 2 + core, "s": k.x * 2 + 1 - core, "x": (1 - k.x) * 2 + core, "d": (1 - k.x) * 2 + 1 - core}
-
-    def rows_at(who, start=0, step=SEQ):
-        return pl.ds(pl.multiple_of(places[who] * SEQ + start, step), step)
+    places = {"o": (k.x, core), "s": (k.x, 1 - core), "x": (1 - k.x, core), "d": (1 - k.x, 1 - core)}
+    part_rows = SEQ // 2
+
+    def rows_at(who, start, step):
+        x, c = places[who]
+        half, inside = (lax.div(start, part_rows), lax.rem(start, part_rows)) if hasattr(start, "dtype") else divmod(start, part_rows)
+        return pl.ds(pl.multiple_of(x * (2 * SEQ) + half * SEQ + c * part_rows + inside, step), step)
 
     def sent_by(place):
         return 2 if place == 24 else 1 if place in (9, 10, 11, 12) or place >= 16 else 0
@@ -1009,19 +1030,23 @@
         m.ff[in_pair(k.me, k.z), UNITS : 2 * UNITS] = m.ifc2[...]
 
     def half_at(who, half):
-        return rows_at(who, half * (SEQ // 2), SEQ // 2)
+        return rows_at(who, half * part_rows, part_rows)
+
+    def send_halves(place, buf, who, device=None):
+        for half in range(2):
+            ref = buf.at[half_at(who, half)]
+            swap(place, ref, ref, device)
 
     def own_cotangent():
         loaded("cot").wait()
-        m.ct[rows_at("o")] = m.cot[...]
-        ref = m.ct.at[rows_at("o")]
-        swap(0, ref, ref)
-        swap(1, ref, ref, k.x_dev)
+        for half in range(2):
+            m.ct[half_at("o", half)] = m.cot[half * part_rows : (half + 1) * part_rows]
+        send_halves(0, m.ct, "o")
+        send_halves(1, m.ct, "o", k.x_dev)
 
     def pass_ct():
-        ref = m.ct.at[rows_at("x")]
-        k.arrive(ref, m.e_r.at[1])
-        swap(2, ref, ref)
+        k.arrive(m.nm, m.e_r.at[1])
+        send_halves(2, m.ct, "x")
 
     def norm1():
         loaded("tok").wait()
@@ -1129,8 +1154,7 @@
             m.n2[rows_at("o", start, step)] = (scaled * m.vec[12:13] + m.vec[13:14]).astype(bf16)
 
         row_loop(SEQ, 32, rows_of)
-        ref = m.n2.at[rows_at("o")]
-        swap(3, ref, ref)
+        send_halves(3, m.n2, "o")
         for half in range(2):
             ref = m.n2.at[half_at("o", half)]
             swap(4 + half, ref, ref, k.x_dev)
@@ -1141,12 +1165,12 @@
         swap(6 + half, ref, ref)
 
     def sibling_rows():
-        k.arrive(m.ct.at[rows_at("s")], m.e_r.at[0])
-        k.arrive(m.n2.at[rows_at("s")], m.e_r.at[3])
+        k.arrive(m.nm, m.e_r.at[0])
+        k.arrive(m.nm, m.e_r.at[3])
 
     def diagonal_rows(half):
         if half == 0:
-            k.arrive(m.ct.at[rows_at("d")], m.e_r.at[2])
+            k.arrive(m.nm, m.e_r.at[2])
         k.arrive(m.n2.at[half_at("d", half)], m.e_r.at[6 + half])
 
     def finish_rows(pieces):
@@ -1187,9 +1211,10 @@
     chunk = UNITS * depth
     ys = (k.y, 1 - k.y)
 
-    def feed(which, who, half=None):
+    def feed(which, half=None):
         blocks = pl.ds(ys[which] * depth, depth)
-        rows = rows_at(who) if half is None else half_at(who, half)
+        start, extent = (k.x * (2 * SEQ), 2 * SEQ) if half is None else ((1 - k.x) * (2 * SEQ) + half * SEQ, SEQ)
+        rows = pl.ds(pl.multiple_of(start, SEQ), extent)
         fc1 = m.ff[blocks, 0:UNITS, :].reshape(chunk, WIDTH)
         fc2 = m.ff[blocks, UNITS : 2 * UNITS, :].reshape(chunk, WIDTH)
         pre = dg(m.n2[rows], fc1, 1, 1) + m.bias[ys[which], 7:8]
@@ -1209,8 +1234,10 @@
             m.dn2[rows] += dg(grad_pre, fc1, 1, 0)
 
     def to_sibling():
-        swap(8, m.dn2.at[rows_at("s")], m.dn2s)
-        swap(9, m.outp.at[rows_at("s")], m.outs)
+        for half in range(2):
+            swap(8, m.dn2.at[half_at("s", half)], m.dn2s.at[half_rows(half)])
+        for half in range(2):
+            swap(9, m.outp.at[half_at("s", half)], m.outs.at[half_rows(half)])
 
     def half_rows(half):
         return pl.ds(half * (SEQ // 2), SEQ // 2)
@@ -1225,11 +1252,14 @@
         swap(13 + half, m.dn2x.at[0, rows], m.dn2x.at[1, rows], k.x_dev)
 
     def out_to_diagonal():
-        swap(12, m.outp.at[rows_at("d")], m.outb)
+        for half in range(2):
+            swap(12, m.outp.at[half_at("d", half)], m.outb.at[half_rows(half)])
 
     def out_to_x():
         k.arrive(m.outb, m.e_r.at[12])
-        m.outx[0] = (m.outp[rows_at("x")] + m.outb[...]).astype(bf16)
+        for half in range(2):
+            rows = half_rows(half)
+            m.outx[0, rows] = (m.outp[half_at("x", half)] + m.outb[rows]).astype(bf16)
         swap(15, m.outx.at[0], m.outx.at[1], k.x_dev)
 
     def feed_grads(which):
@@ -1390,42 +1420,35 @@
         for place, extent in enumerate(extents):
             k.left(extent, m.e_s.at[place])
 
-    compute = {
-        "load": load, "own_blocks": own_blocks, "barrier": k.barrier, "own_cotangent": own_cotangent, "norm1": norm1, "pass_ct": pass_ct,
-        "vectors": vectors, "mixer_kernels": mixer_kernels, "gain1": gain1, "project_qk": project_qk, "project_v": project_v,
-        "hidden": hidden, "norm2": norm2, "sibling_rows": sibling_rows, "to_sibling": to_sibling,
-        "out_to_diagonal": out_to_diagonal, "out_to_x": out_to_x, "grad_mixed": grad_mixed, "grad_normed": grad_normed,
-        "back1": back1, "flip": flip, "vector_tiles": vector_tiles, "small_sums": small_sums, "finish_out": finish_out,
-        "store": all_sent,
-    }
+    compute = [
+        load, own_blocks, k.barrier, own_cotangent, norm1, pass_ct, vectors, mixer_kernels, gain1, project_qk,
+        project_v, hidden, norm2, sibling_rows, to_sibling, out_to_diagonal, out_to_x, grad_mixed,
+        grad_normed, back1, flip, vector_tiles, small_sums, finish_out, all_sent,
+    ]
     for which in range(2):
-        compute["unpack%d" % which] = partial(unpack, which)
-        compute["score%d" % which] = partial(heads, range(6 * which, 6 * which + 6), score_head)
-        compute["mix%d" % which] = partial(heads, range(6 * which, 6 * which + 6), mix_head)
-        compute["back_qk%d" % which] = partial(heads, range(6 * which, 6 * which + 6), back_head)
-        compute["back_v%d" % which] = partial(heads, range(6 * which, 6 * which + 6), back_v_head)
-        for who in "os":
-            compute["feed%d%s" % (which, who)] = partial(feed, which, who)
-        for who in "xd":
-            for half in range(2):
-                compute["feed%d%s%d" % (which, who, half)] = partial(feed, which, who, half)
-        compute["feed_grads%d" % which] = partial(feed_grads, which)
-        compute["pass_n2_%d" % which] = partial(pass_n2, which)
-        compute["diagonal_rows%d" % which] = partial(diagonal_rows, which)
-        compute["to_diagonal%d" % which] = partial(to_diagonal, which)
-        compute["to_x%d" % which] = partial(to_x, which)
-        compute["back2_%d" % which] = partial(back2, which)
-        compute["pack_qk%d" % which] = partial(pack, 0, which)
-        compute["pack_vo%d" % which] = partial(pack, 1, which)
+        compute.append(partial(unpack, which))
+        compute.append(partial(heads, range(6 * which, 6 * which + 6), score_head))
+        compute.append(partial(heads, range(6 * which, 6 * which + 6), mix_head))
+        compute.append(partial(heads, range(6 * which, 6 * which + 6), back_head))
+        compute.append(partial(heads, range(6 * which, 6 * which + 6), back_v_head))
+        compute.append(partial(feed, which))
+        for half in range(2):
+            compute.append(partial(feed, which, half))
+        compute.append(partial(feed_grads, which))
+        compute.append(partial(pass_n2, which))
+        compute.append(partial(diagonal_rows, which))
+        compute.append(partial(to_diagonal, which))
+        compute.append(partial(to_x, which))
+        compute.append(partial(back2, which))
+        compute.append(partial(pack, 0, which))
+        compute.append(partial(pack, 1, which))
     for which in range(4):
-        compute["kernel%d" % which] = partial(heads, range(3 * which, 3 * which + 3), kernel_head)
-        compute["sum_qk%d" % which] = partial(core_sum, 0, which)
-        compute["sum_vo%d" % which] = partial(core_sum, 1, which)
+        compute.append(partial(heads, range(3 * which, 3 * which + 3), kernel_head))
+        compute.append(partial(core_sum, 0, which))
+        compute.append(partial(core_sum, 1, which))
+    everything = [*compute, *(partial(next, step) for step in steps.values())]
     for step in PLAN:
-        if step in compute:
-            compute[step]()
-        else:
-            next(steps[step])
+        everything[step]()
 
 
 def results_kernel(*refs):

time: 101 us -> 101 us (level); the launches traced: 99.1 us -> 100 us
  Pallas kernels: 97.8 us -> 99.1 us
    pallas_call x1, Pallas kernels: 96.5 us -> 97.8 us  [on_device_fast(): pl.pallas_call(partial(layer_kernel, depth), out_shape=[pltpu.VMEM((SEQ,...]
where the time goes in v7:
time: 101 us; the launch traced here: 100 us
  Pallas kernels  99.1 us (98%)
  between operations  1.3 us (1%)
    pallas_call x1, Pallas kernels, on_device_fast(): pl.pallas_call(partial(layer_kernel, depth), out_shape=[pltpu.VMEM((SEQ,...  97.8 us

profile of v7, /device:TPU:0, one launch (start us, length us, event | category | flops | bytes accessed | tf_op | source)
XLA Modules:
  0.0 100.4 jit_solution(11987902835703847429)
XLA Ops:
  1.3 97.8 %h3_layer.1 = (bf16[256,768]{1,0:T(8,128)(2,1)S(1)}, bf16[256,768]{1,0:T(8,128)(2,1)S(1)}, f32[24,768]{1,0:T(8,128)S(1)}, f32[24,768]{1,0:T(8,128)S(1)}, f32[24,...) custom-call(s32[1]{0:T(128)S(6)} %copy.21.refs_0_, ...), custom_call_target="tpu_custom_call" | custom-call | tf_op jit(solution)/shard_map/h3_layer/pallas_call | solution.py:1472
  99.1 1.3 %results.1 = (bf16[256,768]{1,0:T(8,128)(2,1)}, bf16[256,768]{1,0:T(8,128)(2,1)}, f32[24,768]{1,0:T(8,128)}, f32[24,768]{1,0:T(8,128)}, f32[24,768]{1,0:T(8,128)...) custom-call(bf16[256,768]{1,0:T(8,128)(2,1)S(1)} %get-tuple-element.29., ...), custom_call_target="tpu_custom_call" | custom-call | tf_op jit(solution)/shard_map/results/pallas_call | solution.py:1488
